TPU v7x, 32 devices: a whole 2x2x4 slice. The times are simulated.
32 devices in a mesh: rep: 4 (over y, x), grp: 8 (over z, core).
Axes of the slice: x: 2, y: 2, z: 4, core: 2. Of those that a mesh axis runs over, the one named last changes fastest.
Arguments:
- tokens: bfloat16 [8192, 2048], P(('rep', 'grp')), may hold values from -12 to 12
- block_map: int32 [8, 16], P('rep'), may hold values from 0 to 15, each once within a row
- w_qkvg: bfloat16 [2048, 6144], P('grp'), may hold values from -0.125 to 0.125
- w_out: bfloat16 [2048, 2048], P('grp'), may hold values from -0.75 to 0.75
- w_in: bfloat16 [2048, 2, 6144], P('grp'), may hold values from -0.125 to 0.125
- w_down: bfloat16 [6144, 2048], P('grp'), may hold values from -0.078125 to 0.078125
- norm_attn: bfloat16 [2048], P('grp'), may hold values from 0.099609375 to 1.8984375
- norm_query: bfloat16 [128], P('grp'), may hold values from 0.796875 to 1.796875
- norm_key: bfloat16 [128], P('grp'), may hold values from 0.796875 to 1.796875
- norm_mlp: bfloat16 [2048], P('grp'), may hold values from 0.099609375 to 1.8984375
- cotangent: bfloat16 [8192, 2048], P(('rep', 'grp')), may hold values from -6 to 6
Outputs:
- output: bfloat16 [8192, 2048], P(('rep', 'grp'))
- grad_tokens: bfloat16 [8192, 2048], P(('rep', 'grp'))
- grad_w_qkvg: float32 [2048, 6144], P('grp')
- grad_w_out: float32 [2048, 2048], P('grp')
- grad_w_in: float32 [2048, 2, 6144], P('grp')
- grad_w_down: float32 [6144, 2048], P('grp')
- grad_norm_attn: float32 [2048], P('grp')
- grad_norm_query: float32 [128], P('grp')
- grad_norm_key: float32 [128], P('grp')
- grad_norm_mlp: float32 [2048], P('grp')
Inputs may be any that keep to these rules, and one draw needn't show every extreme that they name: `block_map`: each row is a permutation of the 16 blocks of one sequence.
All inputs are finite; a program needn't handle non-finite values.
Results may differ from a plain program's by a relative error of at most 0.02.
Values may be sent and summed in bfloat16 or wider, within the bound.
A program may use at most 512 MiB of HBM per device.

v0:
```python
import jax
import jax.numpy as jnp
from jax import lax
from jax.sharding import PartitionSpec as P

QUERY_HEADS = 16
KEY_VALUE_HEADS = 8
HEAD_SIZE = 128
BLOCK_TOKENS = 64
GROUP_SEQUENCES = 2


norm_epsilon = 1e-06
rotary_base = 1000000.0
masked_value = -1e30


def row_scale(values):
    return lax.rsqrt(jnp.mean(values * values, axis=-1, keepdims=True) + norm_epsilon)


def rotate_half(values):
    middle = values.shape[-1] // 2
    return jnp.concatenate([-values[..., middle:], values[..., :middle]], axis=-1)


def rotary_tables(positions):
    exponent = jnp.arange(HEAD_SIZE // 2, dtype=jnp.float32) * (2.0 / HEAD_SIZE)
    inverse = jnp.power(jnp.float32(rotary_base), -exponent)
    angles = positions.astype(jnp.float32)[..., None] * inverse
    angles = jnp.concatenate([angles, angles], axis=-1)
    return (jnp.cos(angles), jnp.sin(angles))


def unrotate_pairs(gradient, cosine_lookup, sine_lookup):
    return gradient * cosine_lookup - rotate_half(gradient * sine_lookup)


def norm_back(grad_out, normed, scale_rows, gain_vector):
    weighted = grad_out * gain_vector
    grad_in = scale_rows * (weighted - normed * jnp.mean(weighted * normed, axis=-1, keepdims=True))
    return (grad_in, grad_out * normed)


def positions_of(block_ids):
    offsets = jnp.arange(BLOCK_TOKENS, dtype=jnp.int32)
    return (block_ids[:, :, None] * BLOCK_TOKENS + offsets[None, None, :]).reshape(
        block_ids.shape[0], -1
    )


def attention_scores(query_head_groups, key_row_block, query_pos, key_pos):
    key_head_split = key_row_block.reshape(
        key_row_block.shape[0], key_row_block.shape[1], KEY_VALUE_HEADS, HEAD_SIZE
    )
    scores = jnp.einsum(
        "sqhgd,skhd->shgqk", query_head_groups, key_head_split, preferred_element_type=jnp.float32
    ) * HEAD_SIZE ** (-0.5)
    allowed = key_pos[:, None, None, None, :] <= query_pos[:, None, None, :, None]
    return (scores, allowed)


def body(
    tokens,
    block_map,
    w_qkvg,
    w_out,
    w_in,
    w_down,
    norm_attn,
    norm_query,
    norm_key,
    norm_mlp,
    cotangent,
):
    group_index = lax.axis_index("grp")
    query_cols = QUERY_HEADS * HEAD_SIZE
    key_column_span = KEY_VALUE_HEADS * HEAD_SIZE
    group_layout = QUERY_HEADS // KEY_VALUE_HEADS
    shard_local_rows = tokens.shape[0]
    block_ids = lax.dynamic_slice_in_dim(block_map, 2 * group_index, 2, 1)
    query_pos = positions_of(block_ids)
    key_pos = positions_of(block_map)
    cosine_lookup, sine_lookup = rotary_tables(query_pos)
    cosine_lookup = cosine_lookup[:, :, None, :]
    sine_lookup = sine_lookup[:, :, None, :]
    attn_weights = (
        lax.all_gather(w_qkvg, "grp", axis=0, tiled=True),
        lax.all_gather(w_out, "grp", axis=0, tiled=True),
        lax.all_gather(norm_attn, "grp", axis=0, tiled=True),
        lax.all_gather(norm_query, "grp", axis=0, tiled=True),
        lax.all_gather(norm_key, "grp", axis=0, tiled=True),
    )
    qkvg_full = attn_weights[0]
    out_full = attn_weights[1]
    gain_attn = attn_weights[2].astype(jnp.float32)
    gain_query = attn_weights[3].astype(jnp.float32)
    key_norm_gain = attn_weights[4].astype(jnp.float32)
    residual = tokens.astype(jnp.float32)
    scale_first = row_scale(residual)
    normed_first = residual * scale_first
    attn_input = (normed_first * gain_attn).astype(jnp.bfloat16)
    projected = jnp.dot(attn_input, qkvg_full, preferred_element_type=jnp.float32)
    query_heads = projected[:, :query_cols].reshape(shard_local_rows, QUERY_HEADS, HEAD_SIZE)
    gate_raw = projected[:, query_cols : 2 * query_cols]
    key_head_split = projected[:, 2 * query_cols : 2 * query_cols + key_column_span].reshape(
        shard_local_rows, KEY_VALUE_HEADS, HEAD_SIZE
    )
    value_rows = projected[:, 2 * query_cols + key_column_span :].astype(jnp.bfloat16)
    query_scale = row_scale(query_heads)
    query_normed = query_heads * query_scale
    key_scale = row_scale(key_head_split)
    key_after_norm = key_head_split * key_scale
    query_shaped = (query_normed * gain_query).reshape(
        GROUP_SEQUENCES, 2 * BLOCK_TOKENS, QUERY_HEADS, HEAD_SIZE
    )
    query_rotated = (query_shaped * cosine_lookup + rotate_half(query_shaped) * sine_lookup).astype(
        jnp.bfloat16
    )
    key_reshaped = (key_after_norm * key_norm_gain).reshape(
        GROUP_SEQUENCES, 2 * BLOCK_TOKENS, KEY_VALUE_HEADS, HEAD_SIZE
    )
    key_rot = (key_reshaped * cosine_lookup + rotate_half(key_reshaped) * sine_lookup).astype(
        jnp.bfloat16
    )
    key_local = key_rot.reshape(GROUP_SEQUENCES, 2 * BLOCK_TOKENS, key_column_span)
    value_local = value_rows.reshape(GROUP_SEQUENCES, 2 * BLOCK_TOKENS, key_column_span)
    key_all, value_complete = (
        lax.all_gather(key_local, "grp", axis=1, tiled=True),
        lax.all_gather(value_local, "grp", axis=1, tiled=True),
    )
    query_head_groups = query_rotated.reshape(
        GROUP_SEQUENCES, 2 * BLOCK_TOKENS, KEY_VALUE_HEADS, group_layout, HEAD_SIZE
    )
    scores, allowed = attention_scores(query_head_groups, key_all, query_pos, key_pos)
    scores = jnp.where(allowed, scores, masked_value)
    top_score = jnp.max(scores, axis=-1, keepdims=True)
    exp_scores = jnp.exp(scores - top_score)
    exp_total = jnp.sum(exp_scores, axis=-1, keepdims=True)
    probability = (exp_scores / exp_total).astype(jnp.bfloat16)
    log_total = top_score + jnp.log(exp_total)
    value_head_split = value_complete.reshape(GROUP_SEQUENCES, -1, KEY_VALUE_HEADS, HEAD_SIZE)
    attended = jnp.einsum(
        "shgqk,skhd->sqhgd", probability, value_head_split, preferred_element_type=jnp.float32
    ).reshape(shard_local_rows, query_cols)
    gate_sig = jax.nn.sigmoid(gate_raw)
    attn_out = (attended * gate_sig).astype(jnp.bfloat16)
    branch = jnp.dot(attn_out, out_full, preferred_element_type=jnp.float32)
    hidden = residual + branch
    mlp_weights = (
        lax.all_gather(w_in, "grp", axis=0, tiled=True),
        lax.all_gather(w_down, "grp", axis=0, tiled=True),
        lax.all_gather(norm_mlp, "grp", axis=0, tiled=True),
    )
    in_full = mlp_weights[0]
    down_full = mlp_weights[1]
    gain_mlp = mlp_weights[2].astype(jnp.float32)
    scale_second = row_scale(hidden)
    normed_second = hidden * scale_second
    mlp_input = (normed_second * gain_mlp).astype(jnp.bfloat16)
    gate_up = jnp.einsum("td,dcf->tcf", mlp_input, in_full, preferred_element_type=jnp.float32)
    gate_value = gate_up[:, 0]
    up_value = gate_up[:, 1]
    gate_sigmoid = jax.nn.sigmoid(gate_value)
    activated = (gate_value * gate_sigmoid * up_value).astype(jnp.bfloat16)
    mlp_out = jnp.dot(activated, down_full, preferred_element_type=jnp.float32)
    output = (hidden + mlp_out).astype(jnp.bfloat16)
    mlp_again = (
        lax.all_gather(w_in, "grp", axis=0, tiled=True),
        lax.all_gather(w_down, "grp", axis=0, tiled=True),
    )
    in_back = mlp_again[0]
    down_back = mlp_again[1]
    grad_activated = jnp.dot(cotangent, down_back.T, preferred_element_type=jnp.float32)
    grad_gate = (
        grad_activated * up_value * gate_sigmoid * (1.0 + gate_value * (1.0 - gate_sigmoid))
    ).astype(jnp.bfloat16)
    grad_up = (grad_activated * gate_value * gate_sigmoid).astype(jnp.bfloat16)
    grad_gate_up = jnp.stack([grad_gate, grad_up], axis=1)
    grad_mlp_input = jnp.einsum(
        "tcf,dcf->td", grad_gate_up, in_back, preferred_element_type=jnp.float32
    )
    grad_hidden_norm, gain_rows_mlp = norm_back(
        grad_mlp_input, normed_second, scale_second, gain_mlp
    )
    term_in = jnp.einsum("td,tcf->dcf", mlp_input, grad_gate_up, preferred_element_type=jnp.float32)
    term_down = jnp.dot(activated.T, cotangent, preferred_element_type=jnp.float32)
    mlp_terms = (
        lax.psum_scatter(
            term_in.astype(jnp.bfloat16), "grp", scatter_dimension=0, tiled=True
        ).astype(jnp.float32),
        lax.psum_scatter(
            term_down.astype(jnp.bfloat16), "grp", scatter_dimension=0, tiled=True
        ).astype(jnp.float32),
        lax.psum_scatter(
            jnp.sum(gain_rows_mlp, axis=0).astype(jnp.bfloat16),
            "grp",
            scatter_dimension=0,
            tiled=True,
        ).astype(jnp.float32),
    )
    grad_hidden = cotangent.astype(jnp.float32) + grad_hidden_norm
    grad_branch = grad_hidden.astype(jnp.bfloat16)
    attn_again = (
        lax.all_gather(w_qkvg, "grp", axis=0, tiled=True),
        lax.all_gather(w_out, "grp", axis=0, tiled=True),
    )
    qkvg_back = attn_again[0]
    out_back = attn_again[1]
    grad_attn_out = jnp.dot(grad_branch, out_back.T, preferred_element_type=jnp.float32)
    attended_gradient = (grad_attn_out * gate_sig).astype(jnp.bfloat16)
    grad_gate_raw = (grad_attn_out * attended * gate_sig * (1.0 - gate_sig)).astype(jnp.bfloat16)
    key_returned, value_returned = (
        lax.all_gather(key_local, "grp", axis=1, tiled=True),
        lax.all_gather(value_local, "grp", axis=1, tiled=True),
    )
    scores_again, allowed_again = attention_scores(
        query_head_groups, key_returned, query_pos, key_pos
    )
    probs_exact = jnp.where(allowed_again, jnp.exp(scores_again - log_total), 0.0)
    probs_low = probs_exact.astype(jnp.bfloat16)
    head_gradient = attended_gradient.reshape(
        GROUP_SEQUENCES, 2 * BLOCK_TOKENS, KEY_VALUE_HEADS, group_layout, HEAD_SIZE
    )
    value_recomputed = value_returned.reshape(GROUP_SEQUENCES, -1, KEY_VALUE_HEADS, HEAD_SIZE)
    key_recomputed = key_returned.reshape(GROUP_SEQUENCES, -1, KEY_VALUE_HEADS, HEAD_SIZE)
    term_values = jnp.einsum(
        "shgqk,sqhgd->skhd", probs_low, head_gradient, preferred_element_type=jnp.float32
    )
    grad_probs = jnp.einsum(
        "sqhgd,skhd->shgqk", head_gradient, value_recomputed, preferred_element_type=jnp.float32
    )
    inner_sum = jnp.sum(probs_exact * grad_probs, axis=-1, keepdims=True)
    grad_scores = (probs_exact * (grad_probs - inner_sum)).astype(jnp.bfloat16)
    grad_query = jnp.einsum(
        "shgqk,skhd->sqhgd", grad_scores, key_recomputed, preferred_element_type=jnp.float32
    ) * HEAD_SIZE ** (-0.5)
    term_keys = jnp.einsum(
        "shgqk,sqhgd->skhd", grad_scores, query_head_groups, preferred_element_type=jnp.float32
    ) * HEAD_SIZE ** (-0.5)
    key_gradient, value_grads = (
        lax.psum_scatter(term_keys, "grp", scatter_dimension=1, tiled=True),
        lax.psum_scatter(term_values, "grp", scatter_dimension=1, tiled=True),
    )
    grad_query_rot = unrotate_pairs(
        grad_query.reshape(GROUP_SEQUENCES, 2 * BLOCK_TOKENS, QUERY_HEADS, HEAD_SIZE),
        cosine_lookup,
        sine_lookup,
    ).reshape(shard_local_rows, QUERY_HEADS, HEAD_SIZE)
    grad_query_raw, gain_rows_query = norm_back(
        grad_query_rot, query_normed, query_scale, gain_query
    )
    rotated_key_gradient = unrotate_pairs(key_gradient, cosine_lookup, sine_lookup).reshape(
        shard_local_rows, KEY_VALUE_HEADS, HEAD_SIZE
    )
    grad_key_raw, gain_rows_key = norm_back(
        rotated_key_gradient, key_after_norm, key_scale, key_norm_gain
    )
    grad_projected = jnp.concatenate(
        [
            grad_query_raw.reshape(shard_local_rows, query_cols).astype(jnp.bfloat16),
            grad_gate_raw,
            grad_key_raw.reshape(shard_local_rows, key_column_span).astype(jnp.bfloat16),
            value_grads.reshape(shard_local_rows, key_column_span).astype(jnp.bfloat16),
        ],
        axis=-1,
    )
    grad_attn_input = jnp.dot(grad_projected, qkvg_back.T, preferred_element_type=jnp.float32)
    grad_residual_norm, gain_rows_attn = norm_back(
        grad_attn_input, normed_first, scale_first, gain_attn
    )
    grad_tokens = (grad_hidden + grad_residual_norm).astype(jnp.bfloat16)
    gain_attn_sum = jnp.sum(gain_rows_attn, axis=0)
    gain_query_sum = jnp.sum(gain_rows_query, axis=(0, 1))
    gain_key_sum = jnp.sum(gain_rows_key, axis=(0, 1))
    term_qkvg = jnp.dot(attn_input.T, grad_projected, preferred_element_type=jnp.float32)
    term_out = jnp.dot(attn_out.T, grad_branch, preferred_element_type=jnp.float32)
    attn_terms = (
        lax.psum_scatter(
            term_qkvg.astype(jnp.bfloat16), "grp", scatter_dimension=0, tiled=True
        ).astype(jnp.float32),
        lax.psum_scatter(
            term_out.astype(jnp.bfloat16), "grp", scatter_dimension=0, tiled=True
        ).astype(jnp.float32),
        lax.psum_scatter(
            gain_attn_sum.astype(jnp.bfloat16), "grp", scatter_dimension=0, tiled=True
        ).astype(jnp.float32),
        lax.psum_scatter(
            gain_query_sum.astype(jnp.bfloat16), "grp", scatter_dimension=0, tiled=True
        ).astype(jnp.float32),
        lax.psum_scatter(
            gain_key_sum.astype(jnp.bfloat16), "grp", scatter_dimension=0, tiled=True
        ).astype(jnp.float32),
    )
    shard_qkvg = attn_terms[0]
    shard_out = attn_terms[1]
    shard_in = mlp_terms[0]
    shard_down = mlp_terms[1]
    gain_shards = (attn_terms[2], attn_terms[3], attn_terms[4], mlp_terms[2])
    summed = lax.psum(
        (
            shard_qkvg,
            shard_out,
            shard_in,
            shard_down,
            gain_shards[0],
            gain_shards[1],
            gain_shards[2],
            gain_shards[3],
        ),
        "rep",
    )
    return (
        output,
        grad_tokens,
        summed[0],
        summed[1],
        summed[2],
        summed[3],
        summed[4],
        summed[5],
        summed[6],
        summed[7],
    )


def solution(mesh):
    placed = (
        P(("rep", "grp"), None),
        P("rep", None),
        P("grp", None),
        P("grp", None),
        P("grp", None, None),
        P("grp", None),
        P("grp"),
        P("grp"),
        P("grp"),
        P("grp"),
        P(("rep", "grp"), None),
    )
    return jax.shard_map(
        body,
        mesh=mesh,
        in_specs=placed,
        out_specs=(
            P(("rep", "grp"), None),
            P(("rep", "grp"), None),
            P("grp", None),
            P("grp", None),
            P("grp", None, None),
            P("grp", None),
            P("grp"),
            P("grp"),
            P("grp"),
            P("grp"),
        ),
        check_vma=False,
    )
```

profile of v0, /device:TPU:0, one launch (start us, length us, event | category | flops | bytes accessed | tf_op | source)
XLA Modules:
  0.0 3338.5 jit_solution(9908146202313470460)
XLA Ops:
  8.0 13.4 all-gather
  21.8 210.5 %all-gather.9.cloned.1.call-done = bf16[2048,6144]{1,0:T(8,128)(2,1)} async-done(((bf16[256,6144]{1,0:T(8,128)(2,1)}), bf16[2048,6144]{1,0:T(8,128)(2,1)}) %all-gather.9.cloned.1.call-update) | async-done | bytes 25165840 | tf_op jit(solution)/shard_map/all_gather | solution.py:88
  232.3 11.8 fusion.57
  244.1 2.7 copy-done.9
  249.5 14.2 all-reduce.8
  265.3 2.7 fusion.76
  273.7 8.1 copy.179
  282.7 8.5 all-gather.1
  291.6 4.4 fusion.75
  297.2 2.0 copy.218
  299.2 2.3 copy.174
  301.5 4.2 reshape.319
  305.7 2.8 copy.172
  308.5 2.7 multiply_multiply_fusion
  311.4 1.6 fusion.44
  313.0 6.3 copy.166
  319.4 22.3 all-gather.13.cloned.1.call-done
  341.7 12.1 fusion.5
  353.9 9.6 fusion.6
  363.5 9.8 fusion.45
  373.3 4.1 copy.178
  377.5 3.0 reshape.321
  380.4 3.9 multiply_convert_fusion.6
  384.3 39.2 %all-gather.15.cloned.1.call-done = bf16[2048,2048]{1,0:T(8,128)(2,1)} async-done(((bf16[256,2048]{1,0:T(8,128)(2,1)}), bf16[2048,2048]{1,0:T(8,128)(2,1)}) %all-gather.15.cloned.1.call-update) | async-done | bytes 8388624 | tf_op jit(solution)/shard_map/all_gather | solution.py:89
  423.5 6.4 multiply_reduce_fusion.4
  429.9 420.6 %all-gather.17.cloned.1.call-done = bf16[2048,2,6144]{2,0,1:T(8,128)(2,1)} async-done(((bf16[256,2,6144]{2,0,1:T(8,128)(2,1)}), bf16[2048,2,6144]{2,0,1:T(8,128)(2,1)}) %all-gather.17.cloned.1.call-update) | async-done | bytes 50331664 | tf_op jit(solution)/shard_map/all_gather | solution.py:151
  850.5 28.2 fusion.62
  878.7 191.4 %all-gather.19.cloned.1.call-done = bf16[6144,2048]{1,0:T(8,128)(2,1)} async-done(((bf16[768,2048]{1,0:T(8,128)(2,1)}), bf16[6144,2048]{1,0:T(8,128)(2,1)}) %all-gather.19.cloned.1.call-update) | async-done | bytes 25165840 | tf_op jit(solution)/shard_map/all_gather | solution.py:152
  1070.1 20.3 fusion.25
  1090.4 23.9 multiply_reduce_fusion
  1114.3 2.6 multiply_add_fusion
  1117.0 8.6 multiply_convert_fusion.3
  1127.4 14.0 fusion
  1141.4 12.6 fusion.2
  1154.0 3.3 copy-done
  1157.3 6.1 fusion.10
  1163.5 13.4 fusion.17
  1176.9 1.5 copy-done.4
  1178.7 5.7 convolution_convert_fusion.3
  1184.5 1.8 copy-done.21
  1186.3 13.2 convolution_convert_fusion.1
  1202.3 7.5 bitcast_multiply_fusion.6
  1209.8 2.6 copy.183
  1213.8 2.1 copy.184
  1215.9 3.3 copy.185
  1219.2 3.4 multiply_reduce_fusion.1
  1222.7 4.1 reshape.323
  1226.8 2.2 pad_maximum_fusion.6
  1230.7 4.6 fusion.38
  1235.3 16.0 reduce-scatter.7.cloned.1.call-done
  1254.5 87.7 %reduce-scatter.9.cloned.1.call-done = f32[2,128,8,128]{1,3,2,0:T(8,128)} async-done(((f32[2,1024,8,128]{1,3,2,0:T(8,128)}), f32[2,128,8,128]{1,3,2,0:T(8,128)}) %reduce-scatter.9.cloned.1.call-update) | async-done | bytes 1048592 | tf_op jit(solution)/shard_map/reduce_scatter | solution.py:243
  1344.7 2.1 fusion.49
  1347.6 12.5 convolution_convert_fusion.2
  1361.7 23.0 convolution_convert_fusion
  1386.0 13.5 fusion.27
  1399.6 32.9 reduce-scatter.13.cloned.1.call-done
  1432.5 15.1 fusion.34
  1447.6 15.7 all-reduce.7
  1463.5 3.2 fusion.33
  1466.7 214.5 %reduce-scatter.17.cloned.1.call-done = bf16[768,2048]{1,0:T(8,128)(2,1)} async-done(((bf16[6144,2048]{1,0:T(8,128)(2,1)}), bf16[768,2048]{1,0:T(8,128)(2,1)}) %reduce-scatter.17.cloned.1.call-update) | async-done | bytes 3145744 | tf_op jit(solution)/shard_map/reduce_scatter | solution.py:192
  1681.2 247.9 %reduce-scatter.11.cloned.1.call-done = bf16[256,6144]{1,0:T(8,128)(2,1)} async-done(((bf16[2048,6144]{1,0:T(8,128)(2,1)}), bf16[256,6144]{1,0:T(8,128)(2,1)}) %reduce-scatter.11.cloned.1.call-update) | async-done | bytes 3145744 | tf_op jit(solution)/shard_map/reduce_scatter | solution.py:279
  1929.1 483.7 %reduce-scatter.15.cloned.1.call-done = bf16[256,2,6144]{2,0,1:T(8,128)(2,1)} async-done(((bf16[2048,2,6144]{2,0,1:T(8,128)(2,1)}), bf16[256,2,6144]{2,0,1:T(8,128)(2,1)}) %reduce-scatter.15.cloned.1.call-update) | async-done | bytes 6291472 | tf_op jit(solution)/shard_map/reduce_scatter | solution.py:189
  2412.8 896.4 %all-reduce.10 = (f32[256,6144]{1,0:T(8,128)}, f32[256,2048]{1,0:T(8,128)}, f32[256,2,6144]{2,0,1:T(8,128)}, f32[768,2048]{1,0:T(8,128)}, f32[256]{0:T(256)}, /*index=5*/f32[16]{0:T(128)}, f32[16]{0:T(128)}, f32[256]{0:T(256)}) all-reduce(bf16[256,6144]{1,0:T(8,128)(2,1)} %reduce-scatter.11.cloned.1.cal, ...), channel_id=1, replica_groups=mesh['rep'=4,'grp'=8] {'rep'}, use_global_device_ids=true, to_apply=%region_14.15 | all-reduce | flops 6816288 | bytes 40898816 | tf_op jit(solution)/shard_map/psum | solution.py:300
  3309.2 22.0 copy.197
  (235 shorter events, 29.0 us)
Async XLA Ops:
  7.2 14.3 copy-start.14
  7.2 225.1 %all-gather.9.cloned.1.call-start = ((), (), s32[]{:S(2)}) async-start(), calls=%async_computation.6 | async-start | bytes 28311552 | tf_op jit(solution)/shard_map/all_gather | solution.py:88
  7.9 305.1 %all-gather.11.cloned.1.call-start = ((), (), s32[]{:S(2)}) async-start(), calls=%async_computation.7 | async-start | bytes 4718592 | tf_op jit(solution)/shard_map/all_gather | solution.py:130
  21.5 222.6 %copy-start.33 = (f32[8,1,256]{2,1,0:T(1,128)}, f32[8,1,256]{2,1,0:T(1,128)S(1)}, u32[]{:S(2)}) copy-start(f32[8,1,256]{2,1,0:T(1,128)S(1)} %convert_element_type.183) | copy-start | bytes 24580
  21.8 222.3 %copy-start.37 = (f32[256]{0:T(256)}, f32[256]{0:T(256)S(1)}, u32[]{:S(2)}) copy-start(f32[256]{0:T(256)S(1)} %add_rsqrt_fusion.3) | copy-start | bytes 3076
  232.3 15.4 copy-start.59
  232.3 16.7 copy-start.62
  232.3 17.0 copy-start.63
  232.3 31.4 copy-start.53
  244.1 2.7 copy-start.9
  247.7 94.1 %all-gather.13.cloned.1.call-start = ((), (), s32[]{:S(2)}) async-start(), calls=%async_computation.8 | async-start | bytes 4718592 | tf_op jit(solution)/shard_map/all_gather | solution.py:129
  263.7 7.7 copy-start.50
  263.9 4.1 copy-start.46
  264.0 3.9 copy-start.57
  264.0 3.9 copy-start.54
  265.3 46.1 %copy-start.24 = (f32[2,128,128]{1,2,0:T(8,128)}, f32[2,128,128]{1,2,0:T(8,128)S(1)}, u32[]{:S(2)}) copy-start(f32[2,128,128]{1,2,0:T(8,128)S(1)} %get-tuple-element.115) | copy-start | bytes 393220
  265.3 46.1 %copy-start.30 = (f32[2,128,128]{1,2,0:T(8,128)}, f32[2,128,128]{1,2,0:T(8,128)S(1)}, u32[]{:S(2)}) copy-start(f32[2,128,128]{1,2,0:T(8,128)S(1)} %get-tuple-element.116) | copy-start | bytes 393220
  265.3 6.5 copy-start.42
  273.0 150.5 %all-gather.15.cloned.1.call-start = ((), (), s32[]{:S(2)}) async-start(), calls=%async_computation.9 | async-start | bytes 9437184 | tf_op jit(solution)/shard_map/all_gather | solution.py:89
  273.6 576.9 %all-gather.17.cloned.1.call-start = ((), (), s32[]{:S(2)}) async-start(), calls=%async_computation.10 | async-start | bytes 56623104 | tf_op jit(solution)/shard_map/all_gather | solution.py:151
  281.8 788.3 %all-gather.19.cloned.1.call-start = ((), (), s32[]{:S(2)}) async-start(), calls=%async_computation.11 | async-start | bytes 28311552 | tf_op jit(solution)/shard_map/all_gather | solution.py:152
  282.4 969.0 %reduce-scatter.7.cloned.1.call-start = ((), (), s32[]{:S(2)}) async-start(), calls=%async_computation.12 | async-start | bytes 9437184 | tf_op jit(solution)/shard_map/reduce_scatter | solution.py:242
  282.4 29.0 copy-start.48
  297.0 4.5 copy-start.28
  301.5 9.9 copy-start.39
  308.5 2.9 copy-start.6
  313.0 28.7 copy-start.12
  353.9 9.6 copy-start.8
  380.4 3.9 copy-start.17
  429.9 684.5 %copy-start.1 = (f32[256,2048]{1,0:T(8,128)}, f32[256,2048]{1,0:T(8,128)S(1)}, u32[]{:S(2)}) copy-start(f32[256,2048]{1,0:T(8,128)S(1)} %get-tuple-element.124) | copy-start | bytes 6291460
  1114.3 2.6 copy-start.18
  1117.0 8.6 copy-start.3
  1141.4 15.9 copy-start.13
  1154.0 3.3 copy-start
  1163.4 178.8 %reduce-scatter.9.cloned.1.call-start = ((), (), s32[]{:S(2)}) async-start(), calls=%async_computation.13 | async-start | bytes 9437184 | tf_op jit(solution)/shard_map/reduce_scatter | solution.py:243
  1176.8 1.9 copy-start.20
  1176.9 255.6 %reduce-scatter.13.cloned.1.call-start = ((), (), s32[]{:S(2)}) async-start(), calls=%async_computation.15 | async-start | bytes 9437184 | tf_op jit(solution)/shard_map/reduce_scatter | solution.py:282
  1184.4 1.9 copy-start.21
  1184.5 496.7 %reduce-scatter.17.cloned.1.call-start = ((), (), s32[]{:S(2)}) async-start(), calls=%async_computation.17 | async-start | bytes 28311552 | tf_op jit(solution)/shard_map/reduce_scatter | solution.py:192
  1199.5 2.0 copy-start.49
  1199.5 2.6 copy-start.45
  1199.6 729.5 %reduce-scatter.11.cloned.1.call-start = ((), (), s32[]{:S(2)}) async-start(), calls=%async_computation.14 | async-start | bytes 28311552 | tf_op jit(solution)/shard_map/reduce_scatter | solution.py:279
  1209.8 2.6 copy-start.25
  1213.8 5.4 copy-start.7
  1213.8 5.4 copy-start.35
  1222.6 4.2 copy-start.16
  1226.8 2.9 copy-start.29
  1229.0 1.7 copy-start.19
  1229.0 1.7 copy-start.44
  1235.3 111.5 %copy-start.22 = (bf16[256,2048]{1,0:T(8,128)(2,1)}, bf16[256,2048]{1,0:T(8,128)(2,1)S(1)}, u32[]{:S(2)}) copy-start(bf16[256,2048]{1,0:T(8,128)(2,1)S(1)} %fusion.38) | copy-start | bytes 3145732
  1235.3 17.5 copy-start.11
  1235.3 17.5 copy-start.31
  1235.3 17.5 copy-start.51
  1254.5 90.2 %copy-start.43 = (f32[1024]{0:T(1024)S(1)}, f32[1024]{0:T(1024)}, u32[]{:S(2)}) copy-start(f32[1024]{0:T(1024)} %copy-done.42) | copy-start | bytes 12292
  1343.9 2.8 copy-start.26
  1344.3 3.3 copy-start.15
  1344.3 3.3 copy-start.32
  1344.3 3.2 copy-start.34
  1344.3 3.2 copy-start.38
  1360.1 1052.7 %reduce-scatter.15.cloned.1.call-start = ((), (), s32[]{:S(2)}) async-start(), calls=%async_computation.16 | async-start | bytes 56623104 | tf_op jit(solution)/shard_map/reduce_scatter | solution.py:189
  1399.6 48.0 %copy-start.52 = (bf16[2048]{0:T(1024)(128)(2,1)S(1)}, bf16[2048]{0:T(1024)(128)(2,1)}, u32[]{:S(2)}) copy-start(bf16[2048]{0:T(1024)(128)(2,1)} %get-tuple-element.72) | copy-start | bytes 12292
  1399.6 48.0 %copy-start.56 = (bf16[128]{0:T(256)(128)(2,1)S(1)}, bf16[128]{0:T(256)(128)(2,1)}, u32[]{:S(2)}) copy-start(bf16[128]{0:T(256)(128)(2,1)} %get-tuple-element.76) | copy-start | bytes 772
  1399.6 48.0 %copy-start.60 = (bf16[128]{0:T(256)(128)(2,1)S(1)}, bf16[128]{0:T(256)(128)(2,1)}, u32[]{:S(2)}) copy-start(bf16[128]{0:T(256)(128)(2,1)} %get-tuple-element.70) | copy-start | bytes 772
  1399.6 63.9 %copy-start.5 = (f32[256,2048]{1,0:T(8,128)S(1)}, f32[256,2048]{1,0:T(8,128)}, u32[]{:S(2)}) copy-start(f32[256,2048]{1,0:T(8,128)} %copy-done.3) | copy-start | bytes 6291460
  (13 other events, 14.0 us)
Sparse Core Ops, SparseCore 0:
  9.7 222.5 all-gather.8
  247.8 45.7 all-gather.10
  295.1 46.5 all-gather.12
  343.2 80.2 all-gather.14
  425.5 424.9 all-gather.16
  852.0 218.0 all-gather.18
  1163.5 87.7 reduce-scatter.6
  1254.2 87.9 reduce-scatter.8
  1344.5 87.9 reduce-scatter.12
  1434.7 246.4 reduce-scatter.16
  1683.6 245.4 reduce-scatter.10
  1931.3 481.4 reduce-scatter.14
where the time goes:
time: 3350 us; the launch traced here: 3340 us
  waiting for transfers between devices  1970 us (59%)
  blocking collectives  948 us (28%)
  matrix products  245 us (7%)
  local copies, waits for them, and re-layouts  91 us (3%)
  other arithmetic  67.3 us (2%)
    psum x1, blocking collectives, body(): lax.psum((shard_qkvg, shard_out, shard_in, shard_down, gain_shards[0], ga...  896 us
    reduce_scatter x1, waiting for transfers between devices, body(): lax.psum_scatter(term_in.astype(jnp.bfloat16), 'grp', scatter_dimension=0...  484 us
    all_gather x1, waiting for transfers between devices, body(): lax.all_gather(w_in, 'grp', axis=0, tiled=True)  421 us
    reduce_scatter x1, waiting for transfers between devices, body(): lax.psum_scatter(term_qkvg.astype(jnp.bfloat16), 'grp', scatter_dimension...  248 us
    reduce_scatter x1, waiting for transfers between devices, body(): lax.psum_scatter(term_down.astype(jnp.bfloat16), 'grp', scatter_dimension...  215 us
    all_gather x1, waiting for transfers between devices, body(): lax.all_gather(w_qkvg, 'grp', axis=0, tiled=True)  210 us
    all_gather x1, waiting for transfers between devices, body(): lax.all_gather(w_down, 'grp', axis=0, tiled=True)  191 us
    reduce_scatter x1, waiting for transfers between devices, body(): lax.psum_scatter(term_values, 'grp', scatter_dimension=1, tiled=True)  87.7 us
  transfers between devices with their start and end apart: 12, of which 11 were waited for; matrix products, arithmetic and copies ran while one was open for 8% of the time, Pallas kernels for 0%

commit v1 on v0

v1 whole, which is shorter than its diff:
```python
import jax
import jax.numpy as jnp
from jax import lax
from jax.sharding import PartitionSpec as P

QUERY_HEADS = 16
KEY_VALUE_HEADS = 8
HEAD_SIZE = 128
BLOCK_TOKENS = 64
GROUP_SEQUENCES = 2


norm_epsilon = 1e-06
rotary_base = 1000000.0
masked_value = -1e30


def row_scale(values):
    return lax.rsqrt(jnp.mean(values * values, axis=-1, keepdims=True) + norm_epsilon)


def rotate_half(values):
    middle = values.shape[-1] // 2
    return jnp.concatenate([-values[..., middle:], values[..., :middle]], axis=-1)


def rotary_tables(positions):
    exponent = jnp.arange(HEAD_SIZE // 2, dtype=jnp.float32) * (2.0 / HEAD_SIZE)
    inverse = jnp.power(jnp.float32(rotary_base), -exponent)
    angles = positions.astype(jnp.float32)[..., None] * inverse
    angles = jnp.concatenate([angles, angles], axis=-1)
    return (jnp.cos(angles), jnp.sin(angles))


def unrotate_pairs(gradient, cosine_lookup, sine_lookup):
    return gradient * cosine_lookup - rotate_half(gradient * sine_lookup)


def norm_back(grad_out, normed, scale_rows, gain_vector):
    weighted = grad_out * gain_vector
    grad_in = scale_rows * (weighted - normed * jnp.mean(weighted * normed, axis=-1, keepdims=True))
    return (grad_in, grad_out * normed)


def positions_of(block_ids):
    offsets = jnp.arange(BLOCK_TOKENS, dtype=jnp.int32)
    return (block_ids[:, :, None] * BLOCK_TOKENS + offsets[None, None, :]).reshape(
        block_ids.shape[0], -1
    )


def to_columns(piece):
    reps = lax.axis_size("rep")
    rows, owners, columns = piece.shape
    share = rows // reps
    mine = lax.dynamic_slice_in_dim(piece, lax.axis_index("rep") * share, share, 0)
    swapped = lax.all_to_all(mine, "grp", 1, 0, tiled=True)
    swapped = swapped.reshape(owners, share, columns)
    whole = lax.all_gather(swapped, "rep", axis=1, tiled=True)
    return whole.reshape(owners * rows, columns)


def to_rows(gradient):
    reps = lax.axis_size("rep")
    owners = lax.axis_size("grp")
    rows = gradient.shape[0] // owners
    shaped = gradient.reshape(owners, reps, rows // reps, -1)
    shaped = jnp.swapaxes(shaped, 0, 1).reshape(gradient.shape)
    share = lax.psum_scatter(shaped, "rep", scatter_dimension=0, tiled=True)
    share = share.reshape(owners, rows // reps, -1)
    swapped = lax.all_to_all(share, "grp", 0, 0, tiled=True)
    return lax.all_gather(jnp.swapaxes(swapped, 0, 1), "rep", axis=0, tiled=True)


def sum_rep(gradient):
    share = lax.psum_scatter(gradient, "rep", scatter_dimension=0, tiled=True)
    return lax.all_gather(share, "rep", axis=0, tiled=True)


def body(
    tokens,
    block_map,
    w_qkvg,
    w_out,
    w_in,
    w_down,
    norm_attn,
    norm_query,
    norm_key,
    norm_mlp,
    cotangent,
):
    owners = lax.axis_size("grp")
    me = lax.axis_index("grp")
    heads = QUERY_HEADS // owners
    sharers = max(1, owners // KEY_VALUE_HEADS)
    kv_heads = KEY_VALUE_HEADS * sharers // owners
    per_kv = heads // kv_heads
    q_cols = heads * HEAD_SIZE
    kv_cols = kv_heads * HEAD_SIZE
    rows_here, width = tokens.shape
    shard = w_qkvg.shape[0]
    block_rows = 2 * BLOCK_TOKENS
    seq_len = owners * block_rows
    all_q = QUERY_HEADS * HEAD_SIZE
    all_kv = KEY_VALUE_HEADS * HEAD_SIZE
    hidden_units = w_down.shape[0]

    def by_owner(part, repeat):
        split = part.reshape(shard, owners // repeat, -1)
        return jnp.repeat(split, repeat, axis=1) if repeat > 1 else split

    qkvg_pieces = jnp.concatenate(
        [
            by_owner(w_qkvg[:, :all_q], 1),
            by_owner(w_qkvg[:, all_q : 2 * all_q], 1),
            by_owner(w_qkvg[:, 2 * all_q : 2 * all_q + all_kv], sharers),
            by_owner(w_qkvg[:, 2 * all_q + all_kv :], sharers),
        ],
        axis=2,
    )
    in_pieces = jnp.swapaxes(w_in.reshape(shard, 2, owners, hidden_units), 1, 2).reshape(
        shard, owners, 2 * hidden_units
    )
    tokens_all = lax.all_gather(tokens, "grp", axis=0, tiled=True)
    qkvg_cols = to_columns(qkvg_pieces)
    small = jnp.concatenate([norm_attn, norm_mlp, norm_query, norm_key])
    small_all = lax.all_gather(small, "grp", axis=0, tiled=False).astype(jnp.float32)
    head_part = norm_query.shape[0]
    gain_attn = small_all[:, :shard].reshape(-1)
    gain_mlp = small_all[:, shard : 2 * shard].reshape(-1)
    gain_query = small_all[:, 2 * shard : 2 * shard + head_part].reshape(-1)
    gain_key = small_all[:, 2 * shard + head_part :].reshape(-1)
    in_cols = to_columns(in_pieces)
    cotangent_all = lax.all_gather(cotangent, "grp", axis=0, tiled=True)

    positions = positions_of(block_map)
    cosine, sine = rotary_tables(positions)
    cosine = cosine[:, None]
    sine = sine[:, None]

    def to_heads(values):
        count = values.shape[-1] // HEAD_SIZE
        shaped = values.reshape(owners, GROUP_SEQUENCES, block_rows, count, HEAD_SIZE)
        return shaped.transpose(1, 3, 0, 2, 4).reshape(
            GROUP_SEQUENCES, count, seq_len, HEAD_SIZE
        )

    def from_heads(values):
        count = values.shape[1]
        shaped = values.reshape(GROUP_SEQUENCES, count, owners, block_rows, HEAD_SIZE)
        return shaped.transpose(2, 0, 3, 1, 4).reshape(-1, count * HEAD_SIZE)

    wide_tokens = tokens_all.astype(jnp.float32)
    normed_first = wide_tokens * row_scale(wide_tokens)
    attn_input = (normed_first * gain_attn).astype(jnp.bfloat16)
    projected = jnp.dot(attn_input, qkvg_cols, preferred_element_type=jnp.float32)
    query_heads = to_heads(projected[:, :q_cols])
    gate_raw = projected[:, q_cols : 2 * q_cols]
    key_heads = to_heads(projected[:, 2 * q_cols : 2 * q_cols + kv_cols])
    value_heads = to_heads(projected[:, 2 * q_cols + kv_cols :]).astype(jnp.bfloat16)
    query_scale = row_scale(query_heads)
    query_normed = query_heads * query_scale
    key_scale = row_scale(key_heads)
    key_normed = key_heads * key_scale

    def rotate(values):
        return (values * cosine + rotate_half(values) * sine).astype(jnp.bfloat16)

    query_rot = rotate(query_normed * gain_query).reshape(
        GROUP_SEQUENCES, kv_heads, per_kv, seq_len, HEAD_SIZE
    )
    key_rot = rotate(key_normed * gain_key)
    scores = jnp.einsum(
        "shgqd,shkd->shgqk", query_rot, key_rot, preferred_element_type=jnp.float32
    ) * HEAD_SIZE ** (-0.5)
    allowed = (positions[:, None, :] <= positions[:, :, None])[:, None, None]
    scores = jnp.where(allowed, scores, masked_value)
    top_score = jnp.max(scores, axis=-1, keepdims=True)
    exp_scores = jnp.exp(scores - top_score)
    exp_total = jnp.sum(exp_scores, axis=-1, keepdims=True)
    exact = exp_scores / exp_total
    probability = exact.astype(jnp.bfloat16)
    attended = jnp.einsum(
        "shgqk,shkd->shgqd", probability, value_heads, preferred_element_type=jnp.float32
    ).reshape(GROUP_SEQUENCES, heads, seq_len, HEAD_SIZE)
    attended = from_heads(attended)
    gate_sig = jax.nn.sigmoid(gate_raw)
    attn_out = (attended * gate_sig).astype(jnp.bfloat16)

    def scatter_sum(terms):
        return lax.psum_scatter(
            terms.astype(jnp.bfloat16), "grp", scatter_dimension=0, tiled=True
        ).astype(jnp.float32)

    branch = scatter_sum(jnp.dot(attn_out, w_out, preferred_element_type=jnp.float32))
    hidden = tokens.astype(jnp.float32) + branch
    scale_second = row_scale(hidden)
    normed_second = hidden * scale_second
    mlp_input = lax.all_gather(
        (normed_second * gain_mlp).astype(jnp.bfloat16), "grp", axis=0, tiled=True
    )
    gate_up = jnp.dot(mlp_input, in_cols, preferred_element_type=jnp.float32)
    gate_value = gate_up[:, :hidden_units]
    up_value = gate_up[:, hidden_units:]
    gate_sigmoid = jax.nn.sigmoid(gate_value)
    activated = (gate_value * gate_sigmoid * up_value).astype(jnp.bfloat16)
    grad_activated = jnp.dot(cotangent_all, w_down.T, preferred_element_type=jnp.float32)
    grad_gate = (
        grad_activated * up_value * gate_sigmoid * (1.0 + gate_value * (1.0 - gate_sigmoid))
    ).astype(jnp.bfloat16)
    grad_up = (grad_activated * gate_value * gate_sigmoid).astype(jnp.bfloat16)
    grad_gate_up = jnp.concatenate([grad_gate, grad_up], axis=1)
    grad_mlp_input = scatter_sum(
        jnp.dot(grad_gate_up, in_cols.T, preferred_element_type=jnp.float32)
    )
    mlp_out = scatter_sum(jnp.dot(activated, w_down, preferred_element_type=jnp.float32))
    output = (hidden + mlp_out).astype(jnp.bfloat16)
    term_in = jnp.dot(mlp_input.T, grad_gate_up, preferred_element_type=jnp.float32)
    term_down = jnp.dot(activated.T, cotangent_all, preferred_element_type=jnp.float32)
    grad_hidden_norm, gain_rows_mlp = norm_back(
        grad_mlp_input, normed_second, scale_second, gain_mlp
    )
    grad_hidden = cotangent.astype(jnp.float32) + grad_hidden_norm
    grad_branch = lax.all_gather(
        grad_hidden.astype(jnp.bfloat16), "grp", axis=0, tiled=True
    )
    shard_down = sum_rep(term_down.astype(jnp.bfloat16)).astype(jnp.float32)
    rows_in = to_rows(term_in.astype(jnp.bfloat16)).astype(jnp.float32)
    shard_in = jnp.swapaxes(rows_in.reshape(shard, owners, 2, hidden_units), 1, 2).reshape(
        w_in.shape
    )
    grad_attn_out = jnp.dot(grad_branch, w_out.T, preferred_element_type=jnp.float32)
    attended_gradient = (grad_attn_out * gate_sig).astype(jnp.bfloat16)
    grad_gate_raw = (grad_attn_out * attended * gate_sig * (1.0 - gate_sig)).astype(jnp.bfloat16)
    term_out = jnp.dot(attn_out.T, grad_branch, preferred_element_type=jnp.float32)
    shard_out = sum_rep(term_out.astype(jnp.bfloat16)).astype(jnp.float32)
    head_gradient = to_heads(attended_gradient).reshape(query_rot.shape)
    grad_value = jnp.einsum(
        "shgqk,shgqd->shkd", probability, head_gradient, preferred_element_type=jnp.float32
    )
    grad_probs = jnp.einsum(
        "shgqd,shkd->shgqk", head_gradient, value_heads, preferred_element_type=jnp.float32
    )
    inner_sum = jnp.sum(exact * grad_probs, axis=-1, keepdims=True)
    grad_scores = (exact * (grad_probs - inner_sum)).astype(jnp.bfloat16)
    grad_query = jnp.einsum(
        "shgqk,shkd->shgqd", grad_scores, key_rot, preferred_element_type=jnp.float32
    ).reshape(query_heads.shape) * HEAD_SIZE ** (-0.5)
    grad_key = jnp.einsum(
        "shgqk,shgqd->shkd", grad_scores, query_rot, preferred_element_type=jnp.float32
    ) * HEAD_SIZE ** (-0.5)
    grad_query_raw, gain_rows_query = norm_back(
        unrotate_pairs(grad_query, cosine, sine), query_normed, query_scale, gain_query
    )
    grad_key_raw, gain_rows_key = norm_back(
        unrotate_pairs(grad_key, cosine, sine), key_normed, key_scale, gain_key
    )
    grad_projected = jnp.concatenate(
        [
            from_heads(grad_query_raw.astype(jnp.bfloat16)),
            grad_gate_raw,
            from_heads(grad_key_raw.astype(jnp.bfloat16)),
            from_heads(grad_value.astype(jnp.bfloat16)),
        ],
        axis=-1,
    )
    term_qkvg = jnp.dot(attn_input.T, grad_projected, preferred_element_type=jnp.float32)
    grad_attn_input = scatter_sum(
        jnp.dot(grad_projected, qkvg_cols.T, preferred_element_type=jnp.float32)
    )
    own_tokens = tokens.astype(jnp.float32)
    own_scale = row_scale(own_tokens)
    grad_residual_norm, gain_rows_attn = norm_back(
        grad_attn_input, own_tokens * own_scale, own_scale, gain_attn
    )
    grad_tokens = (grad_hidden + grad_residual_norm).astype(jnp.bfloat16)
    rows_qkvg = to_rows(term_qkvg.astype(jnp.bfloat16)).astype(jnp.float32)

    def joined(part, repeat):
        if repeat > 1:
            part = part.reshape(shard, owners // repeat, repeat, -1).sum(2)
        return part.reshape(shard, -1)

    shard_qkvg = jnp.concatenate(
        [
            joined(rows_qkvg[:, :, :q_cols], 1),
            joined(rows_qkvg[:, :, q_cols : 2 * q_cols], 1),
            joined(rows_qkvg[:, :, 2 * q_cols : 2 * q_cols + kv_cols], sharers),
            joined(rows_qkvg[:, :, 2 * q_cols + kv_cols :], sharers),
        ],
        axis=1,
    )
    gains = lax.psum(
        jnp.concatenate(
            [
                jnp.sum(gain_rows_attn, axis=0),
                jnp.sum(gain_rows_mlp, axis=0),
                jnp.sum(gain_rows_query, axis=(0, 1, 2)),
                jnp.sum(gain_rows_key, axis=(0, 1, 2)),
            ]
        ),
        ("rep", "grp"),
    )
    return (
        output,
        grad_tokens,
        shard_qkvg,
        shard_out,
        shard_in,
        shard_down,
        lax.dynamic_slice_in_dim(gains, me * shard, shard),
        lax.dynamic_slice_in_dim(gains, 2 * width + me * head_part, head_part),
        lax.dynamic_slice_in_dim(gains, 2 * width + HEAD_SIZE + me * head_part, head_part),
        lax.dynamic_slice_in_dim(gains, width + me * shard, shard),
    )


def solution(mesh):
    placed = (
        P(("rep", "grp"), None),
        P("rep", None),
        P("grp", None),
        P("grp", None),
        P("grp", None, None),
        P("grp", None),
        P("grp"),
        P("grp"),
        P("grp"),
        P("grp"),
        P(("rep", "grp"), None),
    )
    return jax.shard_map(
        body,
        mesh=mesh,
        in_specs=placed,
        out_specs=(
            P(("rep", "grp"), None),
            P(("rep", "grp"), None),
            P("grp", None),
            P("grp", None),
            P("grp", None, None),
            P("grp", None),
            P("grp"),
            P("grp"),
            P("grp"),
            P("grp"),
        ),
        check_vma=False,
    )
```

time: 3350 us -> 1440 us (0.43)
  waiting for transfers between devices: 1970 us -> 722 us
  blocking collectives: 948 us -> 229 us
  local copies, waits for them, and re-layouts: 91 us -> 170 us
  matrix products: 245 us -> 196 us
    psum x1, blocking collectives: 896 us -> 39.9 us  [body(): lax.psum(jnp.concatenate([jnp.sum(gain_rows_attn, axis=0), jnp.sum(gain_r...]
    reduce_scatter x6 -> x8, waiting for transfers between devices: 1080 us -> 277 us  [the longest x4 222 us: scatter_sum(): lax.psum_scatter(terms.astype(jnp.bfloat16), 'grp', scatter_dimension=0,...]
    all_gather x6 -> x10, waiting for transfers between devices: 884 us -> 443 us  [the longest x2 88.2 us: to_rows(): lax.all_gather(jnp.swapaxes(swapped, 0, 1), 'rep', axis=0, tiled=True)]
    all_to_all x0 -> x4, blocking collectives: none -> 162 us  [the longest x2 94 us: to_columns(): swapped = lax.all_to_all(mine, 'grp', 1, 0, tiled=True)]
    dot_general x16 -> x15, matrix products: 227 us -> 165 us  [the longest x1 19.1 us: body(): gate_up = jnp.dot(mlp_input, in_cols, preferred_element_type=jnp.float32)]
    reshape x9 -> x13, local copies, waits for them, and re-layouts: 18.8 us -> 56.4 us  [the longest x1 14.4 us: body(): jnp.swapaxes(w_in.reshape(shard, 2, owners, hidden_units), 1, 2)]
  transfers between devices with their start and end apart: 12 -> 18, of which waited for: 11 -> 14; matrix products, arithmetic and copies ran while one was open for 8% -> 21% of each run, Pallas kernels for 0% -> 0%
where the time goes in v1:
time: 1440 us; the launch traced here: 1430 us
  waiting for transfers between devices  722 us (50%)
  blocking collectives  229 us (16%)
  matrix products  196 us (14%)
  local copies, waits for them, and re-layouts  170 us (12%)
  other arithmetic  98.5 us (7%)
  between operations  15.9 us (1%)
    reduce_scatter x4, waiting for transfers between devices, scatter_sum(): lax.psum_scatter(terms.astype(jnp.bfloat16), 'grp', scatter_dimension=0,...  222 us
    all_to_all x2, blocking collectives, to_columns(): swapped = lax.all_to_all(mine, 'grp', 1, 0, tiled=True)  94 us
    all_gather x2, waiting for transfers between devices, to_rows(): lax.all_gather(jnp.swapaxes(swapped, 0, 1), 'rep', axis=0, tiled=True)  88.2 us
    all_gather x1, waiting for transfers between devices, body(): lax.all_gather((normed_second * gain_mlp).astype(jnp.bfloat16), 'grp', ax...  84.1 us
    all_gather x2, waiting for transfers between devices, to_columns(): whole = lax.all_gather(swapped, 'rep', axis=1, tiled=True)  82.1 us
    all_gather x1, waiting for transfers between devices, body(): tokens_all = lax.all_gather(tokens, 'grp', axis=0, tiled=True)  79.5 us
    all_to_all x2, blocking collectives, to_rows(): swapped = lax.all_to_all(share, 'grp', 0, 0, tiled=True)  68.3 us
    all_gather x1, waiting for transfers between devices, body(): cotangent_all = lax.all_gather(cotangent, 'grp', axis=0, tiled=True)  62.9 us
  transfers between devices with their start and end apart: 18, of which 14 were waited for; matrix products, arithmetic and copies ran while one was open for 21% of the time, Pallas kernels for 0%

profile of v1, /device:TPU:0, one launch (start us, length us, event | category | flops | bytes accessed | tf_op | source)
XLA Modules:
  0.0 1432.7 jit_solution(3499402709017094940)
XLA Ops:
  9.6 3.1 fusion.71
  21.3 3.0 fusion.45
  26.8 27.4 %all_to_all.40 = bf16[64,8,768]{2,0,1:T(8,128)(2,1)S(1)} all-to-all(bf16[64,8,768]{2,0,1:T(8,128)(2,1)} %copy.164), channel_id=1, replica_groups=mesh['rep'=4,'grp'=8] {'grp'}, dimensions={1} | all-to-all | bytes 1572864 | tf_op jit(solution)/shard_map/all_to_all | solution.py:57
  58.0 27.0 %all-reduce = bf16[4352]{0:T(1024)(128)(2,1)S(1)} all-reduce(bf16[4352]{0:T(1024)(128)(2,1)S(1)} %dynamic-update-slice), channel_id=2, replica_groups=mesh['rep'=4,'grp'=8] {'grp'}, use_global_device_ids=true, to_apply=%add | all-reduce | flops 4352 | bytes 17408
  88.8 9.9 all-gather.30.cloned.1.call-done
  98.6 4.2 copy.166
  102.8 79.5 %all-gather.14.cloned.1.call-done = bf16[2048,2048]{1,0:T(8,128)(2,1)} async-done(((bf16[256,2048]{1,0:T(8,128)(2,1)}), bf16[2048,2048]{1,0:T(8,128)(2,1)}) %all-gather.14.cloned.1.call-update) | async-done | bytes 8388624 | tf_op jit(solution)/shard_map/all_gather | solution.py:125
  182.3 5.2 fusion.1
  188.1 9.1 fusion.19
  208.7 3.2 slice.106
  214.1 3.4 reshape.449
  217.5 4.9 multiply_reduce_fusion.4
  233.2 4.8 fusion.57
  239.9 11.4 fusion.75
  251.3 10.5 fusion.10
  261.8 3.2 copy.175
  269.5 5.7 convolution_convert_fusion.3
  275.3 7.2 copy.223
  282.6 14.4 %reshape.456 = bf16[256,8,1536]{2,0,1:T(8,128)(2,1)} reshape(bf16[256,8,2,768]{3,2,0,1:T(2,128)(2,1)} %bitcast.180) | data formatting | bytes 12582912 | tf_op jit(solution)/shard_map/reshape | solution.py:122
  298.5 66.6 %all_to_all.41 = bf16[64,8,1536]{2,0,1:T(8,128)(2,1)} all-to-all(bf16[64,8,1536]{2,0,1:T(8,128)(2,1)S(1)} %constant_dynamic-slice_fusion), channel_id=1, replica_groups=mesh['rep'=4,'grp'=8] {'grp'}, dimensions={1} | all-to-all | bytes 3145728 | tf_op jit(solution)/shard_map/all_to_all | solution.py:57
  365.2 23.6 %reduce-scatter.9.cloned.1.call-done = bf16[256,2048]{1,0:T(8,128)(2,1)} async-done(((bf16[2048,2048]{1,0:T(8,128)(2,1)}), bf16[256,2048]{1,0:T(8,128)(2,1)}) %reduce-scatter.9.cloned.1.call-update) | async-done | bytes 1048592 | tf_op jit(solution)/shard_map/reduce_scatter | solution.py:192
  394.4 72.2 %all-gather.32.cloned.1.call-done = bf16[8,256,1,1536]{3,1,0,2:T(8,128)(2,1)} async-done(((bf16[8,64,1,1536]{3,1,0,2:T(8,128)(2,1)}), bf16[8,256,1,1536]{3,1,0,2:T(8,128)(2,1)}) %all-gather.32.cloned.1.call-update) | async-done | bytes 6291472 | tf_op jit(solution)/shard_map/all_gather | solution.py:59
  466.6 84.1 %all-gather.16.cloned.1.call-done = bf16[2048,2048]{1,0:T(8,128)(2,1)} async-done(((bf16[256,2048]{1,0:T(8,128)(2,1)}), bf16[2048,2048]{1,0:T(8,128)(2,1)}) %all-gather.16.cloned.1.call-update) | async-done | bytes 8388624 | tf_op jit(solution)/shard_map/all_gather | solution.py:200
  550.7 19.1 %fusion.76 = f32[2048,1536]{0,1:T(8,128)} fusion(bf16[2048,2048]{1,0:T(8,128)(2,1)} %all-gather.16.cloned.1.call-done, bf16[2048,1536]{1,0:T(8,128)(2,1)} %bitcast.234), kind=kOutput, calls=%fused_computation.157 | convolution fusion | flops 12884901888 | bytes 27262976 | tf_op jit(solution)/shard_map/dot_general | solution.py:203
  569.9 62.9 %all-gather.18.cloned.1.call-done = bf16[2048,2048]{1,0:T(8,128)(2,1)} async-done(((bf16[256,2048]{1,0:T(8,128)(2,1)}), bf16[2048,2048]{1,0:T(8,128)(2,1)}) %all-gather.18.cloned.1.call-update) | async-done | bytes 8388624 | tf_op jit(solution)/shard_map/all_gather | solution.py:135
  632.8 15.9 %multiply_convert_fusion.2 = (bf16[2048,768]{0,1:T(8,128)(2,1)S(1)}, bf16[2048,768]{0,1:T(8,128)(2,1)}, bf16[2048,768]{0,1:T(8,128)(2,1)}) fusion(f32[2048,1536]{0,1:T(8,128)} %fusion.76, bf16[2048,2048]{1,0:T(8,128)(2,1)} %all-gather.18.cloned.1.call-done, bf16[768,2048]{1,0:T(8,128)(2,1)S(1)} %copy-done), kind=kOutput, calls=%fused_computation.25 | convolution fusion | flops 6467616768 | bytes 33554432 | tf_op jit(solution)/shard_map/dot_general | solution.py:208
  650.3 18.7 %convolution_convert_fusion.1 = bf16[2048,2048]{1,0:T(8,128)(2,1)} fusion(bf16[2048,1536]{1,0:T(8,128)(2,1)} %bitcast.235, bf16[2048,768]{0,1:T(8,128)(2,1)} %get-tuple-element.64, bf16[2048,768]{0,1:T(8,128)(2,1)S(1)} %get-tuple-element.63), kind=kOutput, calls=%fused_computation.17 | convolution fusion | flops 12901679104 | bytes 20971520 | tf_op jit(solution)/shard_map/dot_general | solution.py:215
  669.1 88.3 %reduce-scatter.13.cloned.1.call-done = bf16[256,2048]{1,0:T(8,128)(2,1)} async-done(((bf16[2048,2048]{1,0:T(8,128)(2,1)}), bf16[256,2048]{1,0:T(8,128)(2,1)}) %reduce-scatter.13.cloned.1.call-update) | async-done | bytes 1048592 | tf_op jit(solution)/shard_map/reduce_scatter | solution.py:192
  757.4 3.7 fusion.27
  761.6 3.3 fusion.66
  765.0 11.9 convolution_convert_fusion.5
  776.9 18.7 %convolution_convert_fusion.4 = bf16[2048,1536]{1,0:T(8,128)(2,1)S(1)} fusion(bf16[2048,2048]{1,0:T(8,128)(2,1)} %all-gather.16.cloned.1.call-done, bf16[2048,768]{0,1:T(8,128)(2,1)} %get-tuple-element.64, bf16[2048,768]{0,1:T(8,128)(2,1)} %copy-done.55), kind=kOutput, calls=%fused_computation.20 | convolution fusion | flops 12900630528 | bytes 20971520 | tf_op jit(solution)/shard_map/dot_general | solution.py:219
  795.7 3.4 copy.190
  799.1 46.4 %all-gather.20.cloned.1.call-done = bf16[2048,2048]{1,0:T(8,128)(2,1)} async-done(((bf16[256,2048]{1,0:T(8,128)(2,1)}), bf16[2048,2048]{1,0:T(8,128)(2,1)}) %all-gather.20.cloned.1.call-update) | async-done | bytes 8388624 | tf_op jit(solution)/shard_map/all_gather | solution.py:225
  845.5 9.1 fusion.34
  858.4 8.7 fusion.50
  867.9 10.9 multiply_reduce_fusion
  878.8 12.7 multiply_convert_fusion
  894.5 4.5 broadcast_multiply_fusion.2
  912.2 5.0 multiply_reduce_fusion.5
  917.2 7.1 convolution_convert_fusion.7
  929.2 11.7 convolution_convert_fusion.6
  943.8 21.5 %reduce-scatter.21.cloned.1.call-done = bf16[512,1536]{1,0:T(8,128)(2,1)} async-done(((bf16[2048,1536]{1,0:T(8,128)(2,1)}), bf16[512,1536]{1,0:T(8,128)(2,1)}) %reduce-scatter.21.cloned.1.call-update) | async-done | bytes 1572880 | tf_op jit(solution)/shard_map/reduce_scatter | solution.py:69
  965.2 42.6 %all_to_all.42 = bf16[8,64,1536]{2,1,0:T(8,128)(2,1)S(1)} all-to-all(bf16[8,64,1536]{2,1,0:T(8,128)(2,1)} %bitcast.213), channel_id=1, replica_groups=mesh['rep'=4,'grp'=8] {'grp'}, dimensions={0} | all-to-all | bytes 3145728 | tf_op jit(solution)/shard_map/all_to_all | solution.py:71
  1010.5 33.1 %reduce-scatter.17.cloned.1.call-done = bf16[512,768]{1,0:T(8,128)(2,1)} async-done(((bf16[2048,768]{1,0:T(8,128)(2,1)}), bf16[512,768]{1,0:T(8,128)(2,1)}) %reduce-scatter.17.cloned.1.call-update) | async-done | bytes 786448 | tf_op jit(solution)/shard_map/reduce_scatter | solution.py:69
  1043.6 25.7 %all_to_all.43 = bf16[8,64,768]{2,1,0:T(8,128)(2,1)} all-to-all(bf16[8,64,768]{2,1,0:T(8,128)(2,1)} %bitcast.218), channel_id=1, replica_groups=mesh['rep'=4,'grp'=8] {'grp'}, dimensions={0} | all-to-all | bytes 1572864 | tf_op jit(solution)/shard_map/all_to_all | solution.py:71
  1069.3 11.9 convolution_convert_fusion
  1081.3 10.9 convolution_convert_fusion.2
  1092.3 5.4 convert_element_type.185
  1097.7 64.5 %all-gather.26.cloned.1.call-done = bf16[256,8,1536]{2,1,0:T(8,128)(2,1)} async-done(((bf16[64,8,1536]{2,1,0:T(8,128)(2,1)}), bf16[256,8,1536]{2,1,0:T(8,128)(2,1)}) %all-gather.26.cloned.1.call-update) | async-done | bytes 6291472 | tf_op jit(solution)/shard_map/all_gather | solution.py:72
  1162.2 9.1 copy.192
  1171.3 9.0 convert_bitcast_fusion
  1180.3 10.4 copy.193
  1190.7 19.4 %copy.195 = f32[256,2,6144]{2,1,0:T(2,128)} copy(f32[256,2,6144]{0,2,1:T(8,128)} %bitcast.178) | data formatting | bytes 25165824
  1212.9 23.7 %all-gather.22.cloned.1.call-done = bf16[256,8,768]{2,0,1:T(8,128)(2,1)} async-done(((bf16[64,8,768]{2,0,1:T(8,128)(2,1)}), bf16[256,8,768]{2,0,1:T(8,128)(2,1)}) %all-gather.22.cloned.1.call-update) | async-done | bytes 3145744 | tf_op jit(solution)/shard_map/all_gather | solution.py:72
  1244.3 4.4 fusion.68
  1248.7 3.0 copy.186
  1251.7 2.9 copy.187
  1254.6 4.9 pad_maximum_fusion.1
  1259.5 6.6 copy.194
  1266.1 62.3 %reduce-scatter.15.cloned.1.call-done = bf16[256,2048]{1,0:T(8,128)(2,1)} async-done(((bf16[2048,2048]{1,0:T(8,128)(2,1)}), bf16[256,2048]{1,0:T(8,128)(2,1)}) %reduce-scatter.15.cloned.1.call-update) | async-done | bytes 1048592 | tf_op jit(solution)/shard_map/reduce_scatter | solution.py:192
  1330.8 39.9 %psum.7 = f32[4352]{0:T(1024)S(1)} all-reduce(f32[4352]{0:T(1024)S(1)} %pad_maximum_fusion.8), channel_id=1, replica_groups=mesh['rep'=4,'grp'=8] {'rep','grp'}, use_global_device_ids=true, to_apply=%region_24.25 | all-reduce | flops 4352 | bytes 34816 | tf_op jit(solution)/shard_map/psum | solution.py:294
  1372.0 47.8 %reduce-scatter.11.cloned.1.call-done = bf16[256,2048]{1,0:T(8,128)(2,1)} async-done(((bf16[2048,2048]{1,0:T(8,128)(2,1)}), bf16[256,2048]{1,0:T(8,128)(2,1)}) %reduce-scatter.11.cloned.1.call-update) | async-done | bytes 1048592 | tf_op jit(solution)/shard_map/reduce_scatter | solution.py:192
  1419.8 5.8 fusion.23
  (233 shorter events, 106.3 us)
Async XLA Ops:
  7.2 625.6 %copy-start = (bf16[768,2048]{1,0:T(8,128)(2,1)S(1)}, bf16[768,2048]{1,0:T(8,128)(2,1)}, u32[]{:S(2)}) copy-start(bf16[768,2048]{1,0:T(8,128)(2,1)} %param.16) | copy-start | bytes 9437188
  7.2 91.4 %all-gather.30.cloned.1.call-start = ((), (), s32[]{:S(2)}) async-start(), calls=%async_computation.28 | async-start | bytes 3932160 | tf_op jit(solution)/shard_map/all_gather | solution.py:59
  24.3 32.1 %copy-start.54 = (u32[32]{0:T(128)S(1)}, u32[32]{0:T(128)}, u32[]{:S(2)}) copy-start(u32[32]{0:T(128)} %constant.71) | copy-start | bytes 388
  24.3 33.4 %copy-start.50 = (bf16[16]{0:T(256)(128)(2,1)S(1)}, bf16[16]{0:T(256)(128)(2,1)}, u32[]{:S(2)}) copy-start(bf16[16]{0:T(256)(128)(2,1)} %param.19) | copy-start | bytes 100
  24.3 33.4 %copy-start.51 = (bf16[16]{0:T(256)(128)(2,1)S(1)}, bf16[16]{0:T(256)(128)(2,1)}, u32[]{:S(2)}) copy-start(bf16[16]{0:T(256)(128)(2,1)} %param.18) | copy-start | bytes 100
  24.3 33.4 %copy-start.52 = (bf16[256]{0:T(256)(128)(2,1)S(1)}, bf16[256]{0:T(256)(128)(2,1)}, u32[]{:S(2)}) copy-start(bf16[256]{0:T(256)(128)(2,1)} %param.20) | copy-start | bytes 1540
  24.3 33.4 %copy-start.53 = (bf16[256]{0:T(256)(128)(2,1)S(1)}, bf16[256]{0:T(256)(128)(2,1)}, u32[]{:S(2)}) copy-start(bf16[256]{0:T(256)(128)(2,1)} %param.17) | copy-start | bytes 1540
  26.8 58.5 %copy-start.49 = (s32[2,16]{1,0:T(2,128)S(1)}, s32[2,16]{1,0:T(2,128)}, u32[]{:S(2)}) copy-start(s32[2,16]{1,0:T(2,128)} %param.12) | copy-start | bytes 388
  55.6 126.7 %all-gather.14.cloned.1.call-start = ((), (), s32[]{:S(2)}) async-start(), calls=%async_computation.12 | async-start | bytes 9437184 | tf_op jit(solution)/shard_map/all_gather | solution.py:125
  56.3 332.6 %reduce-scatter.9.cloned.1.call-start = ((), (), s32[]{:S(2)}) async-start(), calls=%async_computation.13 | async-start | bytes 9437184 | tf_op jit(solution)/shard_map/reduce_scatter | solution.py:192
  85.2 146.5 %copy-start.40 = (f32[128]{0:T(128)}, f32[128]{0:T(128)S(1)}, u32[]{:S(2)}) copy-start(f32[128]{0:T(128)S(1)} %mul.449) | copy-start | bytes 1540
  85.3 152.7 %copy-start.42 = (f32[128]{0:T(128)}, f32[128]{0:T(128)S(1)}, u32[]{:S(2)}) copy-start(f32[128]{0:T(128)S(1)} %mul.434) | copy-start | bytes 1540
  85.4 102.2 %copy-start.33 = (f32[1,2,8,128]{3,1,2,0:T(2,128)}, f32[1,2,8,128]{3,1,2,0:T(2,128)S(1)}, u32[]{:S(2)}) copy-start(f32[1,2,8,128]{3,1,2,0:T(2,128)S(1)} %copy.213) | copy-start | bytes 24580
  182.3 5.8 copy-start.13
  187.5 9.6 copy-start.46
  197.2 2.9 copy-start.18
  208.7 3.2 copy-start.22
  208.7 4.0 copy-start.19
  212.8 19.0 %copy-start.29 = (f32[2,1024]{1,0:T(2,128)}, f32[2,1024]{1,0:T(2,128)S(1)}, u32[]{:S(2)}) copy-start(f32[2,1024]{1,0:T(2,128)S(1)} %rsqrt_bitcast_fusion) | copy-start | bytes 24580
  224.0 14.1 copy-start.27
  231.8 6.3 copy-start.1
  251.3 10.5 copy-start.38
  265.1 4.4 copy-start.25
  275.3 191.3 %all-gather.32.cloned.1.call-start = ((), (), s32[]{:S(2)}) async-start(), calls=%async_computation.29 | async-start | bytes 7864320 | tf_op jit(solution)/shard_map/all_gather | solution.py:59
  365.2 185.6 %all-gather.16.cloned.1.call-start = ((), (), s32[]{:S(2)}) async-start(), calls=%async_computation.14 | async-start | bytes 9437184 | tf_op jit(solution)/shard_map/all_gather | solution.py:200
  365.2 395.9 %copy-start.31 = (f32[1,2,8,128]{3,1,2,0:T(2,128)}, f32[1,2,8,128]{3,1,2,0:T(2,128)S(1)}, u32[]{:S(2)}) copy-start(f32[1,2,8,128]{3,1,2,0:T(2,128)S(1)} %copy.215) | copy-start | bytes 24580
  390.8 370.2 %copy-start.36 = (f32[256]{0:T(256)}, f32[256]{0:T(256)S(1)}, u32[]{:S(2)}) copy-start(f32[256]{0:T(256)S(1)} %add_rsqrt_fusion.3) | copy-start | bytes 3076
  393.8 239.0 %all-gather.18.cloned.1.call-start = ((), (), s32[]{:S(2)}) async-start(), calls=%async_computation.16 | async-start | bytes 9437184 | tf_op jit(solution)/shard_map/all_gather | solution.py:135
  394.4 363.0 %reduce-scatter.13.cloned.1.call-start = ((), (), s32[]{:S(2)}) async-start(), calls=%async_computation.17 | async-start | bytes 9437184 | tf_op jit(solution)/shard_map/reduce_scatter | solution.py:192
  669.1 176.4 %all-gather.20.cloned.1.call-start = ((), (), s32[]{:S(2)}) async-start(), calls=%async_computation.18 | async-start | bytes 9437184 | tf_op jit(solution)/shard_map/all_gather | solution.py:225
  757.4 4.2 copy-start.3
  757.4 4.2 copy-start.4
  757.4 4.2 copy-start.10
  764.9 178.1 %reduce-scatter.23.cloned.1.call-start = ((), (), s32[]{:S(2)}) async-start(), calls=%async_computation.26 | async-start | bytes 3932160 | tf_op jit(solution)/shard_map/reduce_scatter | solution.py:76
  776.9 188.4 %reduce-scatter.21.cloned.1.call-start = ((), (), s32[]{:S(2)}) async-start(), calls=%async_computation.24 | async-start | bytes 7864320 | tf_op jit(solution)/shard_map/reduce_scatter | solution.py:69
  799.1 210.9 %reduce-scatter.19.cloned.1.call-start = ((), (), s32[]{:S(2)}) async-start(), calls=%async_computation.22 | async-start | bytes 1310720 | tf_op jit(solution)/shard_map/reduce_scatter | solution.py:76
  854.6 3.8 copy-start.39
  858.3 9.5 copy-start.26
  878.8 12.8 copy-start.20
  891.5 2.9 copy-start.16
  894.5 5.9 copy-start.11
  894.5 4.5 copy-start.21
  900.4 2.0 copy-start.2
  900.4 2.0 copy-start.28
  905.4 6.7 copy-start.30
  905.4 6.7 copy-start.41
  908.2 3.9 copy-start.6
  908.2 3.9 copy-start.12
  908.2 3.9 copy-start.17
  910.7 6.4 copy-start.8
  924.3 4.9 copy-start.34
  924.3 4.9 copy-start.47
  924.3 119.3 %reduce-scatter.17.cloned.1.call-start = ((), (), s32[]{:S(2)}) async-start(), calls=%async_computation.20 | async-start | bytes 3932160 | tf_op jit(solution)/shard_map/reduce_scatter | solution.py:69
  943.0 149.3 %all-gather.28.cloned.1.call-start = ((), (), s32[]{:S(2)}) async-start(), calls=%async_computation.27 | async-start | bytes 3932160 | tf_op jit(solution)/shard_map/all_gather | solution.py:77
  943.7 218.5 %all-gather.26.cloned.1.call-start = ((), (), s32[]{:S(2)}) async-start(), calls=%async_computation.25 | async-start | bytes 7864320 | tf_op jit(solution)/shard_map/all_gather | solution.py:72
  1009.9 200.2 %all-gather.24.cloned.1.call-start = ((), (), s32[]{:S(2)}) async-start(), calls=%async_computation.23 | async-start | bytes 1310720 | tf_op jit(solution)/shard_map/all_gather | solution.py:77
  1010.5 226.1 %all-gather.22.cloned.1.call-start = ((), (), s32[]{:S(2)}) async-start(), calls=%async_computation.21 | async-start | bytes 3932160 | tf_op jit(solution)/shard_map/all_gather | solution.py:72
  1069.3 259.1 %reduce-scatter.15.cloned.1.call-start = ((), (), s32[]{:S(2)}) async-start(), calls=%async_computation.19 | async-start | bytes 9437184 | tf_op jit(solution)/shard_map/reduce_scatter | solution.py:192
  1081.2 338.5 %reduce-scatter.11.cloned.1.call-start = ((), (), s32[]{:S(2)}) async-start(), calls=%async_computation.15 | async-start | bytes 9437184 | tf_op jit(solution)/shard_map/reduce_scatter | solution.py:192
  1092.2 5.5 copy-start.48
  1259.5 71.3 %copy-start.35 = (f32[2048]{0:T(1024)S(1)}, f32[2048]{0:T(1024)}, u32[]{:S(2)}) copy-start(f32[2048]{0:T(1024)} %get-tuple-element.52) | copy-start | bytes 24580
  1259.5 160.3 %copy-start.32 = (f32[1,2,8,128]{3,1,2,0:T(2,128)S(1)}, f32[1,2,8,128]{3,1,2,0:T(2,128)}, u32[]{:S(2)}) copy-start(f32[1,2,8,128]{3,1,2,0:T(2,128)} %copy-done.31) | copy-start | bytes 24580
  1259.5 160.3 %copy-start.37 = (f32[256]{0:T(256)S(1)}, f32[256]{0:T(256)}, u32[]{:S(2)}) copy-start(f32[256]{0:T(256)} %copy-done.36) | copy-start | bytes 3076
  1259.5 160.3 %copy-start.45 = (f32[256]{0:T(256)S(1)}, f32[256]{0:T(256)}, u32[]{:S(2)}) copy-start(f32[256]{0:T(256)} %copy-done.44) | copy-start | bytes 3076
  (10 other events, 13.2 us)
Sparse Core Ops, SparseCore 0:
  55.7 42.8 all-gather.29
  100.2 82.0 all-gather.13
  275.4 113.4 reduce-scatter.8
  390.6 75.9 all-gather.31
  468.6 82.0 all-gather.15
  552.2 80.5 all-gather.17
  669.2 88.1 reduce-scatter.12
  765.0 80.3 all-gather.19
  849.0 42.5 reduce-scatter.22
  895.0 70.1 reduce-scatter.20
  968.1 27.7 reduce-scatter.18
  999.6 43.9 reduce-scatter.16
  1045.6 43.9 all-gather.27
  1092.0 70.1 all-gather.25
  1164.0 26.6 all-gather.23
  1192.5 43.9 all-gather.21
  1238.8 89.5 reduce-scatter.14
  1330.7 89.0 reduce-scatter.10

commit v2 on v1

--- a/solution.py
+++ b/solution.py
@@ -1,6 +1,10 @@
+import functools
+
 import jax
 import jax.numpy as jnp
 from jax import lax
+from jax.experimental import pallas as pl
+from jax.experimental.pallas import tpu as pltpu
 from jax.sharding import PartitionSpec as P
 
 QUERY_HEADS = 16
@@ -33,13 +37,415 @@
 
 
 def unrotate_pairs(gradient, cosine_lookup, sine_lookup):
-    return gradient * cosine_lookup - rotate_half(gradient * sine_lookup)
+    return gradient * cosine_lookup - jnp.roll(gradient, HEAD_SIZE // 2, -1) * sine_lookup
 
 
 def norm_back(grad_out, normed, scale_rows, gain_vector):
     weighted = grad_out * gain_vector
     grad_in = scale_rows * (weighted - normed * jnp.mean(weighted * normed, axis=-1, keepdims=True))
     return (grad_in, grad_out * normed)
+
+
+MESH = pl.DeviceIdType.MESH
+F32 = jnp.float32
+BF16 = jnp.bfloat16
+
+
+def nearest(place, step, chips):
+    low = jnp.minimum(place, chips - 1 - place)
+    near = (step + 1) // 2
+    both = jnp.where(step % 2 == 1, place - near, place + near)
+    past = step - low
+    rest = jnp.where(place > chips - 1 - place, place - past, place + past)
+    return jnp.where(step <= 2 * low, both, rest)
+
+
+def meet(owners, reps):
+    barrier = pltpu.get_barrier_semaphore()
+    me, rep = lax.axis_index("grp"), lax.axis_index("rep")
+    for ahead in range(1, owners):
+        pl.semaphore_signal(
+            barrier, 1, device_id={"grp": lax.rem(me + ahead, owners)}, device_id_type=MESH
+        )
+    for ahead in range(1, reps):
+        pl.semaphore_signal(
+            barrier, 1, device_id={"rep": lax.rem(rep + ahead, reps)}, device_id_type=MESH
+        )
+    pl.semaphore_wait(barrier, owners + reps - 2)
+
+
+def to_grp(source, target, send, recv, device):
+    return pltpu.make_async_remote_copy(
+        src_ref=source,
+        dst_ref=target,
+        send_sem=send,
+        recv_sem=recv,
+        device_id={"grp": device},
+        device_id_type=MESH,
+    )
+
+
+def to_rep(source, target, send, recv, device):
+    return pltpu.make_async_remote_copy(
+        src_ref=source,
+        dst_ref=target,
+        send_sem=send,
+        recv_sem=recv,
+        device_id={"rep": device},
+        device_id_type=MESH,
+    )
+
+
+def arrived(ref, sem):
+    pltpu.make_async_copy(ref, ref, sem).wait()
+
+
+def dot(a, b):
+    return jnp.dot(a, b, preferred_element_type=F32)
+
+
+def dot_nt(a, b):
+    return lax.dot_general(a, b, (((1,), (1,)), ((), ())), preferred_element_type=F32)
+
+
+def dot_tn(a, b):
+    return lax.dot_general(a, b, (((0,), (0,)), ((), ())), preferred_element_type=F32)
+
+
+class Gather:
+    def __init__(self, owners, buf, send, recv):
+        self.owners, self.chips = owners, owners // 2
+        self.me = lax.axis_index("grp")
+        self.place, self.core = self.me // 2, self.me % 2
+        self.buf, self.send, self.recv = buf, send, recv
+
+    def copies(self, block, source=None):
+        src = self.buf.at[block] if source is None else source
+        at = block // 2
+        ways = (
+            ((at <= self.place) & (self.place < self.chips - 1), self.me + 2),
+            ((at >= self.place) & (self.place > 0), self.me - 2),
+            (None, self.me + 1 - 2 * self.core),
+        )
+        return [
+            (
+                when,
+                to_grp(src, self.buf.at[block], self.send.at[way, at], self.recv.at[block], device),
+            )
+            for way, (when, device) in enumerate(ways)
+        ]
+
+    def forward(self, block, source=None):
+        for when, copy in self.copies(block, source):
+            if when is None:
+                copy.start()
+            else:
+                pl.when(when)(copy.start)
+
+    def step(self, k):
+        block = 2 * nearest(self.place, k, self.chips) + self.core
+        arrived(self.buf.at[block], self.recv.at[block])
+        self.forward(block)
+
+    def sibling(self, k):
+        block = 2 * nearest(self.place, k, self.chips) + 1 - self.core
+        arrived(self.buf.at[block], self.recv.at[block])
+
+    def finish(self):
+        def one(at, _):
+            for when, copy in self.copies(2 * at + self.core):
+                if when is None:
+                    copy.wait_send()
+                else:
+                    pl.when(when)(copy.wait_send)
+            return 0
+
+        lax.fori_loop(0, self.chips, one, 0)
+
+    @staticmethod
+    def scratch(owners):
+        return [
+            pltpu.SemaphoreType.DMA((3, owners // 2)),
+            pltpu.SemaphoreType.DMA((owners,)),
+        ]
+
+
+class Reshard:
+    def __init__(self, owners, reps, buf, sems):
+        self.owners, self.reps = owners, reps
+        self.me, self.rep = lax.axis_index("grp"), lax.axis_index("rep")
+        self.buf = buf
+        self.send1, self.recv1, self.send2, self.recv2 = sems
+
+    def start(self, pieces):
+        for source, columns in pieces(self.me):
+            pltpu.make_async_copy(
+                source, self.buf.at[self.me, self.rep, :, columns], self.recv1.at[self.me]
+            ).start()
+
+        def one(ahead, _):
+            device = lax.rem(self.me + ahead, self.owners)
+            for source, columns in pieces(device):
+                to_grp(
+                    source,
+                    self.buf.at[self.me, self.rep, :, columns],
+                    self.send1.at[device],
+                    self.recv1.at[self.me],
+                    device,
+                ).start()
+            return 0
+
+        lax.fori_loop(1, self.owners, one, 0)
+
+    def relay(self):
+        def one(ahead, _):
+            owner = lax.rem(self.me + ahead, self.owners)
+            part = self.buf.at[owner, self.rep]
+            arrived(part, self.recv1.at[owner])
+            for other in range(1, self.reps):
+                to_rep(
+                    part,
+                    part,
+                    self.send2.at[other],
+                    self.recv2.at[other],
+                    lax.rem(self.rep + other, self.reps),
+                ).start()
+            return 0
+
+        lax.fori_loop(0, self.owners, one, 0)
+
+    def wait(self):
+        for other in range(1, self.reps):
+            source = lax.rem(self.rep + self.reps - other, self.reps)
+            arrived(self.buf.at[:, source], self.recv2.at[other])
+
+    def finish(self):
+        def one(ahead, _):
+            device = lax.rem(self.me + ahead, self.owners)
+            arrived(self.buf.at[device, self.rep], self.send1.at[device])
+            return 0
+
+        lax.fori_loop(1, self.owners, one, 0)
+        for other in range(1, self.reps):
+            arrived(self.buf.at[:, self.rep], self.send2.at[other])
+
+    @staticmethod
+    def scratch(owners, reps):
+        return [
+            pltpu.SemaphoreType.DMA((owners,)),
+            pltpu.SemaphoreType.DMA((owners,)),
+            pltpu.SemaphoreType.DMA((reps,)),
+            pltpu.SemaphoreType.DMA((reps,)),
+        ]
+
+
+def head_norm(values):
+    scale = lax.rsqrt(jnp.mean(values * values, axis=-1, keepdims=True) + norm_epsilon)
+    return values * scale, scale
+
+
+def turn(values, cosine, sine):
+    return values * cosine + pltpu.roll(values, HEAD_SIZE // 2, 1) * sine
+
+
+def turn_back(values, cosine, sine):
+    return values * cosine - pltpu.roll(values, HEAD_SIZE // 2, 1) * sine
+
+
+def first_kernel(
+    owners,
+    reps,
+    heads,
+    kv_heads,
+    sharers,
+    tokens_ref,
+    weight_ref,
+    small_ref,
+    cosine_ref,
+    sine_ref,
+    input_out,
+    query_out,
+    gate_out,
+    key_out,
+    value_out,
+    query_rot_out,
+    key_rot_out,
+    columns_out,
+    small_out,
+    buf,
+    weight_buf,
+    small_send,
+    small_recv,
+    local_sem,
+    out_sem,
+    g_send,
+    g_recv,
+    *r_sems,
+):
+    me, rep = lax.axis_index("grp"), lax.axis_index("rep")
+    rows, width = tokens_ref.shape
+    shard = weight_ref.shape[0]
+    share = shard // reps
+    q_cols, kv_cols = heads * HEAD_SIZE, kv_heads * HEAD_SIZE
+    all_q = QUERY_HEADS * HEAD_SIZE
+    all_kv = KEY_VALUE_HEADS * HEAD_SIZE
+    gather = Gather(owners, buf, g_send, g_recv)
+    reshard = Reshard(owners, reps, weight_buf, r_sems)
+    my_rows = pl.ds(pl.multiple_of(rep * share, share), share)
+
+    def pieces(owner):
+        out = []
+        at = 0
+        for base, cols, step in (
+            (0, q_cols, owner),
+            (all_q, q_cols, owner),
+            (2 * all_q, kv_cols, owner // sharers),
+            (2 * all_q + all_kv, kv_cols, owner // sharers),
+        ):
+            first = pl.multiple_of(base + step * cols, HEAD_SIZE)
+            out.append((weight_ref.at[my_rows, pl.ds(first, cols)], pl.ds(at, cols)))
+            at += cols
+        return out
+
+    own = pltpu.make_async_copy(tokens_ref, buf.at[me], local_sem)
+    own.start()
+    small_out[me] = small_ref[...]
+    meet(owners, reps)
+    reshard.start(pieces)
+
+    def small_copy(device, index):
+        return to_grp(
+            small_ref, small_out.at[me], small_send.at[index], small_recv.at[index], device
+        )
+
+    for ahead in range(1, owners):
+        small_copy(lax.rem(me + ahead, owners), ahead).start()
+    gather.forward(me, tokens_ref)
+    reshard.relay()
+    for ahead in range(1, owners):
+        source = lax.rem(me + owners - ahead, owners)
+        arrived(small_out.at[source], small_recv.at[ahead])
+    own.wait()
+    middle = (gather.place > 0) & (gather.place < gather.chips - 1)
+    early = jnp.where(middle, gather.chips, gather.chips - 1)
+
+    def step(k, _):
+        gather.step(k)
+        return 0
+
+    lax.fori_loop(1, early, step, 0)
+    reshard.wait()
+    columns_copy = pltpu.make_async_copy(weight_buf, columns_out, out_sem)
+    columns_copy.start()
+
+    gain = jnp.concatenate([small_out[e][:, :shard] for e in range(owners)], axis=1)
+    heads_gain = small_out[0][:, 2 * shard :]
+    for e in range(1, owners):
+        heads_gain = heads_gain + small_out[e][:, 2 * shard :]
+    gain_query = heads_gain[:, :HEAD_SIZE]
+    gain_key = heads_gain[:, HEAD_SIZE:]
+    total_cols = 2 * q_cols + 2 * kv_cols
+    weight = weight_buf.reshape(width, total_cols)
+
+    def block(k, _):
+        @pl.when(k >= early)
+        def _():
+            gather.step(k)
+
+        def core(which, _):
+            mine = which == 0
+
+            @pl.when(which == 1)
+            def _():
+                gather.sibling(k)
+
+            at = 2 * nearest(gather.place, k, gather.chips) + jnp.where(
+                mine, gather.core, 1 - gather.core
+            )
+            values = buf[at].astype(F32)
+            normed, _unused = head_norm(values)
+            entry = (normed * gain).astype(BF16)
+            input_out[at] = entry
+            projected = dot(entry, weight[...])
+            cosine, sine = cosine_ref[at], sine_ref[at]
+            for h in range(heads):
+                span = slice(h * HEAD_SIZE, (h + 1) * HEAD_SIZE)
+                raw = projected[:, span]
+                query_out[at, :, span] = raw
+                query_rot_out[at, :, span] = turn(
+                    head_norm(raw)[0] * gain_query, cosine, sine
+                ).astype(BF16)
+            gate_out[at] = projected[:, q_cols : 2 * q_cols]
+            for h in range(kv_heads):
+                span = slice(h * HEAD_SIZE, (h + 1) * HEAD_SIZE)
+                raw = projected[:, 2 * q_cols + h * HEAD_SIZE : 2 * q_cols + (h + 1) * HEAD_SIZE]
+                key_out[at, :, span] = raw
+                key_rot_out[at, :, span] = turn(
+                    head_norm(raw)[0] * gain_key, cosine, sine
+                ).astype(BF16)
+            value_out[at] = projected[:, 2 * q_cols + kv_cols :].astype(BF16)
+            return 0
+
+        lax.fori_loop(0, 2, core, 0)
+        return 0
+
+    lax.fori_loop(0, gather.chips, block, 0)
+    columns_copy.wait()
+    gather.finish()
+    reshard.finish()
+    for ahead in range(1, owners):
+        small_copy(lax.rem(me + ahead, owners), ahead).wait_send()
+
+
+def vmem():
+    return pl.BlockSpec(memory_space=pltpu.VMEM)
+
+
+def anywhere():
+    return pl.BlockSpec(memory_space=pl.ANY)
+
+
+def first(owners, reps, heads, kv_heads, sharers, tokens, w_qkvg, small, cosine, sine):
+    rows, width = tokens.shape
+    shard = w_qkvg.shape[0]
+    q_cols, kv_cols = heads * HEAD_SIZE, kv_heads * HEAD_SIZE
+    cols = 2 * q_cols + 2 * kv_cols
+    shape = jax.ShapeDtypeStruct
+    outs = (
+        shape((owners, rows, width), BF16),
+        shape((owners, rows, q_cols), F32),
+        shape((owners, rows, q_cols), F32),
+        shape((owners, rows, kv_cols), F32),
+        shape((owners, rows, kv_cols), BF16),
+        shape((owners, rows, q_cols), BF16),
+        shape((owners, rows, kv_cols), BF16),
+        shape((owners, reps, shard // reps, cols), BF16),
+        shape((owners,) + small.shape, F32),
+    )
+    flops = 2 * owners * rows * width * cols
+    return pl.pallas_call(
+        functools.partial(first_kernel, owners, reps, heads, kv_heads, sharers),
+        out_shape=outs,
+        in_specs=[anywhere(), anywhere(), vmem(), vmem(), vmem()],
+        out_specs=(vmem(),) * 7 + (anywhere(), vmem()),
+        scratch_shapes=[
+            pltpu.VMEM((owners, rows, width), BF16),
+            pltpu.VMEM((owners, reps, shard // reps, cols), BF16),
+            pltpu.SemaphoreType.DMA((owners,)),
+            pltpu.SemaphoreType.DMA((owners,)),
+            pltpu.SemaphoreType.DMA,
+            pltpu.SemaphoreType.DMA,
+        ]
+        + Gather.scratch(owners)
+        + Reshard.scratch(owners, reps),
+        compiler_params=pltpu.CompilerParams(
+            collective_id=0, has_side_effects=True, vmem_limit_bytes=60 * 2**20
+        ),
+        cost_estimate=pl.CostEstimate(
+            flops=flops, bytes_accessed=40 * 2**20, transcendentals=0
+        ),
+        name="first",
+    )(tokens, w_qkvg, small, cosine, sine)
 
 
 def positions_of(block_ids):
@@ -106,38 +512,62 @@
     all_kv = KEY_VALUE_HEADS * HEAD_SIZE
     hidden_units = w_down.shape[0]
 
-    def by_owner(part, repeat):
-        split = part.reshape(shard, owners // repeat, -1)
-        return jnp.repeat(split, repeat, axis=1) if repeat > 1 else split
-
-    qkvg_pieces = jnp.concatenate(
-        [
-            by_owner(w_qkvg[:, :all_q], 1),
-            by_owner(w_qkvg[:, all_q : 2 * all_q], 1),
-            by_owner(w_qkvg[:, 2 * all_q : 2 * all_q + all_kv], sharers),
-            by_owner(w_qkvg[:, 2 * all_q + all_kv :], sharers),
-        ],
-        axis=2,
-    )
     in_pieces = jnp.swapaxes(w_in.reshape(shard, 2, owners, hidden_units), 1, 2).reshape(
         shard, owners, 2 * hidden_units
     )
-    tokens_all = lax.all_gather(tokens, "grp", axis=0, tiled=True)
-    qkvg_cols = to_columns(qkvg_pieces)
-    small = jnp.concatenate([norm_attn, norm_mlp, norm_query, norm_key])
-    small_all = lax.all_gather(small, "grp", axis=0, tiled=False).astype(jnp.float32)
+    reps = lax.axis_size("rep")
     head_part = norm_query.shape[0]
+    spread = jnp.zeros((2, HEAD_SIZE), jnp.float32)
+    spread = lax.dynamic_update_slice(
+        spread, jnp.stack([norm_query, norm_key]).astype(jnp.float32), (0, me * head_part)
+    )
+    small = jnp.concatenate(
+        [norm_attn.astype(jnp.float32), norm_mlp.astype(jnp.float32), spread.reshape(-1)]
+    )[None]
+    in_cols = to_columns(in_pieces)
+    cotangent_all = lax.all_gather(cotangent, "grp", axis=0, tiled=True)
+
+    positions = positions_of(block_map)
+    cosine, sine = rotary_tables(positions)
+    sine = sine * jnp.where(jnp.arange(HEAD_SIZE) < HEAD_SIZE // 2, -1.0, 1.0)
+
+    def by_block(table):
+        shaped = table.reshape(GROUP_SEQUENCES, owners, block_rows, HEAD_SIZE)
+        return jnp.swapaxes(shaped, 0, 1).reshape(owners, rows_here, HEAD_SIZE)
+
+    (
+        attn_input,
+        query_raw,
+        gate_raw,
+        key_raw,
+        value_rows,
+        query_rot,
+        key_rot,
+        qkvg_cols,
+        small_all,
+    ) = first(
+        owners,
+        reps,
+        heads,
+        kv_heads,
+        sharers,
+        tokens,
+        w_qkvg,
+        small,
+        by_block(cosine),
+        by_block(sine),
+    )
+    cosine = cosine[:, None]
+    sine = sine[:, None]
+    small_all = small_all[:, 0]
     gain_attn = small_all[:, :shard].reshape(-1)
     gain_mlp = small_all[:, shard : 2 * shard].reshape(-1)
-    gain_query = small_all[:, 2 * shard : 2 * shard + head_part].reshape(-1)
-    gain_key = small_all[:, 2 * shard + head_part :].reshape(-1)
-    in_cols = to_columns(in_pieces)
-    cotangent_all = lax.all_gather(cotangent, "grp", axis=0, tiled=True)
-
-    positions = positions_of(block_map)
-    cosine, sine = rotary_tables(positions)
-    cosine = cosine[:, None]
-    sine = sine[:, None]
+    spread = jnp.sum(small_all[:, 2 * shard :], axis=0)
+    gain_query = spread[:HEAD_SIZE]
+    gain_key = spread[HEAD_SIZE:]
+    attn_input = attn_input.reshape(-1, width)
+    gate_raw = gate_raw.reshape(-1, q_cols)
+    qkvg_cols = qkvg_cols.reshape(width, -1)
 
     def to_heads(values):
         count = values.shape[-1] // HEAD_SIZE
@@ -151,26 +581,18 @@
         shaped = values.reshape(GROUP_SEQUENCES, count, owners, block_rows, HEAD_SIZE)
         return shaped.transpose(2, 0, 3, 1, 4).reshape(-1, count * HEAD_SIZE)
 
-    wide_tokens = tokens_all.astype(jnp.float32)
-    normed_first = wide_tokens * row_scale(wide_tokens)
-    attn_input = (normed_first * gain_attn).astype(jnp.bfloat16)
-    projected = jnp.dot(attn_input, qkvg_cols, preferred_element_type=jnp.float32)
-    query_heads = to_heads(projected[:, :q_cols])
-    gate_raw = projected[:, q_cols : 2 * q_cols]
-    key_heads = to_heads(projected[:, 2 * q_cols : 2 * q_cols + kv_cols])
-    value_heads = to_heads(projected[:, 2 * q_cols + kv_cols :]).astype(jnp.bfloat16)
+    query_heads = to_heads(query_raw)
+    key_heads = to_heads(key_raw)
+    value_heads = to_heads(value_rows)
     query_scale = row_scale(query_heads)
     query_normed = query_heads * query_scale
     key_scale = row_scale(key_heads)
     key_normed = key_heads * key_scale
 
-    def rotate(values):
-        return (values * cosine + rotate_half(values) * sine).astype(jnp.bfloat16)
-
-    query_rot = rotate(query_normed * gain_query).reshape(
+    query_rot = to_heads(query_rot).reshape(
         GROUP_SEQUENCES, kv_heads, per_kv, seq_len, HEAD_SIZE
     )
-    key_rot = rotate(key_normed * gain_key)
+    key_rot = to_heads(key_rot)
     scores = jnp.einsum(
         "shgqd,shkd->shgqk", query_rot, key_rot, preferred_element_type=jnp.float32
     ) * HEAD_SIZE ** (-0.5)

time: 1440 us -> 1190 us (0.83)
  waiting for transfers between devices: 722 us -> 403 us
  Pallas kernels: 0 us -> 104 us
  blocking collectives: 229 us -> 173 us
    reduce_scatter x4, waiting for transfers between devices: 222 us -> 113 us  [scatter_sum(): lax.psum_scatter(terms.astype(jnp.bfloat16), 'grp', scatter_dimension=0,...]
    pallas_call x0 -> x1, Pallas kernels: none -> 104 us  [first(): pl.pallas_call(functools.partial(first_kernel, owners, reps, heads, kv_he...]
    all_gather x1 -> x0, waiting for transfers between devices: 79.5 us -> none  [body(): tokens_all = lax.all_gather(tokens, 'grp', axis=0, tiled=True)]
    reduce_scatter x2, waiting for transfers between devices: 54.5 us -> 0.04 us  [to_rows(): share = lax.psum_scatter(shaped, 'rep', scatter_dimension=0, tiled=True)]
    all_gather x2 -> x1, waiting for transfers between devices: 82.1 us -> 38.5 us  [to_columns(): whole = lax.all_gather(swapped, 'rep', axis=1, tiled=True)]
    unnamed x1 -> x0, blocking collectives: 27 us -> none
    all_to_all x2 -> x1, blocking collectives: 94 us -> 67.1 us  [to_columns(): swapped = lax.all_to_all(mine, 'grp', 1, 0, tiled=True)]
    all_gather x1, waiting for transfers between devices: 46.4 us -> 19.8 us  [body(): lax.all_gather(grad_hidden.astype(jnp.bfloat16), 'grp', axis=0, tiled=True)]
  transfers between devices with their start and end apart: 18 -> 16, of which waited for: 14 -> 8; matrix products, arithmetic and copies ran while one was open for 21% -> 30% of each run, Pallas kernels for 0% -> 0%
where the time goes in v2:
time: 1190 us; the launch traced here: 1170 us
  waiting for transfers between devices  403 us (34%)
  matrix products  196 us (16%)
  local copies, waits for them, and re-layouts  182 us (15%)
  blocking collectives  173 us (15%)
  Pallas kernels  104 us (9%)
  other arithmetic  98.8 us (8%)
  between operations  16.3 us (1%)
    reduce_scatter x4, waiting for transfers between devices, scatter_sum(): lax.psum_scatter(terms.astype(jnp.bfloat16), 'grp', scatter_dimension=0,...  113 us
    pallas_call x1, Pallas kernels, first(): pl.pallas_call(functools.partial(first_kernel, owners, reps, heads, kv_he...  104 us
    all_gather x2, waiting for transfers between devices, to_rows(): lax.all_gather(jnp.swapaxes(swapped, 0, 1), 'rep', axis=0, tiled=True)  84.4 us
    all_gather x1, waiting for transfers between devices, body(): lax.all_gather((normed_second * gain_mlp).astype(jnp.bfloat16), 'grp', ax...  84 us
    all_to_all x1, blocking collectives, to_columns(): swapped = lax.all_to_all(mine, 'grp', 1, 0, tiled=True)  67.1 us
    all_to_all x2, blocking collectives, to_rows(): swapped = lax.all_to_all(share, 'grp', 0, 0, tiled=True)  66.5 us
    all_gather x1, waiting for transfers between devices, body(): cotangent_all = lax.all_gather(cotangent, 'grp', axis=0, tiled=True)  62.4 us
    unnamed x76, local copies, waits for them, and re-layouts  41.3 us
  transfers between devices with their start and end apart: 16, of which 8 were waited for; matrix products, arithmetic and copies ran while one was open for 30% of the time, Pallas kernels for 0%

profile of v2, /device:TPU:0, one launch (start us, length us, event | category | flops | bytes accessed | tf_op | source)
XLA Modules:
  0.0 1174.9 jit_solution(4548593731080692038)
XLA Ops:
  15.3 5.0 broadcast_multiply_fusion.1
  20.3 104.3 %first.1 = (bf16[8,256,2048]{2,1,0:T(8,128)(2,1)}, f32[8,256,256]{2,1,0:T(8,128)}, f32[8,256,256]{2,1,0:T(8,128)}, f32[8,256,128]{2,1,0:T(8,128)}, bf16[8,256,12...) custom-call(bf16[256,2048]{1,0:T(8,128)(2,1)} %tokens_ref.1, ...), custom_call_target="tpu_custom_call" | custom-call | flops 6442450944 | bytes 41943040 | tf_op jit(solution)/shard_map/first/pallas_call | solution.py:426
  137.8 3.5 add_divide_fusion.1
  141.3 3.0 copy.191
  144.2 11.2 fusion.70
  155.5 10.5 fusion.7
  166.0 4.1 copy.190
  170.1 3.9 reshape.451
  177.5 5.8 convolution_convert_fusion.3
  183.4 6.9 copy.246
  190.3 14.4 %reshape.453 = bf16[256,8,1536]{2,0,1:T(8,128)(2,1)} reshape(bf16[256,8,2,768]{3,2,0,1:T(2,128)(2,1)} %bitcast.213) | data formatting | bytes 12582912 | tf_op jit(solution)/shard_map/reshape | solution.py:515
  206.3 67.1 %all_to_all.25 = bf16[64,8,1536]{2,0,1:T(8,128)(2,1)} all-to-all(bf16[64,8,1536]{2,0,1:T(8,128)(2,1)S(1)} %constant_dynamic-slice_fusion), channel_id=1, replica_groups=mesh['rep'=4,'grp'=8] {'grp'}, dimensions={1} | all-to-all | bytes 3145728 | tf_op jit(solution)/shard_map/all_to_all | solution.py:463
  274.1 24.4 %reduce-scatter.9.cloned.1.call-done = bf16[256,2048]{1,0:T(8,128)(2,1)} async-done(((bf16[2048,2048]{1,0:T(8,128)(2,1)}), bf16[256,2048]{1,0:T(8,128)(2,1)}) %reduce-scatter.9.cloned.1.call-update) | async-done | bytes 1048592 | tf_op jit(solution)/shard_map/reduce_scatter | solution.py:614
  300.5 2.9 multiply_convert_fusion.7
  304.0 38.5 %all-gather.24.cloned.1.call-done = bf16[8,256,1,1536]{3,1,0,2:T(8,128)(2,1)} async-done(((bf16[8,64,1,1536]{3,1,0,2:T(8,128)(2,1)}), bf16[8,256,1,1536]{3,1,0,2:T(8,128)(2,1)}) %all-gather.24.cloned.1.call-update) | async-done | bytes 6291472 | tf_op jit(solution)/shard_map/all_gather | solution.py:465
  342.5 84.0 %all-gather.10.cloned.1.call-done = bf16[2048,2048]{1,0:T(8,128)(2,1)} async-done(((bf16[256,2048]{1,0:T(8,128)(2,1)}), bf16[2048,2048]{1,0:T(8,128)(2,1)}) %all-gather.10.cloned.1.call-update) | async-done | bytes 8388624 | tf_op jit(solution)/shard_map/all_gather | solution.py:622
  426.5 19.5 %fusion.75 = f32[2048,1536]{0,1:T(8,128)} fusion(bf16[2048,2048]{1,0:T(8,128)(2,1)} %all-gather.10.cloned.1.call-done, bf16[2048,1536]{1,0:T(8,128)(2,1)} %bitcast.266), kind=kOutput, calls=%fused_computation.141 | convolution fusion | flops 12884901888 | bytes 27262976 | tf_op jit(solution)/shard_map/dot_general | solution.py:625
  446.0 62.4 %all-gather.12.cloned.1.call-done = bf16[2048,2048]{1,0:T(8,128)(2,1)} async-done(((bf16[256,2048]{1,0:T(8,128)(2,1)}), bf16[2048,2048]{1,0:T(8,128)(2,1)}) %all-gather.12.cloned.1.call-update) | async-done | bytes 8388624 | tf_op jit(solution)/shard_map/all_gather | solution.py:528
  508.4 15.8 %multiply_convert_fusion.2 = (bf16[2048,768]{0,1:T(8,128)(2,1)S(1)}, bf16[2048,768]{0,1:T(8,128)(2,1)}, bf16[2048,768]{0,1:T(8,128)(2,1)}) fusion(f32[2048,1536]{0,1:T(8,128)} %fusion.75, bf16[2048,2048]{1,0:T(8,128)(2,1)} %all-gather.12.cloned.1.call-done, bf16[768,2048]{1,0:T(8,128)(2,1)S(1)} %copy-done), kind=kOutput, calls=%fused_computation.20 | convolution fusion | flops 6467616768 | bytes 33554432 | tf_op jit(solution)/shard_map/dot_general | solution.py:630
  525.9 18.7 %convolution_convert_fusion.1 = bf16[2048,2048]{1,0:T(8,128)(2,1)} fusion(bf16[2048,1536]{1,0:T(8,128)(2,1)} %bitcast.267, bf16[2048,768]{0,1:T(8,128)(2,1)} %get-tuple-element.81, bf16[2048,768]{0,1:T(8,128)(2,1)S(1)} %get-tuple-element.80), kind=kOutput, calls=%fused_computation.12 | convolution fusion | flops 12901679104 | bytes 20971520 | tf_op jit(solution)/shard_map/dot_general | solution.py:637
  544.7 88.3 %reduce-scatter.13.cloned.1.call-done = bf16[256,2048]{1,0:T(8,128)(2,1)} async-done(((bf16[2048,2048]{1,0:T(8,128)(2,1)}), bf16[256,2048]{1,0:T(8,128)(2,1)}) %reduce-scatter.13.cloned.1.call-update) | async-done | bytes 1048592 | tf_op jit(solution)/shard_map/reduce_scatter | solution.py:614
  633.0 3.7 fusion.21
  637.3 3.3 fusion.61
  640.6 11.9 %convolution_convert_fusion.5 = bf16[768,2048]{1,0:T(8,128)(2,1)} fusion(bf16[2048,768]{0,1:T(8,128)(2,1)} %get-tuple-element.82, bf16[2048,2048]{1,0:T(8,128)(2,1)} %all-gather.12.cloned.1.call-done), kind=kOutput, calls=%fused_computation.28 | convolution fusion | flops 6444023808 | bytes 14680064 | tf_op jit(solution)/shard_map/dot_general | solution.py:642
  652.6 18.8 %convolution_convert_fusion.4 = bf16[2048,1536]{1,0:T(8,128)(2,1)S(1)} fusion(bf16[2048,2048]{1,0:T(8,128)(2,1)} %all-gather.10.cloned.1.call-done, bf16[2048,768]{0,1:T(8,128)(2,1)} %get-tuple-element.81, bf16[2048,768]{0,1:T(8,128)(2,1)} %copy-done.32), kind=kOutput, calls=%fused_computation.15 | convolution fusion | flops 12900630528 | bytes 20971520 | tf_op jit(solution)/shard_map/dot_general | solution.py:641
  671.3 3.4 copy.215
  676.9 3.4 reshape.456
  680.2 4.9 multiply_reduce_fusion.3
  693.1 2.9 copy.201
  696.0 2.8 reshape.460
  701.4 19.8 %all-gather.14.cloned.1.call-done = bf16[2048,2048]{1,0:T(8,128)(2,1)} async-done(((bf16[256,2048]{1,0:T(8,128)(2,1)}), bf16[2048,2048]{1,0:T(8,128)(2,1)}) %all-gather.14.cloned.1.call-update) | async-done | bytes 8388624 | tf_op jit(solution)/shard_map/all_gather | solution.py:647
  721.2 9.3 multiply_convert_fusion.4
  733.0 3.7 copy.196
  736.7 15.5 %multiply_reduce_fusion = (f32[2,2,1024]{2,1,0:T(2,128)S(1)}, f32[2,2,1024,1024]{2,3,1,0:T(8,128)}) fusion(f32[2,2,1024,1024]{2,3,1,0:T(8,128)} %get-tuple-element.110, f32[2,2,1024]{2,1,0:T(2,128)S(1)} %copy-done.24, bf16[2,2,1024,128]{3,2,1,0:T(8,128)(2,1)} %bitcast.248, bf16[2,1024,128,1]{2,1,3,0:T(8,128)(2,1)} %bitcast.252), kind=kOutput, calls=%fused_computation.2 | convolution fusion | flops 1086320640 | bytes 35160064 | tf_op jit(solution)/shard_map/shgqd,shkd->shgqk/dot_general | solution.py:664
  752.2 12.5 %multiply_convert_fusion = bf16[2,2,1024,1024]{2,3,1,0:T(8,128)(2,1)S(1)} fusion(f32[2,2,1024,1024]{2,3,1,0:T(8,128)} %get-tuple-element.112, f32[2,2,1024]{2,1,0:T(2,128)S(1)} %get-tuple-element.111, f32[2,2,1024,1024]{2,3,1,0:T(8,128)} %get-tuple-element.110, f32[2,2,1024]{2,1,0:T(2,128)S(1)} %copy-done.24), kind=kLoop, calls=%fused_computation.1 | loop fusion | flops 16777216 | bytes 41975808 | tf_op jit(solution)/shard_map/convert_element_type | solution.py:668
  764.7 3.3 broadcast_multiply_fusion
  780.0 6.6 fusion.35
  786.7 5.1 multiply_reduce_fusion.5
  794.2 3.4 copy.236
  797.6 3.1 copy.198
  800.7 7.1 convolution_convert_fusion.7
  807.7 9.1 fusion.36
  816.9 10.4 multiply_convert_fusion.5
  841.9 10.2 convolution_convert_fusion.6
  854.7 41.3 %all_to_all.26 = bf16[8,64,1536]{2,1,0:T(8,128)(2,1)S(1)} all-to-all(bf16[8,64,1536]{2,1,0:T(8,128)(2,1)} %bitcast.246), channel_id=1, replica_groups=mesh['rep'=4,'grp'=8] {'grp'}, dimensions={0} | all-to-all | bytes 3145728 | tf_op jit(solution)/shard_map/all_to_all | solution.py:477
  898.9 25.2 %all_to_all.27 = bf16[8,64,768]{2,1,0:T(8,128)(2,1)} all-to-all(bf16[8,64,768]{2,1,0:T(8,128)(2,1)} %bitcast.250), channel_id=1, replica_groups=mesh['rep'=4,'grp'=8] {'grp'}, dimensions={0} | all-to-all | bytes 1572864 | tf_op jit(solution)/shard_map/all_to_all | solution.py:477
  924.2 11.4 convolution_convert_fusion
  935.6 10.9 convolution_convert_fusion.2
  947.3 6.0 convert_element_type.159
  953.3 61.3 %all-gather.20.cloned.1.call-done = bf16[256,8,1536]{2,1,0:T(8,128)(2,1)} async-done(((bf16[64,8,1536]{2,1,0:T(8,128)(2,1)}), bf16[256,8,1536]{2,1,0:T(8,128)(2,1)}) %all-gather.20.cloned.1.call-update) | async-done | bytes 6291472 | tf_op jit(solution)/shard_map/all_gather | solution.py:478
  1014.6 9.1 copy.217
  1023.8 9.3 convert_bitcast_fusion
  1033.0 10.4 copy.218
  1043.4 19.6 %copy.220 = f32[256,2,6144]{2,1,0:T(2,128)} copy(f32[256,2,6144]{0,2,1:T(8,128)} %bitcast.210) | data formatting | bytes 25165824
  1063.0 2.8 convert_element_type.156
  1065.8 23.0 %all-gather.16.cloned.1.call-done = bf16[256,8,768]{2,0,1:T(8,128)(2,1)} async-done(((bf16[64,8,768]{2,0,1:T(8,128)(2,1)}), bf16[256,8,768]{2,0,1:T(8,128)(2,1)}) %all-gather.16.cloned.1.call-update) | async-done | bytes 3145744 | tf_op jit(solution)/shard_map/all_gather | solution.py:478
  1088.8 2.8 fusion.65
  1096.7 4.1 fusion.64
  1100.9 3.0 copy.211
  1103.9 2.9 copy.212
  1106.7 4.8 pad_maximum_fusion.1
  1111.5 6.6 copy.219
  1120.5 39.8 %psum.7 = f32[4352]{0:T(1024)S(1)} all-reduce(f32[4352]{0:T(1024)S(1)} %pad_maximum_fusion.9), channel_id=1, replica_groups=mesh['rep'=4,'grp'=8] {'rep','grp'}, use_global_device_ids=true, to_apply=%region_24.25 | all-reduce | flops 4352 | bytes 34816 | tf_op jit(solution)/shard_map/psum | solution.py:716
  1161.6 5.8 fusion.17
  (184 shorter events, 90.5 us)
Async XLA Ops:
  8.0 500.4 %copy-start = (bf16[768,2048]{1,0:T(8,128)(2,1)S(1)}, bf16[768,2048]{1,0:T(8,128)(2,1)}, u32[]{:S(2)}) copy-start(bf16[768,2048]{1,0:T(8,128)(2,1)} %param.16) | copy-start | bytes 9437188
  8.0 290.5 %reduce-scatter.9.cloned.1.call-start = ((), (), s32[]{:S(2)}) async-start(), calls=%async_computation.11 | async-start | bytes 9437184 | tf_op jit(solution)/shard_map/reduce_scatter | solution.py:614
  8.1 12.2 %copy-start.30 = (f32[64]{0:T(128)}, f32[64]{0:T(128)S(1)}, u32[]{:S(2)}) copy-start(f32[64]{0:T(128)S(1)} %negate_power_fusion) | copy-start | bytes 772
  8.1 12.2 %copy-start.28 = (f32[128]{0:T(128)}, f32[128]{0:T(128)S(1)}, u32[]{:S(2)}) copy-start(f32[128]{0:T(128)S(1)} %compare_select_fusion) | copy-start | bytes 1540
  155.5 10.5 copy-start.23
  174.0 3.6 copy-start.14
  176.6 1.0 copy-start.11
  183.3 159.2 %all-gather.24.cloned.1.call-start = ((), (), s32[]{:S(2)}) async-start(), calls=%async_computation.26 | async-start | bytes 7864320 | tf_op jit(solution)/shard_map/all_gather | solution.py:465
  206.3 67.2 %copy-start.22 = (f32[8,1,768]{2,1,0:T(1,128)S(1)}, f32[8,1,768]{2,1,0:T(1,128)}, u32[]{:S(2)}) copy-start(f32[8,1,768]{2,1,0:T(1,128)} %get-tuple-element.23) | copy-start | bytes 73732
  273.4 153.1 %all-gather.10.cloned.1.call-start = ((), (), s32[]{:S(2)}) async-start(), calls=%async_computation.12 | async-start | bytes 9437184 | tf_op jit(solution)/shard_map/all_gather | solution.py:622
  274.1 362.5 %copy-start.15 = (f32[1,2,8,128]{3,1,2,0:T(2,128)}, f32[1,2,8,128]{3,1,2,0:T(2,128)S(1)}, u32[]{:S(2)}) copy-start(f32[1,2,8,128]{3,1,2,0:T(2,128)S(1)} %copy.235) | copy-start | bytes 24580
  300.4 336.2 %copy-start.20 = (f32[256]{0:T(256)}, f32[256]{0:T(256)S(1)}, u32[]{:S(2)}) copy-start(f32[256]{0:T(256)S(1)} %add_rsqrt_fusion.2) | copy-start | bytes 3076
  303.4 205.1 %all-gather.12.cloned.1.call-start = ((), (), s32[]{:S(2)}) async-start(), calls=%async_computation.14 | async-start | bytes 9437184 | tf_op jit(solution)/shard_map/all_gather | solution.py:528
  304.0 329.0 %reduce-scatter.13.cloned.1.call-start = ((), (), s32[]{:S(2)}) async-start(), calls=%async_computation.15 | async-start | bytes 9437184 | tf_op jit(solution)/shard_map/reduce_scatter | solution.py:614
  524.3 1.7 copy-start.32
  544.6 176.5 %all-gather.14.cloned.1.call-start = ((), (), s32[]{:S(2)}) async-start(), calls=%async_computation.16 | async-start | bytes 9437184 | tf_op jit(solution)/shard_map/all_gather | solution.py:647
  633.0 4.3 copy-start.2
  633.0 4.3 copy-start.3
  633.0 4.3 copy-start.8
  636.7 0.6 copy-start.25
  640.6 213.5 %reduce-scatter.23.cloned.1.call-start = ((), (), s32[]{:S(2)}) async-start(), calls=%async_computation.24 | async-start | bytes 3932160 | tf_op jit(solution)/shard_map/reduce_scatter | solution.py:482
  652.5 202.2 %reduce-scatter.21.cloned.1.call-start = ((), (), s32[]{:S(2)}) async-start(), calls=%async_computation.22 | async-start | bytes 7864320 | tf_op jit(solution)/shard_map/reduce_scatter | solution.py:475
  674.7 223.8 %reduce-scatter.19.cloned.1.call-start = ((), (), s32[]{:S(2)}) async-start(), calls=%async_computation.20 | async-start | bytes 1310720 | tf_op jit(solution)/shard_map/reduce_scatter | solution.py:482
  696.0 4.4 copy-start.18
  696.0 4.4 copy-start.31
  730.5 6.3 copy-start.24
  752.2 12.5 %copy-start.12 = (bf16[2,1024,128,1]{1,2,0,3:T(8,128)(2,1)S(1)}, bf16[2,1024,128,1]{1,2,0,3:T(8,128)(2,1)}, u32[]{:S(2)}) copy-start(bf16[2,1024,128,1]{1,2,0,3:T(8,128)(2,1)} %reshape.492) | copy-start | bytes 1572868
  764.7 4.0 copy-start.1
  769.9 1.0 copy-start.6
  779.9 6.7 copy-start.9
  779.9 6.7 copy-start.13
  779.9 6.7 copy-start.29
  786.7 5.1 copy-start.4
  786.7 5.1 copy-start.5
  786.7 5.1 copy-start.7
  786.7 5.1 copy-start.10
  816.9 82.0 %reduce-scatter.17.cloned.1.call-start = ((), (), s32[]{:S(2)}) async-start(), calls=%async_computation.18 | async-start | bytes 3932160 | tf_op jit(solution)/shard_map/reduce_scatter | solution.py:475
  854.0 93.2 %all-gather.22.cloned.1.call-start = ((), (), s32[]{:S(2)}) async-start(), calls=%async_computation.25 | async-start | bytes 3932160 | tf_op jit(solution)/shard_map/all_gather | solution.py:483
  854.6 160.0 %all-gather.20.cloned.1.call-start = ((), (), s32[]{:S(2)}) async-start(), calls=%async_computation.23 | async-start | bytes 7864320 | tf_op jit(solution)/shard_map/all_gather | solution.py:478
  898.1 164.9 %all-gather.18.cloned.1.call-start = ((), (), s32[]{:S(2)}) async-start(), calls=%async_computation.21 | async-start | bytes 1310720 | tf_op jit(solution)/shard_map/all_gather | solution.py:483
  898.8 190.0 %all-gather.16.cloned.1.call-start = ((), (), s32[]{:S(2)}) async-start(), calls=%async_computation.19 | async-start | bytes 3932160 | tf_op jit(solution)/shard_map/all_gather | solution.py:478
  924.1 194.0 %reduce-scatter.15.cloned.1.call-start = ((), (), s32[]{:S(2)}) async-start(), calls=%async_computation.17 | async-start | bytes 9437184 | tf_op jit(solution)/shard_map/reduce_scatter | solution.py:614
  935.6 226.0 %reduce-scatter.11.cloned.1.call-start = ((), (), s32[]{:S(2)}) async-start(), calls=%async_computation.13 | async-start | bytes 9437184 | tf_op jit(solution)/shard_map/reduce_scatter | solution.py:614
  946.5 0.7 copy-start.19
  947.2 6.1 copy-start.27
  1111.5 9.0 copy-start.17
  1111.5 50.1 %copy-start.16 = (f32[1,2,8,128]{3,1,2,0:T(2,128)S(1)}, f32[1,2,8,128]{3,1,2,0:T(2,128)}, u32[]{:S(2)}) copy-start(f32[1,2,8,128]{3,1,2,0:T(2,128)} %copy-done.15) | copy-start | bytes 24580
  1111.5 50.1 %copy-start.21 = (f32[256]{0:T(256)S(1)}, f32[256]{0:T(256)}, u32[]{:S(2)}) copy-start(f32[256]{0:T(256)} %copy-done.20) | copy-start | bytes 3076
  1111.5 50.1 %copy-start.26 = (f32[256]{0:T(256)S(1)}, f32[256]{0:T(256)}, u32[]{:S(2)}) copy-start(f32[256]{0:T(256)} %copy-done.25) | copy-start | bytes 3076
Sparse Core Ops, SparseCore 0:
  183.5 114.9 reduce-scatter.8
  544.8 88.1 reduce-scatter.12
  640.7 80.3 all-gather.13
  935.7 88.8 reduce-scatter.14
  1026.8 87.9 reduce-scatter.10
Sparse Core Ops, SparseCore 1:
  273.5 69.0 all-gather.23
  344.6 81.9 all-gather.9
  428.0 80.4 all-gather.11
  652.6 42.1 reduce-scatter.22
  698.4 70.0 reduce-scatter.20
  816.9 26.2 reduce-scatter.18
  854.1 42.3 reduce-scatter.16
  898.3 43.8 all-gather.21
  944.6 70.0 all-gather.19
  1016.6 26.4 all-gather.17
  1045.0 43.8 all-gather.15

commit v3 on v2

--- a/solution.py
+++ b/solution.py
@@ -113,14 +113,23 @@
 
 
 class Gather:
-    def __init__(self, owners, buf, send, recv):
+    def __init__(self, owners, buf, send, recv, half=0):
         self.owners, self.chips = owners, owners // 2
         self.me = lax.axis_index("grp")
         self.place, self.core = self.me // 2, self.me % 2
-        self.buf, self.send, self.recv = buf, send, recv
+        self.buf, self.send, self.recv, self.half = buf, send, recv, half
+
+    def of(self, block):
+        return self.buf.at[block, self.half] if len(self.buf.shape) == 4 else self.buf.at[block]
+
+    def sent(self, way, at):
+        return self.send.at[self.half, way, at]
+
+    def got(self, block):
+        return self.recv.at[self.half, block]
 
     def copies(self, block, source=None):
-        src = self.buf.at[block] if source is None else source
+        src = self.of(block) if source is None else source
         at = block // 2
         ways = (
             ((at <= self.place) & (self.place < self.chips - 1), self.me + 2),
@@ -130,7 +139,7 @@
         return [
             (
                 when,
-                to_grp(src, self.buf.at[block], self.send.at[way, at], self.recv.at[block], device),
+                to_grp(src, self.of(block), self.sent(way, at), self.got(block), device),
             )
             for way, (when, device) in enumerate(ways)
         ]
@@ -144,12 +153,12 @@
 
     def step(self, k):
         block = 2 * nearest(self.place, k, self.chips) + self.core
-        arrived(self.buf.at[block], self.recv.at[block])
+        arrived(self.of(block), self.got(block))
         self.forward(block)
 
     def sibling(self, k):
         block = 2 * nearest(self.place, k, self.chips) + 1 - self.core
-        arrived(self.buf.at[block], self.recv.at[block])
+        arrived(self.of(block), self.got(block))
 
     def finish(self):
         def one(at, _):
@@ -163,10 +172,10 @@
         lax.fori_loop(0, self.chips, one, 0)
 
     @staticmethod
-    def scratch(owners):
+    def scratch(owners, halves=1):
         return [
-            pltpu.SemaphoreType.DMA((3, owners // 2)),
-            pltpu.SemaphoreType.DMA((owners,)),
+            pltpu.SemaphoreType.DMA((halves, 3, owners // 2)),
+            pltpu.SemaphoreType.DMA((halves, owners)),
         ]
 
 
@@ -448,22 +457,1099 @@
     )(tokens, w_qkvg, small, cosine, sine)
 
 
+def by_distance(place, step, chips):
+    return nearest(place, chips - 1 - step, chips)
+
+
+class Scatter:
+    def __init__(self, owners, bufs, sems, order, parts, half=0):
+        self.owners, self.chips = owners, owners // 2
+        self.me = lax.axis_index("grp")
+        self.place, self.core = self.me // 2, self.me % 2
+        self.stage, self.near, self.line, self.both = bufs
+        self.acc = self.both.at[self.core]
+        self.near_send, self.near_recv, self.line_send, self.line_recv = sems
+        self.order, self.parts, self.half = order, parts, half
+        self.part = self.both.shape[1] // parts
+
+    def at(self, k):
+        return self.order(self.place, k, self.chips)
+
+    def near_copy(self, k):
+        at = self.at(k)
+        return to_grp(
+            self.stage.at[self.half, k % 2],
+            self.near.at[self.half, at],
+            self.near_send.at[self.half, k % 2],
+            self.near_recv.at[self.half, at],
+            self.me + 1 - 2 * self.core,
+        )
+
+    def rows(self, s):
+        return pl.ds(s * self.part, self.part)
+
+    def line_copy(self, at, s):
+        target = self.place + jnp.where(at > self.place, 1, -1)
+        slot = jnp.where((target == at) & (at < self.place), self.chips, at)
+        return to_grp(
+            self.near.at[self.half, at, self.rows(s)],
+            self.line.at[self.half, slot, self.rows(s)],
+            self.line_send.at[self.half, at, s],
+            self.line_recv.at[self.half, slot, s],
+            2 * target + self.core,
+        )
+
+    def prepare(self, k, term):
+        @pl.when(k >= 2)
+        def _():
+            self.near_copy(k - 2).wait_send()
+
+        self.both[...] = term(self.at(k)).reshape(self.both.shape)
+        self.stage[self.half, k % 2] = self.both[1 - self.core].astype(BF16)
+        self.near_copy(k).start()
+
+    def add(self, slot, s):
+        part = self.line.at[self.half, slot, self.rows(s)]
+        arrived(part, self.line_recv.at[self.half, slot, s])
+        self.acc[self.rows(s)] += part[...].astype(F32)
+
+    def combine(self, k):
+        at = self.at(k)
+        arrived(self.near.at[self.half, at], self.near_recv.at[self.half, at])
+        self.acc[...] += self.near[self.half, at].astype(F32)
+        below = self.place > 0
+        above = self.place < self.chips - 1
+
+        def one(s, _):
+            @pl.when(((at >= self.place) & below) | ((at < self.place) & above))
+            def _():
+                self.add(at, s)
+
+            @pl.when((at == self.place) & above)
+            def _():
+                self.add(self.chips, s)
+
+            @pl.when(at != self.place)
+            def _():
+                self.near[self.half, at, self.rows(s)] = self.acc[self.rows(s)].astype(BF16)
+                self.line_copy(at, s).start()
+
+            return 0
+
+        lax.fori_loop(0, self.parts, one, 0)
+
+    def finish(self):
+        self.near_copy(self.chips - 2).wait_send()
+        self.near_copy(self.chips - 1).wait_send()
+
+        def one(at, _):
+            @pl.when(at != self.place)
+            def _():
+                for s in range(self.parts):
+                    self.line_copy(at, s).wait_send()
+
+            return 0
+
+        lax.fori_loop(0, self.chips, one, 0)
+
+    @staticmethod
+    def scratch(owners, rows, width, parts, halves=1):
+        chips = owners // 2
+        rows //= halves
+        return [
+            pltpu.VMEM((halves, 2, rows, width), BF16),
+            pltpu.VMEM((halves, chips, rows, width), BF16),
+            pltpu.VMEM((halves, chips + 1, rows, width), BF16),
+            pltpu.VMEM((2, rows, width), F32),
+            pltpu.SemaphoreType.DMA((halves, 2)),
+            pltpu.SemaphoreType.DMA((halves, chips)),
+            pltpu.SemaphoreType.DMA((halves, chips, parts)),
+            pltpu.SemaphoreType.DMA((halves, chips + 1, parts)),
+        ]
+
+
+PARTS = 4
+
+
+class RepSum:
+    def __init__(self, owners, reps, units, along, held, came, result, sems):
+        self.owners, self.reps, self.units, self.along = owners, reps, units, along
+        self.me, self.rep = lax.axis_index("grp"), lax.axis_index("rep")
+        self.bits = reps.bit_length() - 1
+        self.held, self.came, self.result = held, came, result
+        self.down_send, self.down_recv, self.own_send, self.own_recv, self.up_send, self.up_recv = sems
+
+    def weight(self, t, j):
+        which = (t + j) % self.bits
+        return sum(jnp.where(which == b, 1 << b, 0) for b in range(self.bits))
+
+    @staticmethod
+    def flip(index, weight):
+        return index + weight * (1 - 2 * ((index // weight) % 2))
+
+    def spread(self, index, t, bits):
+        out = [index]
+        for j in bits:
+            out += [self.flip(i, self.weight(t, j)) for i in out]
+        return out
+
+    def unit(self, t):
+        return lax.rem(self.me + t, self.owners) if self.along else t
+
+    def source(self, t):
+        return lax.rem(self.me + self.owners - t, self.owners) if self.along else t
+
+    def downs(self, t, j):
+        u = self.unit(t)
+        first_index = sum(1 << (self.bits - 1 - i) for i in range(j))
+        partner = self.flip(self.rep, self.weight(t, j))
+        return [
+            to_rep(
+                self.held.at[u, s],
+                self.came.at[u, first_index + c],
+                self.down_send.at[u, first_index + c],
+                self.down_recv.at[u, first_index + c],
+                partner,
+            )
+            for c, s in enumerate(self.spread(partner, t, range(j + 1, self.bits)))
+        ]
+
+    def ups(self, t, j):
+        e = self.source(t)
+        held = self.spread(self.rep, t, range(self.bits - 1, self.bits - 1 - j, -1))
+        partner = self.flip(self.rep, self.weight(t, self.bits - 1 - j))
+        return [
+            to_rep(
+                self.result.at[e, s],
+                self.result.at[e, s],
+                self.up_send.at[e, (1 << j) - 1 + c],
+                self.up_recv.at[e, s],
+                partner,
+            )
+            for c, s in enumerate(held)
+        ]
+
+    def deliver(self, t, do_local, do_remote):
+        u = self.unit(t)
+        source = self.held.at[u, self.rep]
+        slot = self.me if self.along else u
+        local = pltpu.make_async_copy(source, self.result.at[slot, self.rep], self.own_recv.at[slot])
+        if not self.along:
+            do_local(local)
+            return
+        remote = to_grp(
+            source,
+            self.result.at[slot, self.rep],
+            self.own_send.at[u],
+            self.own_recv.at[slot],
+            u,
+        )
+        pl.when(u == self.me)(lambda: do_local(local))
+        pl.when(u != self.me)(lambda: do_remote(remote))
+
+    def tick(self, t, term):
+        def phase(lag):
+            return (t >= lag) & (t < self.units + lag)
+
+        @pl.when(phase(0))
+        def _():
+            u = self.unit(t)
+            self.held[u] = term(t, u).astype(BF16).reshape(self.held.shape[1:])
+            for copy in self.downs(t, 0):
+                copy.start()
+
+        for j in range(1, self.bits + 1):
+
+            @pl.when(phase(j))
+            def _(j=j, t=t - j):
+                u = self.unit(t)
+                first_index = sum(1 << (self.bits - 1 - i) for i in range(j - 1))
+                for c, s in enumerate(self.spread(self.rep, t, range(j, self.bits))):
+                    part = self.came.at[u, first_index + c]
+                    arrived(part, self.down_recv.at[u, first_index + c])
+                    self.held[u, s] = (self.held[u, s].astype(F32) + part[...].astype(F32)).astype(
+                        BF16
+                    )
+                if j < self.bits:
+                    for copy in self.downs(t, j):
+                        copy.start()
+                else:
+                    self.deliver(t, lambda c: c.start(), lambda c: c.start())
+
+        for j in range(self.bits + 1):
+
+            @pl.when(phase(self.bits + 1 + j))
+            def _(j=j, t=t - self.bits - 1 - j):
+                e = self.source(t)
+                if j == 0:
+                    arrived(self.result.at[e, self.rep], self.own_recv.at[e])
+                else:
+                    bit = self.bits - j
+                    held = self.spread(self.rep, t, range(self.bits - 1, bit, -1))
+                    for s in held:
+                        s = self.flip(s, self.weight(t, bit))
+                        arrived(self.result.at[e, s], self.up_recv.at[e, s])
+                if j < self.bits:
+                    for copy in self.ups(t, j):
+                        copy.start()
+
+    def ticks(self):
+        return self.units + 2 * self.bits + 1
+
+    def finish(self):
+        def one(t, _):
+            for j in range(self.bits):
+                for copy in self.downs(t, j) + self.ups(t, j):
+                    copy.wait_send()
+            self.deliver(t, lambda c: None, lambda c: c.wait_send())
+            return 0
+
+        lax.fori_loop(0, self.units, one, 0)
+
+    @staticmethod
+    def scratch(reps, units, share, cols):
+        dma = pltpu.SemaphoreType.DMA
+        return [
+            pltpu.VMEM((units, reps, share, cols), BF16),
+            pltpu.VMEM((units, reps - 1, share, cols), BF16),
+            dma((units, reps - 1)),
+            dma((units, reps - 1)),
+            dma((units,)),
+            dma((units,)),
+            dma((units, reps - 1)),
+            dma((units, reps)),
+        ]
+
+
+def interleave(gather, scatter, term, ready=None, then=None):
+    chips = gather.chips
+    middle = (gather.place > 0) & (gather.place < chips - 1)
+
+    def stage(k, _):
+        if ready is not None:
+            ready(k)
+        scatter.prepare(k, term)
+
+        @pl.when(middle & (2 * k + 1 < chips))
+        def _():
+            gather.step(2 * k + 1)
+
+        @pl.when(middle & (2 * k + 2 < chips))
+        def _():
+            gather.step(2 * k + 2)
+
+        scatter.combine(k)
+
+        @pl.when((~middle) & (k + 1 < chips))
+        def _():
+            gather.step(k + 1)
+
+        then(k)
+        return 0
+
+    lax.fori_loop(0, chips, stage, 0)
+
+
+def attention_kernel(
+    owners,
+    reps,
+    heads,
+    kv_heads,
+    tokens_ref,
+    query_ref,
+    key_ref,
+    value_ref,
+    gate_ref,
+    position_col_ref,
+    position_row_ref,
+    out_ref,
+    gain_ref,
+    cotangent_ref,
+    in_pieces_ref,
+    attn_out,
+    hidden_out,
+    entry_out,
+    cotangent_out,
+    columns_out,
+    local_sem,
+    *rest,
+):
+    me, rep = lax.axis_index("grp"), lax.axis_index("rep")
+    scatter = Scatter(owners, rest[:4], rest[4:8], by_distance, PARTS)
+    gather = Gather(owners, cotangent_out, *rest[8:10])
+    reshard = Reshard(owners, reps, columns_out, rest[10:14])
+    share = in_pieces_ref.shape[1] // reps
+    cols = in_pieces_ref.shape[2]
+    my_rows = pl.ds(pl.multiple_of(rep * share, share), share)
+
+    def pieces(owner):
+        return [(in_pieces_ref.at[owner, my_rows], pl.ds(0, cols))]
+
+    own = pltpu.make_async_copy(cotangent_ref, cotangent_out.at[me], local_sem)
+    own.start()
+    meet(owners, reps)
+    gather.forward(me, cotangent_ref)
+    reshard.start(pieces)
+    per_kv = heads // kv_heads
+    block_rows = 2 * BLOCK_TOKENS
+
+    def attend(at):
+        for s in range(GROUP_SEQUENCES):
+            rows = slice(s * block_rows, (s + 1) * block_rows)
+            allowed = position_row_ref[s] <= position_col_ref[at, rows]
+            allowed = jnp.concatenate([allowed] * per_kv, axis=0)
+            for kv in range(kv_heads):
+                span = slice(kv * HEAD_SIZE, (kv + 1) * HEAD_SIZE)
+                spans = [
+                    slice(h * HEAD_SIZE, (h + 1) * HEAD_SIZE)
+                    for h in range(kv * per_kv, (kv + 1) * per_kv)
+                ]
+                query = jnp.concatenate([query_ref[at, rows, h] for h in spans], axis=0)
+                keys = key_ref[:, rows, span].reshape(-1, HEAD_SIZE)
+                values = value_ref[:, rows, span].reshape(-1, HEAD_SIZE)
+                scores = dot_nt(query, keys) * HEAD_SIZE ** (-0.5)
+                scores = jnp.where(allowed, scores, masked_value)
+                exps = jnp.exp(scores - jnp.max(scores, axis=-1, keepdims=True))
+                probability = exps / jnp.sum(exps, axis=-1, keepdims=True)
+                attended = dot(probability.astype(BF16), values)
+                for i, h in enumerate(spans):
+                    gated = attended[i * block_rows : (i + 1) * block_rows] * jax.nn.sigmoid(
+                        gate_ref[at, rows, h]
+                    )
+                    attn_out[at, rows, h] = gated.astype(BF16)
+
+    def ready(k):
+        at = scatter.at(k)
+
+        def one(core, _):
+            attend(2 * at + core)
+            return 0
+
+        lax.fori_loop(0, 2, one, 0)
+
+    def term(at):
+        both = attn_out[pl.ds(2 * at, 2)]
+        return dot(both.reshape(-1, both.shape[-1]), out_ref[...])
+
+    def then(k):
+        pl.when(k == 0)(reshard.relay)
+        gather.sibling(k)
+
+    interleave(gather, scatter, term, ready, then)
+    hidden = tokens_ref[...].astype(F32) + scatter.acc[...]
+    hidden_out[...] = hidden
+    entry_out[...] = (head_norm(hidden)[0] * gain_ref[...]).astype(BF16)
+    own.wait()
+    reshard.wait()
+    gather.finish()
+    scatter.finish()
+    reshard.finish()
+
+
+def attention(
+    owners,
+    reps,
+    heads,
+    kv_heads,
+    tokens,
+    query_rot,
+    key_rot,
+    value_rows,
+    gate_raw,
+    position_col,
+    position_row,
+    w_out,
+    gain_mlp,
+    cotangent,
+    in_pieces,
+):
+    rows, width = tokens.shape
+    shape = jax.ShapeDtypeStruct
+    share = in_pieces.shape[1] // reps
+    outs = (
+        shape(query_rot.shape, BF16),
+        shape((rows, width), F32),
+        shape((rows, width), BF16),
+        shape((owners, rows, width), BF16),
+        shape((owners, reps, share, in_pieces.shape[2]), BF16),
+    )
+    return pl.pallas_call(
+        functools.partial(attention_kernel, owners, reps, heads, kv_heads),
+        out_shape=outs,
+        in_specs=[vmem()] * 9 + [anywhere()] * 2,
+        out_specs=(vmem(),) * 3 + (anywhere(),) * 2,
+        scratch_shapes=[pltpu.SemaphoreType.DMA]
+        + Scatter.scratch(owners, rows, width, PARTS)
+        + Gather.scratch(owners)
+        + Reshard.scratch(owners, reps),
+        compiler_params=pltpu.CompilerParams(
+            collective_id=1, has_side_effects=True, vmem_limit_bytes=60 * 2**20
+        ),
+        cost_estimate=pl.CostEstimate(
+            flops=4 * owners * rows * width * query_rot.shape[2],
+            bytes_accessed=40 * 2**20,
+            transcendentals=0,
+        ),
+        name="attention",
+    )(
+        tokens,
+        query_rot,
+        key_rot,
+        value_rows,
+        gate_raw,
+        position_col,
+        position_row,
+        w_out,
+        gain_mlp,
+        cotangent,
+        in_pieces,
+    )
+
+
+def mlp_kernel(
+    owners,
+    reps,
+    entry_ref,
+    cotangent_all_ref,
+    in_ref,
+    down_ref,
+    hidden_ref,
+    cotangent_ref,
+    gain_ref,
+    entry_all,
+    activated_out,
+    grads_out,
+    grad_hidden_out,
+    grad_branch_out,
+    gain_out,
+    entry_buf,
+    cotangent_buf,
+    activated_buf,
+    grad_entry_buf,
+    local_sem,
+    load_sem,
+    store_sem,
+    *rest,
+):
+    me = lax.axis_index("grp")
+    chips = owners // 2
+    halves = GROUP_SEQUENCES
+    gathers = [Gather(owners, entry_all, *rest[8:10], half) for half in range(halves)]
+    scatters = [
+        Scatter(owners, rest[:4], rest[4:8], by_distance, HALF_PARTS, half)
+        for half in range(halves)
+    ]
+    units = down_ref.shape[0]
+    place = gathers[0].place
+    own = pltpu.make_async_copy(entry_ref, entry_all.at[me], local_sem)
+    own.start()
+    meet(owners, reps)
+    gathers[0].forward(me, entry_ref.at[0])
+    own.wait()
+
+    def compute(k, half, first):
+        gather = gathers[half]
+        pair = pl.ds(2 * nearest(place, k, chips), 2)
+        cotangent_load = pltpu.make_async_copy(
+            cotangent_all_ref.at[pair, half], cotangent_buf, load_sem.at[1]
+        )
+        cotangent_load.start()
+        gather.sibling(k)
+        entry_load = pltpu.make_async_copy(entry_all.at[pair, half], entry_buf, load_sem.at[0])
+        entry_load.start()
+        cotangent_load.wait()
+        both = cotangent_buf.shape[0] * cotangent_buf.shape[1]
+        grad_activated = dot_nt(cotangent_buf[...].reshape(both, -1), down_ref[...])
+        entry_load.wait()
+        gate_up = dot(entry_buf[...].reshape(both, -1), in_ref[...])
+        gate, up = gate_up[:, :units], gate_up[:, units:]
+        sig = jax.nn.sigmoid(gate)
+        silu = gate * sig
+        store = pltpu.make_async_copy(activated_buf, activated_out.at[pair, half], store_sem)
+
+        @pl.when(jnp.logical_not(first))
+        def _():
+            store.wait()
+
+        activated_buf[...] = (silu * up).astype(BF16).reshape(activated_buf.shape)
+        store.start()
+        shape = activated_buf.shape
+        grads_out[pair, half, :, :units] = (
+            (grad_activated * up * sig * (1.0 + gate * (1.0 - sig))).astype(BF16).reshape(shape)
+        )
+        grads_out[pair, half, :, units:] = (grad_activated * silu).astype(BF16).reshape(shape)
+
+    def term_of(half):
+        def term(at):
+            both = grads_out[pl.ds(2 * at, 2), half]
+            return dot_nt(both.reshape(-1, both.shape[-1]), in_ref[...])
+
+        return term
+
+    def front(k, _):
+        @pl.when(k > 0)
+        def _():
+            gathers[0].step(k)
+
+        compute(k, 0, k == 0)
+        return 0
+
+    lax.fori_loop(0, chips, front, 0)
+    for half in range(1, halves):
+        gathers[half].forward(me, entry_ref.at[half])
+        interleave(
+            gathers[half],
+            scatters[half - 1],
+            term_of(half - 1),
+            then=lambda k, half=half: compute(k, half, k < 0),
+        )
+        grad_entry_buf[half - 1] = scatters[half - 1].acc[...]
+
+    def back(k, _):
+        scatters[-1].prepare(k, term_of(halves - 1))
+        scatters[-1].combine(k)
+        return 0
+
+    lax.fori_loop(0, chips, back, 0)
+    grad_entry_buf[halves - 1] = scatters[-1].acc[...]
+    hidden = hidden_ref[...]
+    normed, scale = head_norm(hidden)
+    grad_entry = grad_entry_buf[...].reshape(hidden.shape)
+    gain_out[...] = jnp.sum(grad_entry * normed, axis=0, keepdims=True)
+    weighted = grad_entry * gain_ref[...]
+    grad_hidden = cotangent_ref[...].astype(F32) + scale * (
+        weighted - normed * jnp.mean(weighted * normed, axis=-1, keepdims=True)
+    )
+    grad_hidden_out[...] = grad_hidden
+    grad_branch_out[...] = grad_hidden.astype(BF16)
+    pltpu.make_async_copy(
+        activated_buf, activated_out.at[pl.ds(0, 2), 0], store_sem
+    ).wait()
+    for half in range(halves):
+        gathers[half].finish()
+        scatters[half].finish()
+
+
+HALF_PARTS = 2
+
+
+def mlp(owners, reps, entry, cotangent_all, in_cols, w_down, hidden, cotangent, gain_mlp):
+    rows, width = entry.shape
+    units = w_down.shape[0]
+    halves = GROUP_SEQUENCES
+    half_rows = rows // halves
+    shape = jax.ShapeDtypeStruct
+    outs = (
+        shape((owners, halves, half_rows, width), BF16),
+        shape((owners, halves, half_rows, units), BF16),
+        shape((owners, halves, half_rows, 2 * units), BF16),
+        shape((rows, width), F32),
+        shape((rows, width), BF16),
+        shape((1, width), F32),
+    )
+    return pl.pallas_call(
+        functools.partial(mlp_kernel, owners, reps),
+        out_shape=outs,
+        in_specs=[anywhere()] * 2 + [vmem()] * 5,
+        out_specs=(anywhere(),) * 2 + (vmem(),) * 4,
+        scratch_shapes=[
+            pltpu.VMEM((2, half_rows, width), BF16),
+            pltpu.VMEM((2, half_rows, width), BF16),
+            pltpu.VMEM((2, half_rows, units), BF16),
+            pltpu.VMEM((halves, half_rows, width), F32),
+            pltpu.SemaphoreType.DMA,
+            pltpu.SemaphoreType.DMA((2,)),
+            pltpu.SemaphoreType.DMA,
+        ]
+        + Scatter.scratch(owners, rows, width, HALF_PARTS, halves)
+        + Gather.scratch(owners, halves),
+        compiler_params=pltpu.CompilerParams(
+            collective_id=2, has_side_effects=True, vmem_limit_bytes=60 * 2**20
+        ),
+        cost_estimate=pl.CostEstimate(
+            flops=10 * owners * rows * width * units,
+            bytes_accessed=40 * 2**20,
+            transcendentals=0,
+        ),
+        name="mlp",
+    )(
+        entry.reshape(halves, half_rows, width),
+        cotangent_all.reshape(owners, halves, half_rows, width),
+        in_cols,
+        w_down,
+        hidden,
+        cotangent,
+        gain_mlp,
+    )
+
+
+def unturned_norm_back(grad, raw, gain, cosine, sine):
+    back = turn_back(grad, cosine, sine)
+    normed, scale = head_norm(raw)
+    weighted = back * gain
+    grad_raw = scale * (weighted - normed * jnp.mean(weighted * normed, axis=-1, keepdims=True))
+    return grad_raw, jnp.sum(back * normed, axis=0, keepdims=True)
+
+
+def backward_kernel(
+    owners,
+    reps,
+    heads,
+    kv_heads,
+    branch_ref,
+    activated_ref,
+    down_ref,
+    out_ref,
+    hidden_ref,
+    query_ref,
+    query_rot_ref,
+    gate_ref,
+    key_ref,
+    key_rot_ref,
+    value_ref,
+    position_col_ref,
+    position_row_ref,
+    cosine_ref,
+    sine_ref,
+    heads_gain_ref,
+    attn_out_ref,
+    branch_all,
+    output_out,
+    grads_out,
+    gain_out,
+    out_term,
+    branch_buf,
+    key_sum,
+    value_sum,
+    local_sem,
+    load_sem,
+    *rest,
+):
+    me = lax.axis_index("grp")
+    chips = owners // 2
+    scatter = Scatter(owners, rest[:4], rest[4:8], by_distance, PARTS)
+    gather = Gather(owners, branch_all, *rest[8:10])
+    own = pltpu.make_async_copy(branch_ref, branch_all.at[me], local_sem)
+    own.start()
+    meet(owners, reps)
+    gather.forward(me, branch_ref)
+    own.wait()
+    key_sum[...] = jnp.zeros_like(key_sum)
+    value_sum[...] = jnp.zeros_like(value_sum)
+    gain_out[...] = jnp.zeros_like(gain_out)
+    out_term[...] = jnp.zeros_like(out_term)
+    per_kv = heads // kv_heads
+    q_cols, kv_cols = heads * HEAD_SIZE, kv_heads * HEAD_SIZE
+    block_rows = 2 * BLOCK_TOKENS
+    root = HEAD_SIZE ** (-0.5)
+    gain_query = heads_gain_ref[:, :HEAD_SIZE]
+    gain_key = heads_gain_ref[:, HEAD_SIZE:]
+
+    def block(at):
+        load = pltpu.make_async_copy(branch_all.at[at], branch_buf, load_sem)
+        load.start()
+        load.wait()
+        grad_attn_out = dot_nt(branch_buf[...], out_ref[...])
+        out_term[...] += dot_tn(attn_out_ref[at], branch_buf[...])
+        for s in range(GROUP_SEQUENCES):
+            rows = slice(s * block_rows, (s + 1) * block_rows)
+            cosine, sine = cosine_ref[at, rows], sine_ref[at, rows]
+            allowed = position_row_ref[s] <= position_col_ref[at, rows]
+            allowed = jnp.concatenate([allowed] * per_kv, axis=0)
+            for kv in range(kv_heads):
+                span = slice(kv * HEAD_SIZE, (kv + 1) * HEAD_SIZE)
+                spans = [
+                    slice(h * HEAD_SIZE, (h + 1) * HEAD_SIZE)
+                    for h in range(kv * per_kv, (kv + 1) * per_kv)
+                ]
+                query = jnp.concatenate([query_rot_ref[at, rows, h] for h in spans], axis=0)
+                keys = key_rot_ref[:, rows, span].reshape(-1, HEAD_SIZE)
+                values = value_ref[:, rows, span].reshape(-1, HEAD_SIZE)
+                scores = dot_nt(query, keys) * root
+                scores = jnp.where(allowed, scores, masked_value)
+                exps = jnp.exp(scores - jnp.max(scores, axis=-1, keepdims=True))
+                exact = exps / jnp.sum(exps, axis=-1, keepdims=True)
+                low = exact.astype(BF16)
+                attended = dot(low, values)
+                inputs = []
+                for i, h in enumerate(spans):
+                    grad = grad_attn_out[rows, h]
+                    sig = jax.nn.sigmoid(gate_ref[at, rows, h])
+                    inputs.append((grad * sig).astype(BF16))
+                    gated = slice(q_cols + h.start, q_cols + h.stop)
+                    grads_out[at, rows, gated] = (
+                        grad
+                        * attended[i * block_rows : (i + 1) * block_rows]
+                        * sig
+                        * (1.0 - sig)
+                    ).astype(BF16)
+                grad_attended = jnp.concatenate(inputs, axis=0)
+                grad_probs = dot_nt(grad_attended, values)
+                inner = jnp.sum(exact * grad_probs, axis=-1, keepdims=True)
+                grad_scores = (exact * (grad_probs - inner)).astype(BF16)
+                grad_query = dot(grad_scores, keys) * root
+                key_sum[s, kv] += dot_tn(grad_scores, query)
+                value_sum[s, kv] += dot_tn(low, grad_attended)
+                for i, h in enumerate(spans):
+                    grad_raw, gain_sum = unturned_norm_back(
+                        grad_query[i * block_rows : (i + 1) * block_rows],
+                        query_ref[at, rows, h],
+                        gain_query,
+                        cosine,
+                        sine,
+                    )
+                    grads_out[at, rows, h] = grad_raw.astype(BF16)
+                    gain_out[:, :HEAD_SIZE] += gain_sum
+
+    def term(at):
+        both = activated_ref[pl.ds(2 * at, 2)]
+        return dot(both.reshape(-1, both.shape[-1]), down_ref[...])
+
+    def then(k):
+        def one(which, _):
+            @pl.when(which == 1)
+            def _():
+                gather.sibling(k)
+
+            block(
+                2 * nearest(gather.place, k, chips)
+                + jnp.where(which == 0, gather.core, 1 - gather.core)
+            )
+            return 0
+
+        lax.fori_loop(0, 2, one, 0)
+
+    interleave(gather, scatter, term, then=then)
+    output_out[...] = (hidden_ref[...] + scatter.acc[...]).astype(BF16)
+
+    def keys(at, _):
+        for s in range(GROUP_SEQUENCES):
+            rows = slice(s * block_rows, (s + 1) * block_rows)
+            for kv in range(kv_heads):
+                span = slice(kv * HEAD_SIZE, (kv + 1) * HEAD_SIZE)
+                place = pl.ds(pl.multiple_of(at * block_rows, block_rows), block_rows)
+                grad_raw, gain_sum = unturned_norm_back(
+                    key_sum[s, kv, place] * root,
+                    key_ref[at, rows, span],
+                    gain_key,
+                    cosine_ref[at, rows],
+                    sine_ref[at, rows],
+                )
+                first_col = 2 * q_cols + kv * HEAD_SIZE
+                grads_out[at, rows, first_col : first_col + HEAD_SIZE] = grad_raw.astype(BF16)
+                first_col += kv_cols
+                grads_out[at, rows, first_col : first_col + HEAD_SIZE] = value_sum[
+                    s, kv, place
+                ].astype(BF16)
+                gain_out[:, HEAD_SIZE:] += gain_sum
+        return 0
+
+    lax.fori_loop(0, owners, keys, 0)
+    gather.finish()
+    scatter.finish()
+
+
+def backward(
+    owners,
+    reps,
+    heads,
+    kv_heads,
+    branch,
+    activated,
+    w_down,
+    w_out,
+    hidden,
+    query_raw,
+    query_rot,
+    gate_raw,
+    key_raw,
+    key_rot,
+    value_rows,
+    position_col,
+    position_row,
+    cosine,
+    sine,
+    heads_gain,
+    attn_out,
+):
+    rows, width = branch.shape
+    cols = 2 * (heads + kv_heads) * HEAD_SIZE
+    seq_len = position_row.shape[-1]
+    shape = jax.ShapeDtypeStruct
+    outs = (
+        shape((owners, rows, width), BF16),
+        shape((rows, width), BF16),
+        shape((owners, rows, cols), BF16),
+        shape((1, 2 * HEAD_SIZE), F32),
+        shape(w_out.shape, F32),
+    )
+    return pl.pallas_call(
+        functools.partial(backward_kernel, owners, reps, heads, kv_heads),
+        out_shape=outs,
+        in_specs=[anywhere()] + [vmem()] * 16,
+        out_specs=(anywhere(),) + (vmem(),) * 4,
+        scratch_shapes=[
+            pltpu.VMEM((rows, width), BF16),
+            pltpu.VMEM((GROUP_SEQUENCES, kv_heads, seq_len, HEAD_SIZE), F32),
+            pltpu.VMEM((GROUP_SEQUENCES, kv_heads, seq_len, HEAD_SIZE), F32),
+            pltpu.SemaphoreType.DMA,
+            pltpu.SemaphoreType.DMA,
+        ]
+        + Scatter.scratch(owners, rows, width, PARTS)
+        + Gather.scratch(owners),
+        compiler_params=pltpu.CompilerParams(
+            collective_id=3, has_side_effects=True, vmem_limit_bytes=60 * 2**20
+        ),
+        cost_estimate=pl.CostEstimate(
+            flops=4 * owners * rows * width * cols,
+            bytes_accessed=40 * 2**20,
+            transcendentals=0,
+        ),
+        name="backward",
+    )(
+        branch,
+        activated,
+        w_down,
+        w_out,
+        hidden,
+        query_raw,
+        query_rot,
+        gate_raw,
+        key_raw,
+        key_rot,
+        value_rows,
+        position_col,
+        position_row,
+        cosine,
+        sine,
+        heads_gain,
+        attn_out,
+    )
+
+
+def column_loads(source_ref, buf, sem, shard):
+    def load(slot, u):
+        columns = pl.ds(pl.multiple_of(u * shard, shard), shard)
+        return pltpu.make_async_copy(source_ref.at[:, :, columns], buf.at[slot], sem.at[slot])
+
+    return load
+
+
+def columns_term(total, load, buf, grads):
+    def term(t, u):
+        @pl.when(t + 1 < total.units)
+        def _():
+            load((t + 1) % 2, total.unit(t + 1)).start()
+
+        load(t % 2, u).wait()
+        entry = buf[t % 2]
+        return dot_tn(entry.reshape(-1, entry.shape[-1]), grads())
+
+    return term
+
+
+def last_kernel(
+    owners,
+    reps,
+    grads_ref,
+    weight_ref,
+    tokens_ref,
+    grad_hidden_ref,
+    gain_ref,
+    out_term_ref,
+    gain_mlp_ref,
+    gain_heads_ref,
+    entry_ref,
+    grad_out,
+    gains_out,
+    weight_out,
+    out_weight_out,
+    entry_buf,
+    gains_send,
+    gains_came,
+    gains_all,
+    load_sem,
+    g_send,
+    g_recv,
+    r_send,
+    r_recv,
+    *rest,
+):
+    me, rep = lax.axis_index("grp"), lax.axis_index("rep")
+    chips = owners // 2
+    scatter = Scatter(owners, rest[:4], rest[4:8], by_distance, PARTS)
+    columns = RepSum(owners, reps, owners, True, rest[8], rest[9], weight_out, rest[10:16])
+    rows = RepSum(owners, reps, 1, False, rest[16], rest[17], out_weight_out, rest[18:24])
+    shard = entry_buf.shape[-1]
+    load = column_loads(entry_ref, entry_buf, load_sem, shard)
+    load(0, me).start()
+    meet(owners, reps)
+
+    def flat(ref):
+        return ref[...].reshape(-1, ref.shape[-1])
+
+    columns_of = columns_term(columns, load, entry_buf, lambda: flat(grads_ref))
+
+    def rows_of(t, u):
+        return out_term_ref[...]
+
+    def tick(t):
+        rows.tick(t, rows_of)
+        columns.tick(t, columns_of)
+
+    def term(at):
+        both = grads_ref[pl.ds(2 * at, 2)]
+        return dot_nt(both.reshape(-1, both.shape[-1]), weight_ref[...])
+
+    def stage(k, _):
+        scatter.prepare(k, term)
+        tick(TICKS * k)
+        scatter.combine(k)
+
+        def one(t, _):
+            tick(t)
+            return 0
+
+        lax.fori_loop(TICKS * k + 1, TICKS * (k + 1), one, 0)
+        return 0
+
+    lax.fori_loop(0, chips, stage, 0)
+    grad = scatter.acc[...]
+    normed, scale = head_norm(tokens_ref[...].astype(F32))
+    gain_attn = jnp.sum(grad * normed, axis=0, keepdims=True)
+    gain_mlp = gain_mlp_ref[...]
+    for e in range(owners):
+        span = slice(e * shard, (e + 1) * shard)
+        gains_send[e] = jnp.concatenate(
+            [gain_attn[:, span], gain_mlp[:, span], gain_heads_ref[...]], axis=1
+        )
+
+    def gains_copy(ahead):
+        device = lax.rem(me + ahead, owners)
+        return to_grp(
+            gains_send.at[device],
+            gains_came.at[me],
+            g_send.at[ahead],
+            g_recv.at[me],
+            device,
+        )
+
+    def gains_up(ahead):
+        return to_rep(
+            gains_all.at[rep],
+            gains_all.at[rep],
+            r_send.at[ahead],
+            r_recv.at[rep],
+            lax.rem(rep + ahead, reps),
+        )
+
+    for ahead in range(1, owners):
+        gains_copy(ahead).start()
+    gains_came[me] = gains_send[me]
+    weighted = grad * gain_ref[...]
+    grad_out[...] = (
+        grad_hidden_ref[...]
+        + scale * (weighted - normed * jnp.mean(weighted * normed, axis=-1, keepdims=True))
+    ).astype(BF16)
+    for ahead in range(1, owners):
+        source = lax.rem(me + ahead, owners)
+        arrived(gains_came.at[source], g_recv.at[source])
+    gains_all[rep] = jnp.sum(gains_came[...], axis=0)
+    for ahead in range(1, reps):
+        gains_up(ahead).start()
+
+    def one(t, _):
+        tick(t)
+        return 0
+
+    lax.fori_loop(TICKS * chips, max(columns.ticks(), rows.ticks()), one, 0)
+    for ahead in range(1, reps):
+        source = lax.rem(rep + ahead, reps)
+        arrived(gains_all.at[source], r_recv.at[source])
+    gains_out[...] = jnp.sum(gains_all[...], axis=0)
+    for ahead in range(1, owners):
+        gains_copy(ahead).wait_send()
+    for ahead in range(1, reps):
+        gains_up(ahead).wait_send()
+    scatter.finish()
+    columns.finish()
+    rows.finish()
+
+
+TICKS = 3
+
+
+def last(
+    owners,
+    reps,
+    grads,
+    weight,
+    tokens,
+    grad_hidden,
+    gain,
+    out_term,
+    gain_mlp,
+    gain_heads,
+    entry_all,
+):
+    rows, width = tokens.shape
+    cols = grads.shape[2]
+    shard = width // owners
+    share = shard // reps
+    small = 2 * shard + gain_heads.shape[1]
+    shape = jax.ShapeDtypeStruct
+    dma = pltpu.SemaphoreType.DMA
+    return pl.pallas_call(
+        functools.partial(last_kernel, owners, reps),
+        out_shape=(
+            shape((rows, width), BF16),
+            shape((1, small), F32),
+            shape((owners, reps, share, cols), BF16),
+            shape((1, reps, share, width), BF16),
+        ),
+        in_specs=[vmem()] * 8 + [anywhere()],
+        out_specs=(vmem(),) * 2 + (anywhere(),) * 2,
+        scratch_shapes=[
+            pltpu.VMEM((2, owners, rows, shard), BF16),
+            pltpu.VMEM((owners, 1, small), F32),
+            pltpu.VMEM((owners, 1, small), F32),
+            pltpu.VMEM((reps, 1, small), F32),
+            dma((2,)),
+            dma((owners,)),
+            dma((owners,)),
+            dma((reps,)),
+            dma((reps,)),
+        ]
+        + Scatter.scratch(owners, rows, width, PARTS)
+        + RepSum.scratch(reps, owners, share, cols)
+        + RepSum.scratch(reps, 1, share, width),
+        compiler_params=pltpu.CompilerParams(
+            collective_id=4, has_side_effects=True, vmem_limit_bytes=60 * 2**20
+        ),
+        cost_estimate=pl.CostEstimate(
+            flops=4 * owners * rows * width * cols,
+            bytes_accessed=40 * 2**20,
+            transcendentals=0,
+        ),
+        name="last",
+    )(
+        grads,
+        weight,
+        tokens,
+        grad_hidden,
+        gain,
+        out_term,
+        gain_mlp,
+        gain_heads,
+        entry_all,
+    )
+
+
 def positions_of(block_ids):
     offsets = jnp.arange(BLOCK_TOKENS, dtype=jnp.int32)
     return (block_ids[:, :, None] * BLOCK_TOKENS + offsets[None, None, :]).reshape(
         block_ids.shape[0], -1
     )
-
-
-def to_columns(piece):
-    reps = lax.axis_size("rep")
-    rows, owners, columns = piece.shape
-    share = rows // reps
-    mine = lax.dynamic_slice_in_dim(piece, lax.axis_index("rep") * share, share, 0)
-    swapped = lax.all_to_all(mine, "grp", 1, 0, tiled=True)
-    swapped = swapped.reshape(owners, share, columns)
-    whole = lax.all_gather(swapped, "rep", axis=1, tiled=True)
-    return whole.reshape(owners * rows, columns)
 
 
 def to_rows(gradient):
@@ -512,9 +1598,8 @@
     all_kv = KEY_VALUE_HEADS * HEAD_SIZE
     hidden_units = w_down.shape[0]
 
-    in_pieces = jnp.swapaxes(w_in.reshape(shard, 2, owners, hidden_units), 1, 2).reshape(
-        shard, owners, 2 * hidden_units
-    )
+    in_pieces = w_in.reshape(shard, 2, owners, hidden_units).transpose(2, 0, 1, 3)
+    in_pieces = in_pieces.reshape(owners, shard, 2 * hidden_units)
     reps = lax.axis_size("rep")
     head_part = norm_query.shape[0]
     spread = jnp.zeros((2, HEAD_SIZE), jnp.float32)
@@ -524,8 +1609,6 @@
     small = jnp.concatenate(
         [norm_attn.astype(jnp.float32), norm_mlp.astype(jnp.float32), spread.reshape(-1)]
     )[None]
-    in_cols = to_columns(in_pieces)
-    cotangent_all = lax.all_gather(cotangent, "grp", axis=0, tiled=True)
 
     positions = positions_of(block_map)
     cosine, sine = rotary_tables(positions)
@@ -535,6 +1618,8 @@
         shaped = table.reshape(GROUP_SEQUENCES, owners, block_rows, HEAD_SIZE)
         return jnp.swapaxes(shaped, 0, 1).reshape(owners, rows_here, HEAD_SIZE)
 
+    cosine = by_block(cosine)
+    sine = by_block(sine)
     (
         attn_input,
         query_raw,
@@ -554,150 +1639,86 @@
         tokens,
         w_qkvg,
         small,
-        by_block(cosine),
-        by_block(sine),
-    )
-    cosine = cosine[:, None]
-    sine = sine[:, None]
+        cosine,
+        sine,
+    )
     small_all = small_all[:, 0]
     gain_attn = small_all[:, :shard].reshape(-1)
     gain_mlp = small_all[:, shard : 2 * shard].reshape(-1)
     spread = jnp.sum(small_all[:, 2 * shard :], axis=0)
-    gain_query = spread[:HEAD_SIZE]
-    gain_key = spread[HEAD_SIZE:]
-    attn_input = attn_input.reshape(-1, width)
-    gate_raw = gate_raw.reshape(-1, q_cols)
-    qkvg_cols = qkvg_cols.reshape(width, -1)
-
-    def to_heads(values):
-        count = values.shape[-1] // HEAD_SIZE
-        shaped = values.reshape(owners, GROUP_SEQUENCES, block_rows, count, HEAD_SIZE)
-        return shaped.transpose(1, 3, 0, 2, 4).reshape(
-            GROUP_SEQUENCES, count, seq_len, HEAD_SIZE
-        )
-
-    def from_heads(values):
-        count = values.shape[1]
-        shaped = values.reshape(GROUP_SEQUENCES, count, owners, block_rows, HEAD_SIZE)
-        return shaped.transpose(2, 0, 3, 1, 4).reshape(-1, count * HEAD_SIZE)
-
-    query_heads = to_heads(query_raw)
-    key_heads = to_heads(key_raw)
-    value_heads = to_heads(value_rows)
-    query_scale = row_scale(query_heads)
-    query_normed = query_heads * query_scale
-    key_scale = row_scale(key_heads)
-    key_normed = key_heads * key_scale
-
-    query_rot = to_heads(query_rot).reshape(
-        GROUP_SEQUENCES, kv_heads, per_kv, seq_len, HEAD_SIZE
-    )
-    key_rot = to_heads(key_rot)
-    scores = jnp.einsum(
-        "shgqd,shkd->shgqk", query_rot, key_rot, preferred_element_type=jnp.float32
-    ) * HEAD_SIZE ** (-0.5)
-    allowed = (positions[:, None, :] <= positions[:, :, None])[:, None, None]
-    scores = jnp.where(allowed, scores, masked_value)
-    top_score = jnp.max(scores, axis=-1, keepdims=True)
-    exp_scores = jnp.exp(scores - top_score)
-    exp_total = jnp.sum(exp_scores, axis=-1, keepdims=True)
-    exact = exp_scores / exp_total
-    probability = exact.astype(jnp.bfloat16)
-    attended = jnp.einsum(
-        "shgqk,shkd->shgqd", probability, value_heads, preferred_element_type=jnp.float32
-    ).reshape(GROUP_SEQUENCES, heads, seq_len, HEAD_SIZE)
-    attended = from_heads(attended)
-    gate_sig = jax.nn.sigmoid(gate_raw)
-    attn_out = (attended * gate_sig).astype(jnp.bfloat16)
-
-    def scatter_sum(terms):
-        return lax.psum_scatter(
-            terms.astype(jnp.bfloat16), "grp", scatter_dimension=0, tiled=True
-        ).astype(jnp.float32)
-
-    branch = scatter_sum(jnp.dot(attn_out, w_out, preferred_element_type=jnp.float32))
-    hidden = tokens.astype(jnp.float32) + branch
-    scale_second = row_scale(hidden)
-    normed_second = hidden * scale_second
-    mlp_input = lax.all_gather(
-        (normed_second * gain_mlp).astype(jnp.bfloat16), "grp", axis=0, tiled=True
-    )
-    gate_up = jnp.dot(mlp_input, in_cols, preferred_element_type=jnp.float32)
-    gate_value = gate_up[:, :hidden_units]
-    up_value = gate_up[:, hidden_units:]
-    gate_sigmoid = jax.nn.sigmoid(gate_value)
-    activated = (gate_value * gate_sigmoid * up_value).astype(jnp.bfloat16)
-    grad_activated = jnp.dot(cotangent_all, w_down.T, preferred_element_type=jnp.float32)
-    grad_gate = (
-        grad_activated * up_value * gate_sigmoid * (1.0 + gate_value * (1.0 - gate_sigmoid))
-    ).astype(jnp.bfloat16)
-    grad_up = (grad_activated * gate_value * gate_sigmoid).astype(jnp.bfloat16)
-    grad_gate_up = jnp.concatenate([grad_gate, grad_up], axis=1)
-    grad_mlp_input = scatter_sum(
-        jnp.dot(grad_gate_up, in_cols.T, preferred_element_type=jnp.float32)
-    )
-    mlp_out = scatter_sum(jnp.dot(activated, w_down, preferred_element_type=jnp.float32))
-    output = (hidden + mlp_out).astype(jnp.bfloat16)
+    position_blocks = jnp.swapaxes(
+        positions.reshape(GROUP_SEQUENCES, owners, block_rows), 0, 1
+    ).reshape(owners, rows_here, 1)
+    attn_out, hidden, mlp_own, cotangent_all, in_cols = attention(
+        owners,
+        reps,
+        heads,
+        kv_heads,
+        tokens,
+        query_rot,
+        key_rot,
+        value_rows,
+        gate_raw,
+        position_blocks,
+        positions[:, None, :],
+        w_out,
+        gain_mlp[None],
+        cotangent,
+        in_pieces,
+    )
+    in_cols = in_cols.reshape(width, -1)
+    mlp_input, activated, grad_gate_up, grad_hidden, branch_own, gain_mlp_sum = mlp(
+        owners, reps, mlp_own, cotangent_all, in_cols, w_down, hidden, cotangent, gain_mlp[None]
+    )
+    mlp_input = mlp_input.reshape(-1, width)
+    grad_gate_up = grad_gate_up.reshape(-1, 2 * hidden_units)
+    cotangent_all = cotangent_all.reshape(-1, width)
+    _, output, grad_projected, gain_heads_sum, out_term = backward(
+        owners,
+        reps,
+        heads,
+        kv_heads,
+        branch_own,
+        activated.reshape(owners, rows_here, hidden_units),
+        w_down,
+        w_out,
+        hidden,
+        query_raw,
+        query_rot,
+        gate_raw,
+        key_raw,
+        key_rot,
+        value_rows,
+        position_blocks,
+        positions[:, None, :],
+        cosine,
+        sine,
+        spread[None],
+        attn_out,
+    )
+    grad_tokens, gains, rows_qkvg, rows_out = last(
+        owners,
+        reps,
+        grad_projected,
+        qkvg_cols.reshape(width, -1),
+        tokens,
+        grad_hidden,
+        gain_attn[None],
+        out_term,
+        gain_mlp_sum,
+        gain_heads_sum,
+        attn_input,
+    )
+    activated = activated.reshape(-1, hidden_units)
     term_in = jnp.dot(mlp_input.T, grad_gate_up, preferred_element_type=jnp.float32)
     term_down = jnp.dot(activated.T, cotangent_all, preferred_element_type=jnp.float32)
-    grad_hidden_norm, gain_rows_mlp = norm_back(
-        grad_mlp_input, normed_second, scale_second, gain_mlp
-    )
-    grad_hidden = cotangent.astype(jnp.float32) + grad_hidden_norm
-    grad_branch = lax.all_gather(
-        grad_hidden.astype(jnp.bfloat16), "grp", axis=0, tiled=True
-    )
     shard_down = sum_rep(term_down.astype(jnp.bfloat16)).astype(jnp.float32)
     rows_in = to_rows(term_in.astype(jnp.bfloat16)).astype(jnp.float32)
     shard_in = jnp.swapaxes(rows_in.reshape(shard, owners, 2, hidden_units), 1, 2).reshape(
         w_in.shape
     )
-    grad_attn_out = jnp.dot(grad_branch, w_out.T, preferred_element_type=jnp.float32)
-    attended_gradient = (grad_attn_out * gate_sig).astype(jnp.bfloat16)
-    grad_gate_raw = (grad_attn_out * attended * gate_sig * (1.0 - gate_sig)).astype(jnp.bfloat16)
-    term_out = jnp.dot(attn_out.T, grad_branch, preferred_element_type=jnp.float32)
-    shard_out = sum_rep(term_out.astype(jnp.bfloat16)).astype(jnp.float32)
-    head_gradient = to_heads(attended_gradient).reshape(query_rot.shape)
-    grad_value = jnp.einsum(
-        "shgqk,shgqd->shkd", probability, head_gradient, preferred_element_type=jnp.float32
-    )
-    grad_probs = jnp.einsum(
-        "shgqd,shkd->shgqk", head_gradient, value_heads, preferred_element_type=jnp.float32
-    )
-    inner_sum = jnp.sum(exact * grad_probs, axis=-1, keepdims=True)
-    grad_scores = (exact * (grad_probs - inner_sum)).astype(jnp.bfloat16)
-    grad_query = jnp.einsum(
-        "shgqk,shkd->shgqd", grad_scores, key_rot, preferred_element_type=jnp.float32
-    ).reshape(query_heads.shape) * HEAD_SIZE ** (-0.5)
-    grad_key = jnp.einsum(
-        "shgqk,shgqd->shkd", grad_scores, query_rot, preferred_element_type=jnp.float32
-    ) * HEAD_SIZE ** (-0.5)
-    grad_query_raw, gain_rows_query = norm_back(
-        unrotate_pairs(grad_query, cosine, sine), query_normed, query_scale, gain_query
-    )
-    grad_key_raw, gain_rows_key = norm_back(
-        unrotate_pairs(grad_key, cosine, sine), key_normed, key_scale, gain_key
-    )
-    grad_projected = jnp.concatenate(
-        [
-            from_heads(grad_query_raw.astype(jnp.bfloat16)),
-            grad_gate_raw,
-            from_heads(grad_key_raw.astype(jnp.bfloat16)),
-            from_heads(grad_value.astype(jnp.bfloat16)),
-        ],
-        axis=-1,
-    )
-    term_qkvg = jnp.dot(attn_input.T, grad_projected, preferred_element_type=jnp.float32)
-    grad_attn_input = scatter_sum(
-        jnp.dot(grad_projected, qkvg_cols.T, preferred_element_type=jnp.float32)
-    )
-    own_tokens = tokens.astype(jnp.float32)
-    own_scale = row_scale(own_tokens)
-    grad_residual_norm, gain_rows_attn = norm_back(
-        grad_attn_input, own_tokens * own_scale, own_scale, gain_attn
-    )
-    grad_tokens = (grad_hidden + grad_residual_norm).astype(jnp.bfloat16)
-    rows_qkvg = to_rows(term_qkvg.astype(jnp.bfloat16)).astype(jnp.float32)
+    shard_out = rows_out.reshape(w_out.shape).astype(jnp.float32)
+    rows_qkvg = rows_qkvg.reshape(owners, shard, -1).swapaxes(0, 1).astype(jnp.float32)
 
     def joined(part, repeat):
         if repeat > 1:
@@ -713,17 +1734,6 @@
         ],
         axis=1,
     )
-    gains = lax.psum(
-        jnp.concatenate(
-            [
-                jnp.sum(gain_rows_attn, axis=0),
-                jnp.sum(gain_rows_mlp, axis=0),
-                jnp.sum(gain_rows_query, axis=(0, 1, 2)),
-                jnp.sum(gain_rows_key, axis=(0, 1, 2)),
-            ]
-        ),
-        ("rep", "grp"),
-    )
     return (
         output,
         grad_tokens,
@@ -731,10 +1741,10 @@
         shard_out,
         shard_in,
         shard_down,
-        lax.dynamic_slice_in_dim(gains, me * shard, shard),
-        lax.dynamic_slice_in_dim(gains, 2 * width + me * head_part, head_part),
-        lax.dynamic_slice_in_dim(gains, 2 * width + HEAD_SIZE + me * head_part, head_part),
-        lax.dynamic_slice_in_dim(gains, width + me * shard, shard),
+        gains[0, :shard],
+        lax.dynamic_slice_in_dim(gains[0], 2 * shard + me * head_part, head_part),
+        lax.dynamic_slice_in_dim(gains[0], 2 * shard + HEAD_SIZE + me * head_part, head_part),
+        gains[0, shard : 2 * shard],
     )
 
 

time: 1190 us -> 1040 us (0.87)
  Pallas kernels: 104 us -> 743 us
  waiting for transfers between devices: 403 us -> 94.3 us
  matrix products: 196 us -> 29.5 us
  blocking collectives: 173 us -> 42.4 us
  local copies, waits for them, and re-layouts: 182 us -> 79.2 us
  other arithmetic: 98.8 us -> 30.4 us
    pallas_call x0 -> x4, Pallas kernels: none -> 639 us  [the longest x1 209 us: mlp(): pl.pallas_call(functools.partial(mlp_kernel, owners, reps), out_shape=out...]
    all_gather x4 -> x0, waiting for transfers between devices: 205 us -> none  [the longest x1 84 us: body(): lax.all_gather((normed_second * gain_mlp).astype(jnp.bfloat16), 'grp', ax...]
    dot_general x14 -> x0, matrix products: 154 us -> none  [the longest x1 19.5 us: body(): gate_up = jnp.dot(mlp_input, in_cols, preferred_element_type=jnp.float32)]
    reduce_scatter x4 -> x0, waiting for transfers between devices: 113 us -> none  [scatter_sum(): lax.psum_scatter(terms.astype(jnp.bfloat16), 'grp', scatter_dimension=0,...]
    all_gather x2 -> x1, waiting for transfers between devices: 84.4 us -> 0.01 us  [to_rows(): lax.all_gather(jnp.swapaxes(swapped, 0, 1), 'rep', axis=0, tiled=True)]
    reduce_scatter x2 -> x1, waiting for transfers between devices: 0.04 us -> 73.7 us  [to_rows(): share = lax.psum_scatter(shaped, 'rep', scatter_dimension=0, tiled=True)]
    all_to_all x1 -> x0, blocking collectives: 67.1 us -> none  [to_columns(): swapped = lax.all_to_all(mine, 'grp', 1, 0, tiled=True)]
    psum x1 -> x0, blocking collectives: 39.8 us -> none  [body(): lax.psum(jnp.concatenate([jnp.sum(gain_rows_attn, axis=0), jnp.sum(gain_r...]
  transfers between devices with their start and end apart: 16 -> 4, of which waited for: 8 -> 2; matrix products, arithmetic and copies ran while one was open for 30% -> 4% of each run, Pallas kernels for 0% -> 28%
where the time goes in v3:
time: 1040 us; the launch traced here: 1030 us
  Pallas kernels  743 us (71%)
  waiting for transfers between devices  94.3 us (9%)
  local copies, waits for them, and re-layouts  79.2 us (8%)
  blocking collectives  42.4 us (4%)
  other arithmetic  30.4 us (3%)
  matrix products  29.5 us (3%)
  between operations  14.4 us (1%)
    pallas_call x1, Pallas kernels, mlp(): pl.pallas_call(functools.partial(mlp_kernel, owners, reps), out_shape=out...  209 us
    pallas_call x1, Pallas kernels, backward(): pl.pallas_call(functools.partial(backward_kernel, owners, reps, heads, kv...  147 us
    pallas_call x1, Pallas kernels, last(): pl.pallas_call(functools.partial(last_kernel, owners, reps), out_shape=(s...  146 us
    pallas_call x1, Pallas kernels, attention(): pl.pallas_call(functools.partial(attention_kernel, owners, reps, heads, k...  137 us
    pallas_call x1, Pallas kernels, first(): pl.pallas_call(functools.partial(first_kernel, owners, reps, heads, kv_he...  104 us
    reduce_scatter x1, waiting for transfers between devices, to_rows(): share = lax.psum_scatter(shaped, 'rep', scatter_dimension=0, tiled=True)  73.7 us
    all_to_all x1, blocking collectives, to_rows(): swapped = lax.all_to_all(share, 'grp', 0, 0, tiled=True)  42.4 us
    unnamed x20, local copies, waits for them, and re-layouts  27.4 us
  transfers between devices with their start and end apart: 4, of which 2 were waited for; matrix products, arithmetic and copies ran while one was open for 4% of the time, Pallas kernels for 28%

profile of v3, /device:TPU:0, one launch (start us, length us, event | category | flops | bytes accessed | tf_op | source)
XLA Modules:
  0.0 1033.4 jit_solution(12337678711452875157)
XLA Ops:
  7.2 0.0 reduce-scatter.5.cloned.1.call-start
  7.3 0.7 broadcast_multiply_fusion.1
  7.9 0.1 add.69
  8.0 0.1 add.79
  8.1 0.1 add.70
  8.2 0.7 convert_element_type.42
  8.8 0.7 convert_element_type.43
  9.5 0.7 maximum_convert_fusion
  10.2 0.1 dynamic_update_slice.3
  10.3 0.6 broadcast_in_dim.23.small_ref
  10.9 0.1 add.76
  11.0 0.1 add.81
  11.1 0.1 add.72
  11.2 1.3 copy.55.position_col_ref
  12.5 6.9 copy.81
  19.4 14.4 %reshape.190.in_pieces_ref = bf16[8,256,1536]{2,1,0:T(8,128)(2,1)} reshape(bf16[8,256,2,768]{3,2,1,0:T(2,128)(2,1)} %bitcast.88) | data formatting | bytes 12582912 | tf_op jit(solution)/shard_map/reshape | solution.py:1602
  33.8 0.3 broadcast_multiply_fusion
  34.1 4.9 sine_multiply_fusion
  39.0 104.3 %first.1 = (bf16[8,256,2048]{2,1,0:T(8,128)(2,1)}, f32[8,256,256]{2,1,0:T(8,128)}, f32[8,256,256]{2,1,0:T(8,128)}, f32[8,256,128]{2,1,0:T(8,128)}, bf16[8,256,12...) custom-call(bf16[256,2048]{1,0:T(8,128)(2,1)} %tokens_ref.5, ...), custom_call_target="tpu_custom_call" | custom-call | flops 6442450944 | bytes 41943040 | tf_op jit(solution)/shard_map/first/pallas_call | solution.py:435
  143.3 0.7 copy.82
  144.0 0.6 slice_bitcast_fusion.4
  144.6 0.6 copy.75
  145.2 0.6 broadcast_add_fusion.position_row_ref
  145.8 136.9 %attention.1 = (bf16[8,256,256]{2,1,0:T(8,128)(2,1)}, f32[256,2048]{1,0:T(8,128)}, bf16[256,2048]{1,0:T(8,128)(2,1)}, bf16[8,256,2048]{2,1,0:T(8,128)(2,1)}, bf16[8,4,64,1536]{3,2,1,0:T(8,128)(2,1)}) custom-call(bf16[256,2048]{1,0:T(8,128)(2,1)} %tokens_ref.5, bf16[8,256,256]{2,1,0:T(8,128)(2,1)} %get-tuple-element.38.query_ref.query_rot_ref, ...), custom_call_target="tpu_custom_call" | custom-call | flops 4294967296 | bytes 41943040 | tf_op jit(solution)/shard_map/attention/pallas_call | solution.py:876
  282.8 208.6 %mlp.1 = (bf16[8,2,128,2048]{3,2,1,0:T(8,128)(2,1)}, bf16[8,2,128,768]{3,2,1,0:T(8,128)(2,1)}, bf16[8,2,128,1536]{3,2,1,0:T(8,128)(2,1)}, f32[256,2048]{1,0:T(8,...) custom-call(bf16[2,128,2048]{2,1,0:T(8,128)(2,1)} %bitcast.116, bf16[8,2,128,2048]{3,2,1,0:T(8,128)(2,1)} %bitcast.110, ...), custom_call_target="tpu_custom_call" | custom-call | flops 32212254720 | bytes 41943040 | tf_op jit(solution)/shard_map/mlp/pallas_call | solution.py:1050
  491.4 12.0 %convolution_convert_fusion = bf16[768,2048]{1,0:T(8,128)(2,1)} fusion(bf16[2048,768]{1,0:T(8,128)(2,1)} %bitcast.114, bf16[2048,2048]{1,0:T(8,128)(2,1)} %bitcast.111), kind=kOutput, calls=%fused_computation.5 | convolution fusion | flops 6444023808 | bytes 14680064 | tf_op jit(solution)/shard_map/dot_general | solution.py:1714
  503.4 0.0 reduce-scatter.5.cloned.1.call-update
  503.4 0.0 reduce-scatter.3.cloned.1.call-start
  503.4 17.5 %bitcast_convert_fusion = bf16[2048,1536]{1,0:T(8,128)(2,1)S(1)} fusion(bf16[8,2,128,2048]{3,2,1,0:T(8,128)(2,1)} %get-tuple-element.63, bf16[8,2,128,1536]{3,2,1,0:T(8,128)(2,1)} %get-tuple-element.64), kind=kOutput, calls=%fused_computation.1 | convolution fusion | flops 12888047616 | bytes 20971520 | tf_op jit(solution)/shard_map/dot_general | solution.py:1713
  521.0 3.4 copy.62
  524.4 0.0 reduce-scatter.3.cloned.1.call-update
  524.4 0.0 all-gather.5.cloned.1.call-start
  524.5 20.5 %reduce-scatter.5.cloned.1.call-done = bf16[192,2048]{1,0:T(8,128)(2,1)} async-done(((bf16[768,2048]{1,0:T(8,128)(2,1)}), bf16[192,2048]{1,0:T(8,128)(2,1)}) %reduce-scatter.5.cloned.1.call-update) | async-done | bytes 786448 | tf_op jit(solution)/shard_map/reduce_scatter | solution.py:1568
  545.0 0.0 all-gather.5.cloned.1.call-update
  545.0 0.0 all-gather.3.cloned.1.call-start
  545.0 73.7 %reduce-scatter.3.cloned.1.call-done = bf16[512,1536]{1,0:T(8,128)(2,1)} async-done(((bf16[2048,1536]{1,0:T(8,128)(2,1)}), bf16[512,1536]{1,0:T(8,128)(2,1)}) %reduce-scatter.3.cloned.1.call-update) | async-done | bytes 1572880 | tf_op jit(solution)/shard_map/reduce_scatter | solution.py:1561
  618.7 42.4 %all_to_all.5 = bf16[8,64,1536]{2,1,0:T(8,128)(2,1)S(1)} all-to-all(bf16[8,64,1536]{2,1,0:T(8,128)(2,1)} %bitcast.95), channel_id=1, replica_groups=mesh['rep'=4,'grp'=8] {'grp'}, dimensions={0} | all-to-all | bytes 3145728 | tf_op jit(solution)/shard_map/all_to_all | solution.py:1563
  661.2 2.0 copy.63
  663.2 0.0 all-gather.3.cloned.1.call-update
  663.2 0.6 copy.76
  663.8 147.2 %backward.1 = (bf16[8,256,2048]{2,1,0:T(8,128)(2,1)}, bf16[256,2048]{1,0:T(8,128)(2,1)}, bf16[8,256,768]{2,1,0:T(8,128)(2,1)}, f32[1,256]{1,0:T(1,128)}, f32[256,2048]{1,0:T(8,128)}) custom-call(bf16[256,2048]{1,0:T(8,128)(2,1)} %get-tuple-element.47.branch_ref, bf16[8,256,768]{2,1,0:T(8,128)(2,1)} %bitcast.115, bf16[768,2048]{1,0:T(8,128)(2,1)} %down_ref.3, ...), custom_call_target="tpu_custom_call" | custom-call | flops 12884901888 | bytes 41943040 | tf_op jit(solution)/shard_map/backward/pallas_call | solution.py:1286
  811.0 145.9 %last.1 = (bf16[256,2048]{1,0:T(8,128)(2,1)}, f32[1,768]{1,0:T(1,128)}, bf16[8,4,64,768]{3,2,1,0:T(8,128)(2,1)}, bf16[1,4,64,2048]{3,2,1,0:T(8,128)(2,1)}) custom-call(bf16[8,256,768]{2,1,0:T(8,128)(2,1)} %get-tuple-element.53.grads_ref, bf16[2048,768]{1,0:T(8,128)(2,1)} %bitcast.113, bf16[256,2048]{1,0:T(8,128)(2,1)} %tokens_ref.5, ...), custom_call_target="tpu_custom_call" | custom-call | flops 12884901888 | bytes 41943040 | tf_op jit(solution)/shard_map/last/pallas_call | solution.py:1502
  957.0 2.4 convert_bitcast_fusion.1
  959.4 0.0 copy-start
  959.5 0.5 slice_bitcast_fusion.1
  960.0 0.0 copy-start.5
  960.0 0.3 copy.71
  960.3 1.9 copy-done
  962.2 1.6 copy.72
  963.8 0.0 copy-done.5
  963.8 0.6 dynamic-slice_bitcast_fusion
  964.3 0.6 fusion.1
  964.9 1.7 slice_bitcast_fusion.3
  966.6 0.3 copy_bitcast_fusion
  966.9 0.0 copy-done.2
  966.9 1.6 bitcast_convert_fusion.1
  968.5 2.9 pad_maximum_fusion
  971.5 5.4 convert_element_type.53
  976.9 9.0 copy.64
  985.9 8.9 convert_bitcast_fusion
  994.8 10.2 copy.65
  1005.1 19.4 %copy.66 = f32[256,2,6144]{2,1,0:T(2,128)} copy(f32[256,2,6144]{0,2,1:T(8,128)} %bitcast.86) | data formatting | bytes 25165824
  1024.5 1.0 copy.86
  1025.5 1.0 copy.87
  (18 shorter events, 0.1 us)
Async XLA Ops:
  7.2 537.8 %reduce-scatter.5.cloned.1.call-start = ((), (), s32[]{:S(2)}) async-start(), calls=%async_computation.5 | async-start | bytes 3932160 | tf_op jit(solution)/shard_map/reduce_scatter | solution.py:1568
  503.4 115.3 %reduce-scatter.3.cloned.1.call-start = ((), (), s32[]{:S(2)}) async-start(), calls=%async_computation.3 | async-start | bytes 7864320 | tf_op jit(solution)/shard_map/reduce_scatter | solution.py:1561
  524.4 447.1 %all-gather.5.cloned.1.call-start = ((), (), s32[]{:S(2)}) async-start(), calls=%async_computation.6 | async-start | bytes 3932160 | tf_op jit(solution)/shard_map/all_gather | solution.py:1569
  545.0 431.9 %all-gather.3.cloned.1.call-start = ((), (), s32[]{:S(2)}) async-start(), calls=%async_computation.4 | async-start | bytes 7864320 | tf_op jit(solution)/shard_map/all_gather | solution.py:1564
  959.4 2.7 copy-start
  960.0 3.8 copy-start.5
  962.1 4.7 copy-start.2
  963.8 4.8 copy-start.1
  1005.1 19.4 %copy-start.3 = (bf16[256,2048]{1,0:T(8,128)(2,1)S(1)}, bf16[256,2048]{1,0:T(8,128)(2,1)}, u32[]{:S(2)}) copy-start(bf16[256,2048]{1,0:T(8,128)(2,1)} %get-tuple-element.113) | copy-start | bytes 3145732
  1005.1 20.4 %copy-start.4 = (bf16[256,2048]{1,0:T(8,128)(2,1)S(1)}, bf16[256,2048]{1,0:T(8,128)(2,1)}, u32[]{:S(2)}) copy-start(bf16[256,2048]{1,0:T(8,128)(2,1)} %get-tuple-element.114) | copy-start | bytes 3145732
Sparse Core Ops, SparseCore 0:
  503.5 41.4 reduce-scatter.4
  548.5 70.1 reduce-scatter.2
  620.6 43.9 all-gather.4
  666.9 70.1 all-gather.2

commit v4 on v3

--- a/solution.py
+++ b/solution.py
@@ -19,31 +19,11 @@
 masked_value = -1e30
 
 
-def row_scale(values):
-    return lax.rsqrt(jnp.mean(values * values, axis=-1, keepdims=True) + norm_epsilon)
-
-
-def rotate_half(values):
-    middle = values.shape[-1] // 2
-    return jnp.concatenate([-values[..., middle:], values[..., :middle]], axis=-1)
-
-
-def rotary_tables(positions):
+def rotary_table(positions):
     exponent = jnp.arange(HEAD_SIZE // 2, dtype=jnp.float32) * (2.0 / HEAD_SIZE)
     inverse = jnp.power(jnp.float32(rotary_base), -exponent)
-    angles = positions.astype(jnp.float32)[..., None] * inverse
-    angles = jnp.concatenate([angles, angles], axis=-1)
-    return (jnp.cos(angles), jnp.sin(angles))
-
-
-def unrotate_pairs(gradient, cosine_lookup, sine_lookup):
-    return gradient * cosine_lookup - jnp.roll(gradient, HEAD_SIZE // 2, -1) * sine_lookup
-
-
-def norm_back(grad_out, normed, scale_rows, gain_vector):
-    weighted = grad_out * gain_vector
-    grad_in = scale_rows * (weighted - normed * jnp.mean(weighted * normed, axis=-1, keepdims=True))
-    return (grad_in, grad_out * normed)
+    angle = positions.astype(jnp.float32)[..., None] * inverse
+    return jnp.concatenate([jnp.cos(angle), jnp.sin(angle)], axis=-1)
 
 
 MESH = pl.DeviceIdType.MESH
@@ -248,6 +228,21 @@
         ]
 
 
+def query_positions(map_ref, s, at):
+    row = lax.broadcasted_iota(jnp.int32, (2 * BLOCK_TOKENS, 1), 0)
+    return row + jnp.where(
+        row < BLOCK_TOKENS,
+        map_ref[s, 2 * at] * BLOCK_TOKENS,
+        (map_ref[s, 2 * at + 1] - 1) * BLOCK_TOKENS,
+    )
+
+
+def angles(table):
+    turned = pltpu.roll(table, HEAD_SIZE // 2, 1)
+    low = lax.broadcasted_iota(jnp.int32, table.shape, 1) < HEAD_SIZE // 2
+    return jnp.where(low, table, turned), jnp.where(low, -turned, table)
+
+
 def head_norm(values):
     scale = lax.rsqrt(jnp.mean(values * values, axis=-1, keepdims=True) + norm_epsilon)
     return values * scale, scale
@@ -270,8 +265,7 @@
     tokens_ref,
     weight_ref,
     small_ref,
-    cosine_ref,
-    sine_ref,
+    table_ref,
     input_out,
     query_out,
     gate_out,
@@ -376,7 +370,7 @@
             entry = (normed * gain).astype(BF16)
             input_out[at] = entry
             projected = dot(entry, weight[...])
-            cosine, sine = cosine_ref[at], sine_ref[at]
+            cosine, sine = angles(table_ref[at])
             for h in range(heads):
                 span = slice(h * HEAD_SIZE, (h + 1) * HEAD_SIZE)
                 raw = projected[:, span]
@@ -410,11 +404,15 @@
     return pl.BlockSpec(memory_space=pltpu.VMEM)
 
 
+def smem():
+    return pl.BlockSpec(memory_space=pltpu.SMEM)
+
+
 def anywhere():
     return pl.BlockSpec(memory_space=pl.ANY)
 
 
-def first(owners, reps, heads, kv_heads, sharers, tokens, w_qkvg, small, cosine, sine):
+def first(owners, reps, heads, kv_heads, sharers, tokens, w_qkvg, small, table):
     rows, width = tokens.shape
     shard = w_qkvg.shape[0]
     q_cols, kv_cols = heads * HEAD_SIZE, kv_heads * HEAD_SIZE
@@ -435,7 +433,7 @@
     return pl.pallas_call(
         functools.partial(first_kernel, owners, reps, heads, kv_heads, sharers),
         out_shape=outs,
-        in_specs=[anywhere(), anywhere(), vmem(), vmem(), vmem()],
+        in_specs=[anywhere(), anywhere(), vmem(), vmem()],
         out_specs=(vmem(),) * 7 + (anywhere(), vmem()),
         scratch_shapes=[
             pltpu.VMEM((owners, rows, width), BF16),
@@ -454,7 +452,7 @@
             flops=flops, bytes_accessed=40 * 2**20, transcendentals=0
         ),
         name="first",
-    )(tokens, w_qkvg, small, cosine, sine)
+    )(tokens, w_qkvg, small, table)
 
 
 def by_distance(place, step, chips):
@@ -721,7 +719,7 @@
         ]
 
 
-def interleave(gather, scatter, term, ready=None, then=None):
+def interleave(gather, scatter, term, ready=None, then=None, fill=None):
     chips = gather.chips
     middle = (gather.place > 0) & (gather.place < chips - 1)
 
@@ -729,6 +727,8 @@
         if ready is not None:
             ready(k)
         scatter.prepare(k, term)
+        if fill is not None:
+            fill(k)
 
         @pl.when(middle & (2 * k + 1 < chips))
         def _():
@@ -760,7 +760,7 @@
     key_ref,
     value_ref,
     gate_ref,
-    position_col_ref,
+    map_ref,
     position_row_ref,
     out_ref,
     gain_ref,
@@ -778,12 +778,10 @@
     scatter = Scatter(owners, rest[:4], rest[4:8], by_distance, PARTS)
     gather = Gather(owners, cotangent_out, *rest[8:10])
     reshard = Reshard(owners, reps, columns_out, rest[10:14])
-    share = in_pieces_ref.shape[1] // reps
     cols = in_pieces_ref.shape[2]
-    my_rows = pl.ds(pl.multiple_of(rep * share, share), share)
 
     def pieces(owner):
-        return [(in_pieces_ref.at[owner, my_rows], pl.ds(0, cols))]
+        return [(in_pieces_ref.at[owner], pl.ds(0, cols))]
 
     own = pltpu.make_async_copy(cotangent_ref, cotangent_out.at[me], local_sem)
     own.start()
@@ -796,7 +794,7 @@
     def attend(at):
         for s in range(GROUP_SEQUENCES):
             rows = slice(s * block_rows, (s + 1) * block_rows)
-            allowed = position_row_ref[s] <= position_col_ref[at, rows]
+            allowed = position_row_ref[s] <= query_positions(map_ref, s, at)
             allowed = jnp.concatenate([allowed] * per_kv, axis=0)
             for kv in range(kv_heads):
                 span = slice(kv * HEAD_SIZE, (kv + 1) * HEAD_SIZE)
@@ -856,7 +854,7 @@
     key_rot,
     value_rows,
     gate_raw,
-    position_col,
+    block_map,
     position_row,
     w_out,
     gain_mlp,
@@ -865,7 +863,7 @@
 ):
     rows, width = tokens.shape
     shape = jax.ShapeDtypeStruct
-    share = in_pieces.shape[1] // reps
+    share = in_pieces.shape[1]
     outs = (
         shape(query_rot.shape, BF16),
         shape((rows, width), F32),
@@ -876,7 +874,7 @@
     return pl.pallas_call(
         functools.partial(attention_kernel, owners, reps, heads, kv_heads),
         out_shape=outs,
-        in_specs=[vmem()] * 9 + [anywhere()] * 2,
+        in_specs=[vmem()] * 5 + [smem()] + [vmem()] * 3 + [anywhere()] * 2,
         out_specs=(vmem(),) * 3 + (anywhere(),) * 2,
         scratch_shapes=[pltpu.SemaphoreType.DMA]
         + Scatter.scratch(owners, rows, width, PARTS)
@@ -897,7 +895,7 @@
         key_rot,
         value_rows,
         gate_raw,
-        position_col,
+        block_map,
         position_row,
         w_out,
         gain_mlp,
@@ -922,10 +920,11 @@
     grad_hidden_out,
     grad_branch_out,
     gain_out,
+    weight_out,
     entry_buf,
     cotangent_buf,
     activated_buf,
-    grad_entry_buf,
+    down_sum,
     local_sem,
     load_sem,
     store_sem,
@@ -933,88 +932,110 @@
 ):
     me = lax.axis_index("grp")
     chips = owners // 2
-    halves = GROUP_SEQUENCES
-    gathers = [Gather(owners, entry_all, *rest[8:10], half) for half in range(halves)]
-    scatters = [
-        Scatter(owners, rest[:4], rest[4:8], by_distance, HALF_PARTS, half)
-        for half in range(halves)
-    ]
+    gather = Gather(owners, entry_all, *rest[8:10])
+    scatter = Scatter(owners, rest[:4], rest[4:8], by_distance, PARTS)
+    shard = weight_out.shape[1] * weight_out.shape[2]
+    rows = RepSum(
+        owners, reps, down_ref.shape[0] // shard, False, rest[10], rest[11], weight_out, rest[12:18]
+    )
     units = down_ref.shape[0]
-    place = gathers[0].place
     own = pltpu.make_async_copy(entry_ref, entry_all.at[me], local_sem)
     own.start()
     meet(owners, reps)
-    gathers[0].forward(me, entry_ref.at[0])
+    gather.forward(me, entry_ref)
+    down_sum[...] = jnp.zeros_like(down_sum)
     own.wait()
 
-    def compute(k, half, first):
-        gather = gathers[half]
-        pair = pl.ds(2 * nearest(place, k, chips), 2)
-        cotangent_load = pltpu.make_async_copy(
-            cotangent_all_ref.at[pair, half], cotangent_buf, load_sem.at[1]
+    def block_of(k, which):
+        return 2 * nearest(gather.place, k, chips) + jnp.where(
+            which == 0, gather.core, 1 - gather.core
         )
-        cotangent_load.start()
-        gather.sibling(k)
-        entry_load = pltpu.make_async_copy(entry_all.at[pair, half], entry_buf, load_sem.at[0])
-        entry_load.start()
-        cotangent_load.wait()
-        both = cotangent_buf.shape[0] * cotangent_buf.shape[1]
-        grad_activated = dot_nt(cotangent_buf[...].reshape(both, -1), down_ref[...])
-        entry_load.wait()
-        gate_up = dot(entry_buf[...].reshape(both, -1), in_ref[...])
-        gate, up = gate_up[:, :units], gate_up[:, units:]
-        sig = jax.nn.sigmoid(gate)
-        silu = gate * sig
-        store = pltpu.make_async_copy(activated_buf, activated_out.at[pair, half], store_sem)
-
-        @pl.when(jnp.logical_not(first))
+
+    def store(which, at):
+        return pltpu.make_async_copy(
+            activated_buf.at[which], activated_out.at[at], store_sem.at[which]
+        )
+
+    def compute(k):
+        def one(which, _):
+            at = block_of(k, which)
+            cotangent_load = pltpu.make_async_copy(
+                cotangent_all_ref.at[at], cotangent_buf.at[which], load_sem.at[1, which]
+            )
+            cotangent_load.start()
+
+            @pl.when(which == 1)
+            def _():
+                gather.sibling(k)
+
+            entry_load = pltpu.make_async_copy(
+                entry_all.at[at], entry_buf.at[which], load_sem.at[0, which]
+            )
+            entry_load.start()
+            cotangent_load.wait()
+            grad_activated = dot_nt(cotangent_buf[which], down_ref[...])
+            entry_load.wait()
+            gate_up = dot(entry_buf[which], in_ref[...])
+            gate, up = gate_up[:, :units], gate_up[:, units:]
+            sig = jax.nn.sigmoid(gate)
+            silu = gate * sig
+
+            @pl.when(k > 0)
+            def _():
+                store(which, at).wait()
+
+            activated_buf[which] = (silu * up).astype(BF16)
+            store(which, at).start()
+            grads_out[at, :, :units] = (
+                grad_activated * up * sig * (1.0 + gate * (1.0 - sig))
+            ).astype(BF16)
+            grads_out[at, :, units:] = (grad_activated * silu).astype(BF16)
+            down_sum[...] += dot_tn(activated_buf[which], cotangent_buf[which])
+            return 0
+
+        lax.fori_loop(0, 2, one, 0)
+
+    def term(at):
+        both = grads_out[pl.ds(2 * at, 2)]
+        return dot_nt(both.reshape(-1, both.shape[-1]), in_ref[...])
+
+    def rows_of(t, u):
+        return down_sum[pl.ds(pl.multiple_of(u * shard, shard), shard)]
+
+    middle = (gather.place > 0) & (gather.place < chips - 1)
+    early = jnp.where(middle, chips, 1)
+
+    def step(k, _):
+        gather.step(k)
+        return 0
+
+    def front(k, _):
+        @pl.when(k >= early)
         def _():
-            store.wait()
-
-        activated_buf[...] = (silu * up).astype(BF16).reshape(activated_buf.shape)
-        store.start()
-        shape = activated_buf.shape
-        grads_out[pair, half, :, :units] = (
-            (grad_activated * up * sig * (1.0 + gate * (1.0 - sig))).astype(BF16).reshape(shape)
-        )
-        grads_out[pair, half, :, units:] = (grad_activated * silu).astype(BF16).reshape(shape)
-
-    def term_of(half):
-        def term(at):
-            both = grads_out[pl.ds(2 * at, 2), half]
-            return dot_nt(both.reshape(-1, both.shape[-1]), in_ref[...])
-
-        return term
-
-    def front(k, _):
-        @pl.when(k > 0)
-        def _():
-            gathers[0].step(k)
-
-        compute(k, 0, k == 0)
+            gather.step(k)
+
+        compute(k)
         return 0
 
+    lax.fori_loop(1, early, step, 0)
     lax.fori_loop(0, chips, front, 0)
-    for half in range(1, halves):
-        gathers[half].forward(me, entry_ref.at[half])
-        interleave(
-            gathers[half],
-            scatters[half - 1],
-            term_of(half - 1),
-            then=lambda k, half=half: compute(k, half, k < 0),
-        )
-        grad_entry_buf[half - 1] = scatters[half - 1].acc[...]
 
     def back(k, _):
-        scatters[-1].prepare(k, term_of(halves - 1))
-        scatters[-1].combine(k)
+        scatter.prepare(k, term)
+        rows.tick(TICKS * k, rows_of)
+        scatter.combine(k)
+
+        def one(t, _):
+            rows.tick(t, rows_of)
+            return 0
+
+        lax.fori_loop(TICKS * k + 1, TICKS * (k + 1), one, 0)
         return 0
 
     lax.fori_loop(0, chips, back, 0)
-    grad_entry_buf[halves - 1] = scatters[-1].acc[...]
     hidden = hidden_ref[...]
     normed, scale = head_norm(hidden)
-    grad_entry = grad_entry_buf[...].reshape(hidden.shape)
+    grad_entry = scatter.acc[...]
     gain_out[...] = jnp.sum(grad_entry * normed, axis=0, keepdims=True)
     weighted = grad_entry * gain_ref[...]
     grad_hidden = cotangent_ref[...].astype(F32) + scale * (
@@ -1022,65 +1043,61 @@
     )
     grad_hidden_out[...] = grad_hidden
     grad_branch_out[...] = grad_hidden.astype(BF16)
-    pltpu.make_async_copy(
-        activated_buf, activated_out.at[pl.ds(0, 2), 0], store_sem
-    ).wait()
-    for half in range(halves):
-        gathers[half].finish()
-        scatters[half].finish()
-
-
-HALF_PARTS = 2
+
+    def late(t, _):
+        rows.tick(t, rows_of)
+        return 0
+
+    lax.fori_loop(TICKS * chips, rows.ticks(), late, 0)
+    for which in range(2):
+        store(which, block_of(chips - 1, which)).wait()
+    gather.finish()
+    scatter.finish()
+    rows.finish()
 
 
 def mlp(owners, reps, entry, cotangent_all, in_cols, w_down, hidden, cotangent, gain_mlp):
     rows, width = entry.shape
     units = w_down.shape[0]
-    halves = GROUP_SEQUENCES
-    half_rows = rows // halves
+    shard = width // owners
+    share = shard // reps
     shape = jax.ShapeDtypeStruct
     outs = (
-        shape((owners, halves, half_rows, width), BF16),
-        shape((owners, halves, half_rows, units), BF16),
-        shape((owners, halves, half_rows, 2 * units), BF16),
+        shape((owners, rows, width), BF16),
+        shape((owners, rows, units), BF16),
+        shape((owners, rows, 2 * units), BF16),
         shape((rows, width), F32),
         shape((rows, width), BF16),
         shape((1, width), F32),
+        shape((units // shard, reps, share, width), BF16),
     )
     return pl.pallas_call(
         functools.partial(mlp_kernel, owners, reps),
         out_shape=outs,
         in_specs=[anywhere()] * 2 + [vmem()] * 5,
-        out_specs=(anywhere(),) * 2 + (vmem(),) * 4,
+        out_specs=(anywhere(),) * 2 + (vmem(),) * 4 + (anywhere(),),
         scratch_shapes=[
-            pltpu.VMEM((2, half_rows, width), BF16),
-            pltpu.VMEM((2, half_rows, width), BF16),
-            pltpu.VMEM((2, half_rows, units), BF16),
-            pltpu.VMEM((halves, half_rows, width), F32),
+            pltpu.VMEM((2, rows, width), BF16),
+            pltpu.VMEM((2, rows, width), BF16),
+            pltpu.VMEM((2, rows, units), BF16),
+            pltpu.VMEM((units, width), F32),
             pltpu.SemaphoreType.DMA,
+            pltpu.SemaphoreType.DMA((2, 2)),
             pltpu.SemaphoreType.DMA((2,)),
-            pltpu.SemaphoreType.DMA,
         ]
-        + Scatter.scratch(owners, rows, width, HALF_PARTS, halves)
-        + Gather.scratch(owners, halves),
+        + Scatter.scratch(owners, rows, width, PARTS)
+        + Gather.scratch(owners)
+        + RepSum.scratch(reps, units // shard, share, width),
         compiler_params=pltpu.CompilerParams(
-            collective_id=2, has_side_effects=True, vmem_limit_bytes=60 * 2**20
+            collective_id=2, has_side_effects=True, vmem_limit_bytes=63 * 2**20
         ),
         cost_estimate=pl.CostEstimate(
-            flops=10 * owners * rows * width * units,
+            flops=12 * owners * rows * width * units,
             bytes_accessed=40 * 2**20,
             transcendentals=0,
         ),
         name="mlp",
-    )(
-        entry.reshape(halves, half_rows, width),
-        cotangent_all.reshape(owners, halves, half_rows, width),
-        in_cols,
-        w_down,
-        hidden,
-        cotangent,
-        gain_mlp,
-    )
+    )(entry, cotangent_all, in_cols, w_down, hidden, cotangent, gain_mlp)
 
 
 def unturned_norm_back(grad, raw, gain, cosine, sine):
@@ -1107,28 +1124,46 @@
     key_ref,
     key_rot_ref,
     value_ref,
-    position_col_ref,
+    map_ref,
     position_row_ref,
-    cosine_ref,
-    sine_ref,
+    table_ref,
     heads_gain_ref,
     attn_out_ref,
+    grad_gate_up_ref,
+    entry_ref,
     branch_all,
     output_out,
     grads_out,
     gain_out,
     out_term,
+    weight_out,
     branch_buf,
     key_sum,
     value_sum,
+    entry_buf,
+    activated_buf,
+    attn_buf,
     local_sem,
     load_sem,
+    entry_sem,
     *rest,
 ):
     me = lax.axis_index("grp")
     chips = owners // 2
     scatter = Scatter(owners, rest[:4], rest[4:8], by_distance, PARTS)
     gather = Gather(owners, branch_all, *rest[8:10])
+    columns = RepSum(owners, reps, owners, True, rest[10], rest[11], weight_out, rest[12:18])
+    load_columns = column_loads(entry_ref, entry_buf, entry_sem, entry_buf.shape[-1])
+    load_columns(0, me).start()
+    columns_of = columns_term(
+        columns,
+        load_columns,
+        entry_buf,
+        lambda: grad_gate_up_ref[...].reshape(-1, grad_gate_up_ref.shape[-1]),
+    )
+
+    def tick(t):
+        columns.tick(t, columns_of)
     own = pltpu.make_async_copy(branch_ref, branch_all.at[me], local_sem)
     own.start()
     meet(owners, reps)
@@ -1147,14 +1182,17 @@
 
     def block(at):
         load = pltpu.make_async_copy(branch_all.at[at], branch_buf, load_sem)
+        load_attn = pltpu.make_async_copy(attn_out_ref.at[at], attn_buf, local_sem)
         load.start()
+        load_attn.start()
         load.wait()
         grad_attn_out = dot_nt(branch_buf[...], out_ref[...])
-        out_term[...] += dot_tn(attn_out_ref[at], branch_buf[...])
+        load_attn.wait()
+        out_term[...] += dot_tn(attn_buf[...], branch_buf[...])
         for s in range(GROUP_SEQUENCES):
             rows = slice(s * block_rows, (s + 1) * block_rows)
-            cosine, sine = cosine_ref[at, rows], sine_ref[at, rows]
-            allowed = position_row_ref[s] <= position_col_ref[at, rows]
+            cosine, sine = angles(table_ref[at, rows])
+            allowed = position_row_ref[s] <= query_positions(map_ref, s, at)
             allowed = jnp.concatenate([allowed] * per_kv, axis=0)
             for kv in range(kv_heads):
                 span = slice(kv * HEAD_SIZE, (kv + 1) * HEAD_SIZE)
@@ -1202,7 +1240,10 @@
                     gain_out[:, :HEAD_SIZE] += gain_sum
 
     def term(at):
-        both = activated_ref[pl.ds(2 * at, 2)]
+        load = pltpu.make_async_copy(activated_ref.at[pl.ds(2 * at, 2)], activated_buf, load_sem)
+        load.start()
+        load.wait()
+        both = activated_buf[...]
         return dot(both.reshape(-1, both.shape[-1]), down_ref[...])
 
     def then(k):
@@ -1215,12 +1256,29 @@
                 2 * nearest(gather.place, k, chips)
                 + jnp.where(which == 0, gather.core, 1 - gather.core)
             )
+            tick(TICKS * k + 1 + which)
             return 0
 
         lax.fori_loop(0, 2, one, 0)
 
-    interleave(gather, scatter, term, then=then)
-    output_out[...] = (hidden_ref[...] + scatter.acc[...]).astype(BF16)
+    interleave(gather, scatter, term, then=then, fill=lambda k: tick(TICKS * k))
+    hidden = scatter.both.at[1 - scatter.core]
+    load_hidden = pltpu.make_async_copy(hidden_ref, hidden, local_sem)
+    load_hidden.start()
+    load_hidden.wait()
+    output_out[...] = (hidden[...] + scatter.acc[...]).astype(BF16)
+
+    key_raw = scatter.both.at[0]
+
+    def key_columns(at):
+        return pl.ds(pl.multiple_of(at * kv_cols, HEAD_SIZE), kv_cols)
+
+    def load_keys(at, _):
+        pltpu.make_async_copy(key_ref.at[at], key_raw.at[:, key_columns(at)], load_sem).start()
+        return 0
+
+    lax.fori_loop(0, owners, load_keys, 0)
+    arrived(key_raw.at[:, pl.ds(0, owners * kv_cols)], load_sem)
 
     def keys(at, _):
         for s in range(GROUP_SEQUENCES):
@@ -1230,10 +1288,11 @@
                 place = pl.ds(pl.multiple_of(at * block_rows, block_rows), block_rows)
                 grad_raw, gain_sum = unturned_norm_back(
                     key_sum[s, kv, place] * root,
-                    key_ref[at, rows, span],
+                    key_raw[
+                        rows, pl.ds(pl.multiple_of(at * kv_cols, HEAD_SIZE) + span.start, HEAD_SIZE)
+                    ],
                     gain_key,
-                    cosine_ref[at, rows],
-                    sine_ref[at, rows],
+                    *angles(table_ref[at, rows]),
                 )
                 first_col = 2 * q_cols + kv * HEAD_SIZE
                 grads_out[at, rows, first_col : first_col + HEAD_SIZE] = grad_raw.astype(BF16)
@@ -1245,8 +1304,15 @@
         return 0
 
     lax.fori_loop(0, owners, keys, 0)
+
+    def late(t, _):
+        tick(t)
+        return 0
+
+    lax.fori_loop(TICKS * chips, columns.ticks(), late, 0)
     gather.finish()
     scatter.finish()
+    columns.finish()
 
 
 def backward(
@@ -1265,16 +1331,18 @@
     key_raw,
     key_rot,
     value_rows,
-    position_col,
+    block_map,
     position_row,
-    cosine,
-    sine,
+    table,
     heads_gain,
     attn_out,
+    grad_gate_up,
+    entry_all,
 ):
     rows, width = branch.shape
     cols = 2 * (heads + kv_heads) * HEAD_SIZE
     seq_len = position_row.shape[-1]
+    shard = width // owners
     shape = jax.ShapeDtypeStruct
     outs = (
         shape((owners, rows, width), BF16),
@@ -1282,23 +1350,39 @@
         shape((owners, rows, cols), BF16),
         shape((1, 2 * HEAD_SIZE), F32),
         shape(w_out.shape, F32),
+        shape((owners, reps, shard // reps, grad_gate_up.shape[2]), BF16),
     )
     return pl.pallas_call(
         functools.partial(backward_kernel, owners, reps, heads, kv_heads),
         out_shape=outs,
-        in_specs=[anywhere()] + [vmem()] * 16,
-        out_specs=(anywhere(),) + (vmem(),) * 4,
+        in_specs=[anywhere()] * 2
+        + [vmem()] * 2
+        + [anywhere()]
+        + [vmem()] * 3
+        + [anywhere()]
+        + [vmem()] * 2
+        + [smem()]
+        + [vmem()] * 3
+        + [anywhere()]
+        + [vmem()]
+        + [anywhere()],
+        out_specs=(anywhere(),) + (vmem(),) * 4 + (anywhere(),),
         scratch_shapes=[
             pltpu.VMEM((rows, width), BF16),
             pltpu.VMEM((GROUP_SEQUENCES, kv_heads, seq_len, HEAD_SIZE), F32),
             pltpu.VMEM((GROUP_SEQUENCES, kv_heads, seq_len, HEAD_SIZE), F32),
+            pltpu.VMEM((2, owners, rows, shard), BF16),
+            pltpu.VMEM((2,) + activated.shape[1:], BF16),
+            pltpu.VMEM(attn_out.shape[1:], BF16),
             pltpu.SemaphoreType.DMA,
             pltpu.SemaphoreType.DMA,
+            pltpu.SemaphoreType.DMA((2,)),
         ]
         + Scatter.scratch(owners, rows, width, PARTS)
-        + Gather.scratch(owners),
+        + Gather.scratch(owners)
+        + RepSum.scratch(reps, owners, shard // reps, grad_gate_up.shape[2]),
         compiler_params=pltpu.CompilerParams(
-            collective_id=3, has_side_effects=True, vmem_limit_bytes=60 * 2**20
+            collective_id=3, has_side_effects=True, vmem_limit_bytes=63 * 2**20
         ),
         cost_estimate=pl.CostEstimate(
             flops=4 * owners * rows * width * cols,
@@ -1318,12 +1402,13 @@
         key_raw,
         key_rot,
         value_rows,
-        position_col,
+        block_map,
         position_row,
-        cosine,
-        sine,
+        table,
         heads_gain,
         attn_out,
+        grad_gate_up,
+        entry_all,
     )
 
 
@@ -1545,28 +1630,84 @@
     )
 
 
+def in_rows_kernel(grads_ref, out_ref):
+    units = out_ref.shape[2]
+    grads = grads_ref[0].reshape(-1, 2 * units).astype(F32)
+    out_ref[:, 0, :] = grads[:, :units]
+    out_ref[:, 1, :] = grads[:, units:]
+
+
+def in_rows(grads):
+    owners, reps, share, cols = grads.shape
+    units = cols // 2
+    return pl.pallas_call(
+        in_rows_kernel,
+        grid=(owners,),
+        out_shape=jax.ShapeDtypeStruct((reps * share, 2, owners * units), F32),
+        in_specs=[pl.BlockSpec((1, reps, share, cols), lambda e: (e, 0, 0, 0))],
+        out_specs=pl.BlockSpec((reps * share, 2, units), lambda e: (0, 0, e)),
+        compiler_params=pltpu.CompilerParams(vmem_limit_bytes=40 * 2**20),
+        name="in_rows",
+    )(grads)
+
+
+def qkvg_rows_kernel(groups, grads_ref, out_ref, buf, sem):
+    e = pl.program_id(0)
+    owners = pl.num_programs(0)
+
+    def copies(e):
+        slot = e % 2
+        for i, (base, at, cols) in enumerate(groups):
+            yield pltpu.make_async_copy(
+                buf.at[slot, :, pl.ds(at, cols)],
+                out_ref.at[:, pl.ds(pl.multiple_of(base + e * cols, HEAD_SIZE), cols)],
+                sem.at[slot, i],
+            )
+
+    @pl.when(e >= 2)
+    def _():
+        for copy in copies(e - 2):
+            copy.wait()
+
+    buf[e % 2] = grads_ref[0].reshape(buf.shape[1:]).astype(F32)
+    for copy in copies(e):
+        copy.start()
+
+    @pl.when(e == owners - 1)
+    def _():
+        for late in (e - 1, e):
+            for copy in copies(late):
+                copy.wait()
+
+
+def qkvg_rows(grads, heads, kv_heads):
+    owners, reps, share, cols = grads.shape
+    q_cols, kv_cols = heads * HEAD_SIZE, kv_heads * HEAD_SIZE
+    groups, base, at = [], 0, 0
+    for width in (q_cols, q_cols, kv_cols, kv_cols):
+        groups.append((base, at, width))
+        base += width * owners
+        at += width
+    return pl.pallas_call(
+        functools.partial(qkvg_rows_kernel, tuple(groups)),
+        grid=(owners,),
+        out_shape=jax.ShapeDtypeStruct((reps * share, owners * cols), F32),
+        in_specs=[pl.BlockSpec((1, reps, share, cols), lambda e: (e, 0, 0, 0))],
+        out_specs=anywhere(),
+        scratch_shapes=[
+            pltpu.VMEM((2, reps * share, cols), F32),
+            pltpu.SemaphoreType.DMA((2, len(groups))),
+        ],
+        compiler_params=pltpu.CompilerParams(vmem_limit_bytes=40 * 2**20),
+        name="qkvg_rows",
+    )(grads)
+
+
 def positions_of(block_ids):
     offsets = jnp.arange(BLOCK_TOKENS, dtype=jnp.int32)
     return (block_ids[:, :, None] * BLOCK_TOKENS + offsets[None, None, :]).reshape(
         block_ids.shape[0], -1
     )
-
-
-def to_rows(gradient):
-    reps = lax.axis_size("rep")
-    owners = lax.axis_size("grp")
-    rows = gradient.shape[0] // owners
-    shaped = gradient.reshape(owners, reps, rows // reps, -1)
-    shaped = jnp.swapaxes(shaped, 0, 1).reshape(gradient.shape)
-    share = lax.psum_scatter(shaped, "rep", scatter_dimension=0, tiled=True)
-    share = share.reshape(owners, rows // reps, -1)
-    swapped = lax.all_to_all(share, "grp", 0, 0, tiled=True)
-    return lax.all_gather(jnp.swapaxes(swapped, 0, 1), "rep", axis=0, tiled=True)
-
-
-def sum_rep(gradient):
-    share = lax.psum_scatter(gradient, "rep", scatter_dimension=0, tiled=True)
-    return lax.all_gather(share, "rep", axis=0, tiled=True)
 
 
 def body(
@@ -1598,9 +1739,11 @@
     all_kv = KEY_VALUE_HEADS * HEAD_SIZE
     hidden_units = w_down.shape[0]
 
-    in_pieces = w_in.reshape(shard, 2, owners, hidden_units).transpose(2, 0, 1, 3)
-    in_pieces = in_pieces.reshape(owners, shard, 2 * hidden_units)
     reps = lax.axis_size("rep")
+    share = shard // reps
+    in_pieces = lax.dynamic_slice_in_dim(w_in, lax.axis_index("rep") * share, share, 0)
+    in_pieces = in_pieces.reshape(share, 2, owners, hidden_units).transpose(2, 0, 1, 3)
+    in_pieces = in_pieces.reshape(owners, share, 2 * hidden_units)
     head_part = norm_query.shape[0]
     spread = jnp.zeros((2, HEAD_SIZE), jnp.float32)
     spread = lax.dynamic_update_slice(
@@ -1611,15 +1754,9 @@
     )[None]
 
     positions = positions_of(block_map)
-    cosine, sine = rotary_tables(positions)
-    sine = sine * jnp.where(jnp.arange(HEAD_SIZE) < HEAD_SIZE // 2, -1.0, 1.0)
-
-    def by_block(table):
-        shaped = table.reshape(GROUP_SEQUENCES, owners, block_rows, HEAD_SIZE)
-        return jnp.swapaxes(shaped, 0, 1).reshape(owners, rows_here, HEAD_SIZE)
-
-    cosine = by_block(cosine)
-    sine = by_block(sine)
+    table = rotary_table(positions)
+    table = table.reshape(GROUP_SEQUENCES, owners, block_rows, HEAD_SIZE)
+    table = jnp.swapaxes(table, 0, 1).reshape(owners, rows_here, HEAD_SIZE)
     (
         attn_input,
         query_raw,
@@ -1639,16 +1776,12 @@
         tokens,
         w_qkvg,
         small,
-        cosine,
-        sine,
+        table,
     )
     small_all = small_all[:, 0]
     gain_attn = small_all[:, :shard].reshape(-1)
     gain_mlp = small_all[:, shard : 2 * shard].reshape(-1)
     spread = jnp.sum(small_all[:, 2 * shard :], axis=0)
-    position_blocks = jnp.swapaxes(
-        positions.reshape(GROUP_SEQUENCES, owners, block_rows), 0, 1
-    ).reshape(owners, rows_here, 1)
     attn_out, hidden, mlp_own, cotangent_all, in_cols = attention(
         owners,
         reps,
@@ -1659,7 +1792,7 @@
         key_rot,
         value_rows,
         gate_raw,
-        position_blocks,
+        block_map,
         positions[:, None, :],
         w_out,
         gain_mlp[None],
@@ -1667,13 +1800,18 @@
         in_pieces,
     )
     in_cols = in_cols.reshape(width, -1)
-    mlp_input, activated, grad_gate_up, grad_hidden, branch_own, gain_mlp_sum = mlp(
+    (
+        mlp_input,
+        activated,
+        grad_gate_up,
+        grad_hidden,
+        branch_own,
+        gain_mlp_sum,
+        rows_down,
+    ) = mlp(
         owners, reps, mlp_own, cotangent_all, in_cols, w_down, hidden, cotangent, gain_mlp[None]
     )
-    mlp_input = mlp_input.reshape(-1, width)
-    grad_gate_up = grad_gate_up.reshape(-1, 2 * hidden_units)
-    cotangent_all = cotangent_all.reshape(-1, width)
-    _, output, grad_projected, gain_heads_sum, out_term = backward(
+    _, output, grad_projected, gain_heads_sum, out_term, rows_in = backward(
         owners,
         reps,
         heads,
@@ -1689,12 +1827,13 @@
         key_raw,
         key_rot,
         value_rows,
-        position_blocks,
+        block_map,
         positions[:, None, :],
-        cosine,
-        sine,
+        table,
         spread[None],
         attn_out,
+        grad_gate_up.reshape(owners, rows_here, 2 * hidden_units),
+        mlp_input.reshape(owners, rows_here, width),
     )
     grad_tokens, gains, rows_qkvg, rows_out = last(
         owners,
@@ -1709,31 +1848,23 @@
         gain_heads_sum,
         attn_input,
     )
-    activated = activated.reshape(-1, hidden_units)
-    term_in = jnp.dot(mlp_input.T, grad_gate_up, preferred_element_type=jnp.float32)
-    term_down = jnp.dot(activated.T, cotangent_all, preferred_element_type=jnp.float32)
-    shard_down = sum_rep(term_down.astype(jnp.bfloat16)).astype(jnp.float32)
-    rows_in = to_rows(term_in.astype(jnp.bfloat16)).astype(jnp.float32)
-    shard_in = jnp.swapaxes(rows_in.reshape(shard, owners, 2, hidden_units), 1, 2).reshape(
-        w_in.shape
-    )
+    shard_in = in_rows(rows_in)
+    shard_down = rows_down.reshape(w_down.shape).astype(jnp.float32)
     shard_out = rows_out.reshape(w_out.shape).astype(jnp.float32)
-    rows_qkvg = rows_qkvg.reshape(owners, shard, -1).swapaxes(0, 1).astype(jnp.float32)
-
-    def joined(part, repeat):
-        if repeat > 1:
-            part = part.reshape(shard, owners // repeat, repeat, -1).sum(2)
-        return part.reshape(shard, -1)
-
-    shard_qkvg = jnp.concatenate(
-        [
-            joined(rows_qkvg[:, :, :q_cols], 1),
-            joined(rows_qkvg[:, :, q_cols : 2 * q_cols], 1),
-            joined(rows_qkvg[:, :, 2 * q_cols : 2 * q_cols + kv_cols], sharers),
-            joined(rows_qkvg[:, :, 2 * q_cols + kv_cols :], sharers),
-        ],
-        axis=1,
-    )
+    if sharers == 1:
+        shard_qkvg = qkvg_rows(rows_qkvg, heads, kv_heads)
+    else:
+        rows_qkvg = rows_qkvg.reshape(owners, shard, -1).swapaxes(0, 1).astype(jnp.float32)
+        queries = [rows_qkvg[:, :, i * q_cols : (i + 1) * q_cols] for i in range(2)]
+        others = [
+            rows_qkvg[:, :, 2 * q_cols + i * kv_cols : 2 * q_cols + (i + 1) * kv_cols]
+            .reshape(shard, owners // sharers, sharers, kv_cols)
+            .sum(2)
+            for i in range(2)
+        ]
+        shard_qkvg = jnp.concatenate(
+            [part.reshape(shard, -1) for part in queries + others], axis=1
+        )
     return (
         output,
         grad_tokens,

time: 1040 us -> 890 us (0.86)
  Pallas kernels: 743 us -> 851 us
  waiting for transfers between devices: 94.3 us -> 0 us
  local copies, waits for them, and re-layouts: 79.2 us -> 15.7 us
  blocking collectives: 42.4 us -> 0 us
  matrix products: 29.5 us -> 0 us
  other arithmetic: 30.4 us -> 14.3 us
  between operations: 14.4 us -> 1.2 us
    reduce_scatter x2 -> x0, waiting for transfers between devices: 94.2 us -> none  [the longest x1 73.7 us: to_rows(): share = lax.psum_scatter(shaped, 'rep', scatter_dimension=0, tiled=True)]
    pallas_call x1, Pallas kernels: 147 us -> 219 us  [backward(): pl.pallas_call(functools.partial(backward_kernel, owners, reps, heads, kv...]
    all_to_all x1 -> x0, blocking collectives: 42.4 us -> none  [to_rows(): swapped = lax.all_to_all(share, 'grp', 0, 0, tiled=True)]
    reshape x8 -> x2, local copies, waits for them, and re-layouts: 38.4 us -> 2.95 us  [the longest x1 1.91 us: body(): in_pieces = in_pieces.reshape(owners, share, 2 * hidden_units)]
    dot_general x2 -> x0, matrix products: 29.5 us -> none  [the longest x1 17.5 us: body(): jnp.dot(mlp_input.T, grad_gate_up, preferred_element_type=jnp.float32)]
    unnamed x20 -> x19, local copies, waits for them, and re-layouts: 27.4 us -> 6.78 us
    pallas_call x1, Pallas kernels: 209 us -> 225 us  [mlp(): pl.pallas_call(functools.partial(mlp_kernel, owners, reps), out_shape=out...]
    pallas_call x0 -> x2, Pallas kernels: none -> 10.4 us  [the longest x1 6.45 us: in_rows(): pl.pallas_call(in_rows_kernel, grid=(owners,), out_shape=jax.ShapeDtypeSt...]
  transfers between devices with their start and end apart: 4 -> 0, of which waited for: 2 -> 0; matrix products, arithmetic and copies ran while one was open for 4% -> 0% of each run, Pallas kernels for 28% -> 0%
where the time goes in v4:
time: 890 us; the launch traced here: 882 us
  Pallas kernels  851 us (96%)
  local copies, waits for them, and re-layouts  15.7 us (2%)
  other arithmetic  14.3 us (2%)
    pallas_call x1, Pallas kernels, mlp(): pl.pallas_call(functools.partial(mlp_kernel, owners, reps), out_shape=out...  225 us
    pallas_call x1, Pallas kernels, backward(): pl.pallas_call(functools.partial(backward_kernel, owners, reps, heads, kv...  219 us
    pallas_call x1, Pallas kernels, last(): pl.pallas_call(functools.partial(last_kernel, owners, reps), out_shape=(s...  156 us
    pallas_call x1, Pallas kernels, attention(): pl.pallas_call(functools.partial(attention_kernel, owners, reps, heads, k...  137 us
    pallas_call x1, Pallas kernels, first(): pl.pallas_call(functools.partial(first_kernel, owners, reps, heads, kv_he...  104 us

profile of v4, /device:TPU:0, one launch (start us, length us, event | category | flops | bytes accessed | tf_op | source)
XLA Modules:
  0.0 882.2 jit_solution(9410651743664800214)
XLA Ops:
  0.6 0.7 maximum_convert_fusion
  1.3 0.1 dynamic_update_slice.3
  1.5 0.7 convert_element_type.28
  2.1 0.7 convert_element_type.29
  2.8 0.6 broadcast_in_dim.14.small_ref
  3.4 0.7 broadcast_multiply_fusion
  4.1 0.1 add.58
  4.2 0.1 add.59
  4.2 0.1 add.61
  4.3 3.7 multiply_cosine_fusion
  8.0 1.3 pad_maximum_fusion
  9.3 103.9 %first.1 = (bf16[8,256,2048]{2,1,0:T(8,128)(2,1)}, f32[8,256,256]{2,1,0:T(8,128)}, f32[8,256,256]{2,1,0:T(8,128)}, f32[8,256,128]{2,1,0:T(8,128)}, bf16[8,256,12...) custom-call(bf16[256,2048]{1,0:T(8,128)(2,1)} %tokens_ref.5, ...), custom_call_target="tpu_custom_call" | custom-call | flops 6442450944 | bytes 41943040 | tf_op jit(solution)/shard_map/first/pallas_call | solution.py:433
  113.2 0.7 copy.34
  114.0 0.6 slice_bitcast_fusion
  114.6 0.6 copy.31
  115.2 2.5 constant_dynamic-slice_fusion.2
  117.7 1.0 reshape.125
  118.7 1.2 copy.27
  119.9 1.9 reshape.120.in_pieces_ref
  121.8 0.1 add.64
  121.9 0.1 add.66
  122.0 0.6 broadcast_add_fusion.position_row_ref
  122.6 136.6 %attention.1 = (bf16[8,256,256]{2,1,0:T(8,128)(2,1)}, f32[256,2048]{1,0:T(8,128)}, bf16[256,2048]{1,0:T(8,128)(2,1)}, bf16[8,256,2048]{2,1,0:T(8,128)(2,1)}, bf16[8,4,64,1536]{3,2,1,0:T(8,128)(2,1)}) custom-call(bf16[256,2048]{1,0:T(8,128)(2,1)} %tokens_ref.5, bf16[8,256,256]{2,1,0:T(8,128)(2,1)} %get-tuple-element.40.query_ref.query_rot_ref, ...), custom_call_target="tpu_custom_call" | custom-call | flops 4294967296 | bytes 41943040 | tf_op jit(solution)/shard_map/attention/pallas_call | solution.py:874
  259.2 225.2 %mlp.1 = (bf16[8,256,2048]{2,1,0:T(8,128)(2,1)}, bf16[8,256,768]{2,1,0:T(8,128)(2,1)}, bf16[8,256,1536]{2,1,0:T(8,128)(2,1)}, f32[256,2048]{1,0:T(8,128)}, bf16[...) custom-call(bf16[256,2048]{1,0:T(8,128)(2,1)} %get-tuple-element.45.entry_ref, ...), custom_call_target="tpu_custom_call" | custom-call | flops 38654705664 | bytes 41943040 | tf_op jit(solution)/shard_map/mlp/pallas_call | solution.py:1074
  484.4 219.3 %backward.1 = (bf16[8,256,2048]{2,1,0:T(8,128)(2,1)}, bf16[256,2048]{1,0:T(8,128)(2,1)}, bf16[8,256,768]{2,1,0:T(8,128)(2,1)}, f32[1,256]{1,0:T(1,128)}, f32[256...) custom-call(bf16[256,2048]{1,0:T(8,128)(2,1)} %get-tuple-element.49.branch_ref, ...), custom_call_target="tpu_custom_call" | custom-call | flops 12884901888 | bytes 41943040 | tf_op jit(solution)/shard_map/backward/pallas_call | solution.py:1355
  703.7 0.6 copy.32
  704.3 155.6 %last.1 = (bf16[256,2048]{1,0:T(8,128)(2,1)}, f32[1,768]{1,0:T(1,128)}, bf16[8,4,64,768]{3,2,1,0:T(8,128)(2,1)}, bf16[1,4,64,2048]{3,2,1,0:T(8,128)(2,1)}) custom-call(bf16[8,256,768]{2,1,0:T(8,128)(2,1)} %get-tuple-element.57.grads_ref, bf16[2048,768]{1,0:T(8,128)(2,1)} %bitcast.48, bf16[256,2048]{1,0:T(8,128)(2,1)} %tokens_ref.5, ...), custom_call_target="tpu_custom_call" | custom-call | flops 12884901888 | bytes 41943040 | tf_op jit(solution)/shard_map/last/pallas_call | solution.py:1587
  860.0 0.0 copy-start.1
  860.0 1.9 copy-done.1
  861.9 0.0 copy-start
  861.9 4.0 qkvg_rows.1
  865.9 1.0 copy-done
  866.8 0.0 copy-start.3
  866.8 6.5 in_rows.1
  873.3 0.0 copy-start.6
  873.3 0.0 copy-start.2
  873.3 0.0 copy-done.3
  873.3 1.6 bitcast_convert_fusion.1
  874.9 0.0 copy-done.6
  874.9 0.6 fusion.1
  875.5 0.6 fusion.2
  876.1 0.0 copy-done.2
  876.1 0.0 copy-start.4
  876.1 0.0 copy-start.5
  876.1 3.8 bitcast_convert_fusion
  879.9 0.0 copy-done.4
  879.9 1.0 copy.38
  880.8 0.0 copy-done.5
  880.8 1.0 copy.39
  (7 shorter events, 0.0 us)
Async XLA Ops:
  860.0 1.9 copy-start.1
  861.9 5.0 copy-start
  866.8 6.5 copy-start.3
  873.3 1.6 copy-start.6
  873.3 2.8 copy-start.2
  876.1 3.8 copy-start.4
  876.1 4.7 copy-start.5

commit v5 on v4

--- a/solution.py
+++ b/solution.py
@@ -34,7 +34,8 @@
 def nearest(place, step, chips):
     low = jnp.minimum(place, chips - 1 - place)
     near = (step + 1) // 2
-    both = jnp.where(step % 2 == 1, place - near, place + near)
+    side = jnp.where(2 * place < chips, near, -near)
+    both = jnp.where(step % 2 == 1, place + side, place - side)
     past = step - low
     rest = jnp.where(place > chips - 1 - place, place - past, place + past)
     return jnp.where(step <= 2 * low, both, rest)
@@ -156,6 +157,98 @@
         return [
             pltpu.SemaphoreType.DMA((halves, 3, owners // 2)),
             pltpu.SemaphoreType.DMA((halves, owners)),
+        ]
+
+
+class FarGather:
+    def __init__(self, owners, buf, send, recv, parts):
+        self.owners, self.chips, self.parts = owners, owners // 2, parts
+        self.me = lax.axis_index("grp")
+        self.place, self.core = self.me // 2, self.me % 2
+        self.buf, self.send, self.recv = buf, send, recv
+        self.part = buf.shape[1] // parts
+        self.devices = (self.me + 2, self.me - 2, self.me + 1 - 2 * self.core)
+
+    def rows(self, part):
+        return pl.ds(part * self.part, self.part)
+
+    def copy(self, way, block, part):
+        ref = self.buf.at[block, self.rows(part)]
+        return to_grp(
+            ref,
+            ref,
+            self.send.at[way, block // 2, part],
+            self.recv.at[block, part],
+            self.devices[way],
+        )
+
+    def own(self, way):
+        for part in range(self.parts):
+            self.copy(way, self.me, part).start()
+
+    def begin(self):
+        self.own(2)
+        pl.when(self.place == 0)(lambda: self.own(0))
+        pl.when(self.place == self.chips - 1)(lambda: self.own(1))
+
+    def pass_on(self, way, at, part, onward):
+        block = 2 * at + self.core
+        arrived(self.buf.at[block, self.rows(part)], self.recv.at[block, part])
+        pl.when(onward)(lambda: self.copy(way, block, part).start())
+        self.copy(2, block, part).start()
+
+    def up(self, r, part):
+        pl.when(r < self.place)(
+            lambda: self.pass_on(0, r, part, self.place < self.chips - 1)
+        )
+
+    def down(self, r, part):
+        at = self.chips - 1 - r
+        pl.when(at > self.place)(lambda: self.pass_on(1, at, part, self.place > 0))
+
+    def round(self, r):
+        def flows(ahead, behind):
+            ahead(r, 0)
+            for part in range(1, self.parts):
+                ahead(r, part)
+                behind(r, part - 1)
+            behind(r, self.parts - 1)
+
+        lower = 2 * self.place < self.chips
+        pl.when(lower)(lambda: flows(self.up, self.down))
+        pl.when(jnp.logical_not(lower))(lambda: flows(self.down, self.up))
+        last = self.chips - 1
+        pl.when((r == self.place - 1) & (self.place < last))(lambda: self.own(0))
+        pl.when((last - r == self.place + 1) & (self.place > 0))(lambda: self.own(1))
+
+    def sibling(self, at):
+        block = 2 * at + 1 - self.core
+        for part in range(self.parts):
+            arrived(self.buf.at[block, self.rows(part)], self.recv.at[block, part])
+
+    def finish(self):
+        last = self.chips - 1
+
+        def one(at, _):
+            block = 2 * at + self.core
+            for part in range(self.parts):
+                for way, when in (
+                    (0, (at <= self.place) & (self.place < last)),
+                    (1, (at >= self.place) & (self.place > 0)),
+                ):
+                    pl.when(when)(
+                        lambda way=way, part=part: self.copy(way, block, part).wait_send()
+                    )
+                self.copy(2, block, part).wait_send()
+            return 0
+
+        lax.fori_loop(0, self.chips, one, 0)
+
+    @staticmethod
+    def scratch(owners, parts):
+        return [
+            pltpu.SemaphoreType.DMA((3, owners // 2, parts)),
+            pltpu.SemaphoreType.DMA((owners, parts)),
         ]
 
 
@@ -627,27 +720,29 @@
             for c, s in enumerate(held)
         ]
 
-    def deliver(self, t, do_local, do_remote):
+    def deliver(self, t, sent=False):
         u = self.unit(t)
         source = self.held.at[u, self.rep]
         slot = self.me if self.along else u
-        local = pltpu.make_async_copy(source, self.result.at[slot, self.rep], self.own_recv.at[slot])
-        if not self.along:
-            do_local(local)
-            return
-        remote = to_grp(
-            source,
-            self.result.at[slot, self.rep],
-            self.own_send.at[u],
-            self.own_recv.at[slot],
-            u,
-        )
-        pl.when(u == self.me)(lambda: do_local(local))
-        pl.when(u != self.me)(lambda: do_remote(remote))
+        target = self.result.at[slot, self.rep]
+
+        def local():
+            if not sent:
+                pltpu.make_async_copy(source, target, self.own_recv.at[slot]).start()
+
+        def remote():
+            copy = to_grp(source, target, self.own_send.at[u], self.own_recv.at[slot], u)
+            copy.wait_send() if sent else copy.start()
+
+        if self.along:
+            pl.when(u == self.me)(local)
+            pl.when(u != self.me)(remote)
+        else:
+            local()
 
     def tick(self, t, term):
-        def phase(lag):
-            return (t >= lag) & (t < self.units + lag)
+        def phase(step, more=0):
+            return (t >= LAG * step + more) & (t < self.units + LAG * step + more)
 
         @pl.when(phase(0))
         def _():
@@ -659,7 +754,7 @@
         for j in range(1, self.bits + 1):
 
             @pl.when(phase(j))
-            def _(j=j, t=t - j):
+            def _(j=j, t=t - LAG * j):
                 u = self.unit(t)
                 first_index = sum(1 << (self.bits - 1 - i) for i in range(j - 1))
                 for c, s in enumerate(self.spread(self.rep, t, range(j, self.bits))):
@@ -672,12 +767,12 @@
                     for copy in self.downs(t, j):
                         copy.start()
                 else:
-                    self.deliver(t, lambda c: c.start(), lambda c: c.start())
+                    self.deliver(t)
 
         for j in range(self.bits + 1):
 
-            @pl.when(phase(self.bits + 1 + j))
-            def _(j=j, t=t - self.bits - 1 - j):
+            @pl.when(phase(self.bits + 1 + j, FAR_LAG))
+            def _(j=j, t=t - LAG * (self.bits + 1 + j) - FAR_LAG):
                 e = self.source(t)
                 if j == 0:
                     arrived(self.result.at[e, self.rep], self.own_recv.at[e])
@@ -692,14 +787,14 @@
                         copy.start()
 
     def ticks(self):
-        return self.units + 2 * self.bits + 1
+        return self.units + LAG * (2 * self.bits + 1) + FAR_LAG
 
     def finish(self):
         def one(t, _):
             for j in range(self.bits):
                 for copy in self.downs(t, j) + self.ups(t, j):
                     copy.wait_send()
-            self.deliver(t, lambda c: None, lambda c: c.wait_send())
+            self.deliver(t, True)
             return 0
 
         lax.fori_loop(0, self.units, one, 0)
@@ -719,32 +814,49 @@
         ]
 
 
-def interleave(gather, scatter, term, ready=None, then=None, fill=None):
+def staged(scatter, chips, k, term, work):
+    middle = (scatter.place > 0) & (scatter.place < chips - 1)
+    scatter.prepare(k, term)
+
+    @pl.when(~middle)
+    def _():
+        scatter.combine(k)
+
+    work()
+
+    @pl.when(middle)
+    def _():
+        scatter.combine(k)
+
+
+LAG = 2
+FAR_LAG = 0
+
+
+def interleave(gather, scatter, term, ready=None, then=None):
     chips = gather.chips
     middle = (gather.place > 0) & (gather.place < chips - 1)
 
     def stage(k, _):
         if ready is not None:
             ready(k)
-        scatter.prepare(k, term)
-        if fill is not None:
-            fill(k)
-
-        @pl.when(middle & (2 * k + 1 < chips))
-        def _():
-            gather.step(2 * k + 1)
-
-        @pl.when(middle & (2 * k + 2 < chips))
-        def _():
-            gather.step(2 * k + 2)
-
-        scatter.combine(k)
-
-        @pl.when((~middle) & (k + 1 < chips))
-        def _():
-            gather.step(k + 1)
-
-        then(k)
+
+        def work():
+            then(k)
+
+            @pl.when((~middle) & (k + 1 < chips))
+            def _():
+                gather.step(k + 1)
+
+            @pl.when(middle & (2 * k + 1 < chips))
+            def _():
+                gather.step(2 * k + 1)
+
+            @pl.when(middle & (2 * k + 2 < chips))
+            def _():
+                gather.step(2 * k + 2)
+
+        staged(scatter, chips, k, term, work)
         return 0
 
     lax.fori_loop(0, chips, stage, 0)
@@ -920,11 +1032,10 @@
     grad_hidden_out,
     grad_branch_out,
     gain_out,
-    weight_out,
+    down_sum,
     entry_buf,
     cotangent_buf,
     activated_buf,
-    down_sum,
     local_sem,
     load_sem,
     store_sem,
@@ -932,108 +1043,89 @@
 ):
     me = lax.axis_index("grp")
     chips = owners // 2
-    gather = Gather(owners, entry_all, *rest[8:10])
+    gather = FarGather(owners, entry_all, *rest[8:10], PARTS)
     scatter = Scatter(owners, rest[:4], rest[4:8], by_distance, PARTS)
-    shard = weight_out.shape[1] * weight_out.shape[2]
-    rows = RepSum(
-        owners, reps, down_ref.shape[0] // shard, False, rest[10], rest[11], weight_out, rest[12:18]
-    )
     units = down_ref.shape[0]
+    middle = (gather.place > 0) & (gather.place < chips - 1)
     own = pltpu.make_async_copy(entry_ref, entry_all.at[me], local_sem)
     own.start()
     meet(owners, reps)
-    gather.forward(me, entry_ref)
+    own.wait()
+    gather.begin()
     down_sum[...] = jnp.zeros_like(down_sum)
-    own.wait()
-
-    def block_of(k, which):
-        return 2 * nearest(gather.place, k, chips) + jnp.where(
-            which == 0, gather.core, 1 - gather.core
+
+    def stores(at):
+        return pltpu.make_async_copy(
+            activated_buf, activated_out.at[pl.ds(2 * at, 2)], store_sem
         )
 
-    def store(which, at):
-        return pltpu.make_async_copy(
-            activated_buf.at[which], activated_out.at[at], store_sem.at[which]
+    def compute(at, first=False):
+        pair = pl.ds(2 * at, 2)
+        cotangent_load = pltpu.make_async_copy(
+            cotangent_all_ref.at[pair], cotangent_buf, load_sem.at[1]
         )
-
-    def compute(k):
-        def one(which, _):
-            at = block_of(k, which)
-            cotangent_load = pltpu.make_async_copy(
-                cotangent_all_ref.at[at], cotangent_buf.at[which], load_sem.at[1, which]
-            )
-            cotangent_load.start()
-
-            @pl.when(which == 1)
-            def _():
-                gather.sibling(k)
-
-            entry_load = pltpu.make_async_copy(
-                entry_all.at[at], entry_buf.at[which], load_sem.at[0, which]
-            )
-            entry_load.start()
-            cotangent_load.wait()
-            grad_activated = dot_nt(cotangent_buf[which], down_ref[...])
-            entry_load.wait()
-            gate_up = dot(entry_buf[which], in_ref[...])
-            gate, up = gate_up[:, :units], gate_up[:, units:]
-            sig = jax.nn.sigmoid(gate)
-            silu = gate * sig
-
-            @pl.when(k > 0)
-            def _():
-                store(which, at).wait()
-
-            activated_buf[which] = (silu * up).astype(BF16)
-            store(which, at).start()
-            grads_out[at, :, :units] = (
-                grad_activated * up * sig * (1.0 + gate * (1.0 - sig))
-            ).astype(BF16)
-            grads_out[at, :, units:] = (grad_activated * silu).astype(BF16)
-            down_sum[...] += dot_tn(activated_buf[which], cotangent_buf[which])
-            return 0
-
-        lax.fori_loop(0, 2, one, 0)
+        cotangent_load.start()
+        gather.sibling(at)
+        entry_load = pltpu.make_async_copy(entry_all.at[pair], entry_buf, load_sem.at[0])
+        entry_load.start()
+        cotangent_load.wait()
+        cotangent = cotangent_buf[...].reshape(-1, cotangent_buf.shape[-1])
+        grad_activated = dot_nt(cotangent, down_ref[...])
+        entry_load.wait()
+        gate_up = dot(entry_buf[...].reshape(-1, entry_buf.shape[-1]), in_ref[...])
+        gate, up = gate_up[:, :units], gate_up[:, units:]
+        sig = jax.nn.sigmoid(gate)
+        silu = gate * sig
+        if not first:
+            stores(at).wait()
+        activated = (silu * up).astype(BF16)
+        shape = activated_buf.shape
+        activated_buf[...] = activated.reshape(shape)
+        stores(at).start()
+        grads_out[pair, :, :units] = (
+            (grad_activated * up * sig * (1.0 + gate * (1.0 - sig))).astype(BF16).reshape(shape)
+        )
+        grads_out[pair, :, units:] = (grad_activated * silu).astype(BF16).reshape(shape)
+        down_sum[...] += dot_tn(activated, cotangent)
 
     def term(at):
         both = grads_out[pl.ds(2 * at, 2)]
         return dot_nt(both.reshape(-1, both.shape[-1]), in_ref[...])
 
-    def rows_of(t, u):
-        return down_sum[pl.ds(pl.multiple_of(u * shard, shard), shard)]
-
-    middle = (gather.place > 0) & (gather.place < chips - 1)
-    early = jnp.where(middle, chips, 1)
-
-    def step(k, _):
-        gather.step(k)
+    def step(r, _):
+        gather.round(r)
         return 0
 
-    def front(k, _):
-        @pl.when(k >= early)
-        def _():
-            gather.step(k)
-
-        compute(k)
+    lax.fori_loop(0, jnp.where(middle, chips - 1, 1), step, 0)
+    stores(0).start()
+
+    def compute_step(k, _):
+        compute(jnp.where(k < 0, gather.place, scatter.at(jnp.maximum(k, 0))))
         return 0
 
-    lax.fori_loop(1, early, step, 0)
-    lax.fori_loop(0, chips, front, 0)
+    lax.fori_loop(jnp.where(middle, 0, -1), 1, compute_step, 0)
 
     def back(k, _):
-        scatter.prepare(k, term)
-        rows.tick(TICKS * k, rows_of)
-        scatter.combine(k)
-
-        def one(t, _):
-            rows.tick(t, rows_of)
-            return 0
-
-        lax.fori_loop(TICKS * k + 1, TICKS * (k + 1), one, 0)
+        more = jnp.where(middle, k + 1 < chips, k + 1 < chips - 1)
+
+        def work():
+            @pl.when(more & (~middle))
+            def _():
+                gather.round(k + 1)
+
+            @pl.when(more)
+            def _():
+                compute(scatter.at(k + 1))
+
+        staged(scatter, chips, k, term, work)
         return 0
 
     lax.fori_loop(0, chips, back, 0)
-    hidden = hidden_ref[...]
+    hidden_buf = scatter.both.at[1 - scatter.core]
+    load_hidden = pltpu.make_async_copy(hidden_ref, hidden_buf, local_sem)
+    load_hidden.start()
+    load_hidden.wait()
+    hidden = hidden_buf[...]
     normed, scale = head_norm(hidden)
     grad_entry = scatter.acc[...]
     gain_out[...] = jnp.sum(grad_entry * normed, axis=0, keepdims=True)
@@ -1043,24 +1135,14 @@
     )
     grad_hidden_out[...] = grad_hidden
     grad_branch_out[...] = grad_hidden.astype(BF16)
-
-    def late(t, _):
-        rows.tick(t, rows_of)
-        return 0
-
-    lax.fori_loop(TICKS * chips, rows.ticks(), late, 0)
-    for which in range(2):
-        store(which, block_of(chips - 1, which)).wait()
+    stores(0).wait()
     gather.finish()
     scatter.finish()
-    rows.finish()
 
 
 def mlp(owners, reps, entry, cotangent_all, in_cols, w_down, hidden, cotangent, gain_mlp):
     rows, width = entry.shape
     units = w_down.shape[0]
-    shard = width // owners
-    share = shard // reps
     shape = jax.ShapeDtypeStruct
     outs = (
         shape((owners, rows, width), BF16),
@@ -1069,25 +1151,23 @@
         shape((rows, width), F32),
         shape((rows, width), BF16),
         shape((1, width), F32),
-        shape((units // shard, reps, share, width), BF16),
+        shape((units, width), F32),
     )
     return pl.pallas_call(
         functools.partial(mlp_kernel, owners, reps),
         out_shape=outs,
-        in_specs=[anywhere()] * 2 + [vmem()] * 5,
-        out_specs=(anywhere(),) * 2 + (vmem(),) * 4 + (anywhere(),),
+        in_specs=[anywhere()] * 2 + [vmem()] * 2 + [anywhere()] + [vmem()] * 2,
+        out_specs=(anywhere(),) * 2 + (vmem(),) * 5,
         scratch_shapes=[
             pltpu.VMEM((2, rows, width), BF16),
             pltpu.VMEM((2, rows, width), BF16),
             pltpu.VMEM((2, rows, units), BF16),
-            pltpu.VMEM((units, width), F32),
             pltpu.SemaphoreType.DMA,
-            pltpu.SemaphoreType.DMA((2, 2)),
             pltpu.SemaphoreType.DMA((2,)),
+            pltpu.SemaphoreType.DMA,
         ]
         + Scatter.scratch(owners, rows, width, PARTS)
-        + Gather.scratch(owners)
-        + RepSum.scratch(reps, units // shard, share, width),
+        + FarGather.scratch(owners, PARTS),
         compiler_params=pltpu.CompilerParams(
             collective_id=2, has_side_effects=True, vmem_limit_bytes=63 * 2**20
         ),
@@ -1143,8 +1223,12 @@
     entry_buf,
     activated_buf,
     attn_buf,
+    grad_attn_buf,
+    gate_buf,
     local_sem,
     load_sem,
+    activated_sem,
+    gate_sem,
     entry_sem,
     *rest,
 ):
@@ -1180,15 +1264,8 @@
     gain_query = heads_gain_ref[:, :HEAD_SIZE]
     gain_key = heads_gain_ref[:, HEAD_SIZE:]
 
-    def block(at):
-        load = pltpu.make_async_copy(branch_all.at[at], branch_buf, load_sem)
-        load_attn = pltpu.make_async_copy(attn_out_ref.at[at], attn_buf, local_sem)
-        load.start()
-        load_attn.start()
-        load.wait()
-        grad_attn_out = dot_nt(branch_buf[...], out_ref[...])
-        load_attn.wait()
-        out_term[...] += dot_tn(attn_buf[...], branch_buf[...])
+    def block(at, which):
+        grad_attn_out = grad_attn_buf[which]
         for s in range(GROUP_SEQUENCES):
             rows = slice(s * block_rows, (s + 1) * block_rows)
             cosine, sine = angles(table_ref[at, rows])
@@ -1212,7 +1289,7 @@
                 inputs = []
                 for i, h in enumerate(spans):
                     grad = grad_attn_out[rows, h]
-                    sig = jax.nn.sigmoid(gate_ref[at, rows, h])
+                    sig = jax.nn.sigmoid(gate_buf[which, rows, h])
                     inputs.append((grad * sig).astype(BF16))
                     gated = slice(q_cols + h.start, q_cols + h.stop)
                     grads_out[at, rows, gated] = (
@@ -1239,29 +1316,54 @@
                     grads_out[at, rows, h] = grad_raw.astype(BF16)
                     gain_out[:, :HEAD_SIZE] += gain_sum
 
+    def load_activated(k):
+        pair = pl.ds(2 * scatter.at(k), 2)
+        return pltpu.make_async_copy(activated_ref.at[pair], activated_buf, activated_sem)
+
+    load_activated(0).start()
+
     def term(at):
-        load = pltpu.make_async_copy(activated_ref.at[pl.ds(2 * at, 2)], activated_buf, load_sem)
-        load.start()
-        load.wait()
+        load_activated(0).wait()
         both = activated_buf[...]
         return dot(both.reshape(-1, both.shape[-1]), down_ref[...])
 
     def then(k):
+        @pl.when(k + 1 < chips)
+        def _():
+            load_activated(k + 1).start()
+
+        at = nearest(gather.place, k, chips)
+        pair = pl.ds(2 * at, 2)
+        gather.sibling(k)
+        load = pltpu.make_async_copy(branch_all.at[pair], branch_buf, load_sem)
+        load_attn = pltpu.make_async_copy(attn_out_ref.at[pair], attn_buf, local_sem)
+        load_gate = pltpu.make_async_copy(gate_ref.at[pair], gate_buf, gate_sem)
+        load.start()
+        load_attn.start()
+        load_gate.start()
+        tick(TICKS * k)
+        load.wait()
+        load_attn.wait()
+        load_gate.wait()
+        branch = branch_buf[...].reshape(-1, branch_buf.shape[-1])
+        grad_attn_buf[...] = dot_nt(branch, out_ref[...]).reshape(grad_attn_buf.shape)
+        out_term[...] += dot_tn(attn_buf[...].reshape(-1, attn_buf.shape[-1]), branch)
+
         def one(which, _):
-            @pl.when(which == 1)
-            def _():
-                gather.sibling(k)
-
-            block(
-                2 * nearest(gather.place, k, chips)
-                + jnp.where(which == 0, gather.core, 1 - gather.core)
-            )
-            tick(TICKS * k + 1 + which)
+            block(2 * at + which, which)
+            late_tick(TICKS * k + 1 + TICKS // 2 * which)
             return 0
 
         lax.fori_loop(0, 2, one, 0)
 
-    interleave(gather, scatter, term, then=then, fill=lambda k: tick(TICKS * k))
+    def late_tick(t):
+        def two(t, _):
+            tick(t)
+            return 0
+
+        lax.fori_loop(t, t + TICKS // 2, two, 0)
+
+    interleave(gather, scatter, term, then=then)
     hidden = scatter.both.at[1 - scatter.core]
     load_hidden = pltpu.make_async_copy(hidden_ref, hidden, local_sem)
     load_hidden.start()
@@ -1313,6 +1415,9 @@
     gather.finish()
     scatter.finish()
     columns.finish()
+
+
+VMEM_LIMIT = 63 * 2**20 + 2**19
 
 
 def backward(
@@ -1358,8 +1463,8 @@
         in_specs=[anywhere()] * 2
         + [vmem()] * 2
         + [anywhere()]
-        + [vmem()] * 3
-        + [anywhere()]
+        + [vmem()] * 2
+        + [anywhere()] * 2
         + [vmem()] * 2
         + [smem()]
         + [vmem()] * 3
@@ -1368,12 +1473,16 @@
         + [anywhere()],
         out_specs=(anywhere(),) + (vmem(),) * 4 + (anywhere(),),
         scratch_shapes=[
-            pltpu.VMEM((rows, width), BF16),
+            pltpu.VMEM((2, rows, width), BF16),
             pltpu.VMEM((GROUP_SEQUENCES, kv_heads, seq_len, HEAD_SIZE), F32),
             pltpu.VMEM((GROUP_SEQUENCES, kv_heads, seq_len, HEAD_SIZE), F32),
             pltpu.VMEM((2, owners, rows, shard), BF16),
             pltpu.VMEM((2,) + activated.shape[1:], BF16),
-            pltpu.VMEM(attn_out.shape[1:], BF16),
+            pltpu.VMEM((2,) + attn_out.shape[1:], BF16),
+            pltpu.VMEM((2,) + attn_out.shape[1:], F32),
+            pltpu.VMEM((2,) + attn_out.shape[1:], F32),
+            pltpu.SemaphoreType.DMA,
+            pltpu.SemaphoreType.DMA,
             pltpu.SemaphoreType.DMA,
             pltpu.SemaphoreType.DMA,
             pltpu.SemaphoreType.DMA((2,)),
@@ -1382,7 +1491,7 @@
         + Gather.scratch(owners)
         + RepSum.scratch(reps, owners, shard // reps, grad_gate_up.shape[2]),
         compiler_params=pltpu.CompilerParams(
-            collective_id=3, has_side_effects=True, vmem_limit_bytes=63 * 2**20
+            collective_id=3, has_side_effects=True, vmem_limit_bytes=VMEM_LIMIT
         ),
         cost_estimate=pl.CostEstimate(
             flops=4 * owners * rows * width * cols,
@@ -1442,13 +1551,14 @@
     grad_hidden_ref,
     gain_ref,
     out_term_ref,
+    down_term_ref,
     gain_mlp_ref,
     gain_heads_ref,
     entry_ref,
     grad_out,
     gains_out,
     weight_out,
-    out_weight_out,
+    rows_out,
     entry_buf,
     gains_send,
     gains_came,
@@ -1464,7 +1574,9 @@
     chips = owners // 2
     scatter = Scatter(owners, rest[:4], rest[4:8], by_distance, PARTS)
     columns = RepSum(owners, reps, owners, True, rest[8], rest[9], weight_out, rest[10:16])
-    rows = RepSum(owners, reps, 1, False, rest[16], rest[17], out_weight_out, rest[18:24])
+    rows = RepSum(
+        owners, reps, rows_out.shape[0], False, rest[16], rest[17], rows_out, rest[18:24]
+    )
     shard = entry_buf.shape[-1]
     load = column_loads(entry_ref, entry_buf, load_sem, shard)
     load(0, me).start()
@@ -1475,8 +1587,12 @@
 
     columns_of = columns_term(columns, load, entry_buf, lambda: flat(grads_ref))
 
+    down_units = down_term_ref.shape[0] // shard
+
     def rows_of(t, u):
-        return out_term_ref[...]
+        at = jnp.minimum(u, down_units - 1) * shard
+        down = down_term_ref[pl.ds(pl.multiple_of(at, shard), shard)]
+        return jnp.where(u < down_units, down, out_term_ref[...])
 
     def tick(t):
         rows.tick(t, rows_of)
@@ -1487,15 +1603,17 @@
         return dot_nt(both.reshape(-1, both.shape[-1]), weight_ref[...])
 
     def stage(k, _):
-        scatter.prepare(k, term)
-        tick(TICKS * k)
-        scatter.combine(k)
-
         def one(t, _):
             tick(t)
             return 0
 
-        lax.fori_loop(TICKS * k + 1, TICKS * (k + 1), one, 0)
+        staged(
+            scatter,
+            chips,
+            k,
+            term,
+            lambda: lax.fori_loop(TICKS * k, TICKS * (k + 1), one, 0),
+        )
         return 0
 
     lax.fori_loop(0, chips, stage, 0)
@@ -1561,7 +1679,7 @@
     rows.finish()
 
 
-TICKS = 3
+TICKS = 5
 
 
 def last(
@@ -1573,6 +1691,7 @@
     grad_hidden,
     gain,
     out_term,
+    down_term,
     gain_mlp,
     gain_heads,
     entry_all,
@@ -1582,6 +1701,7 @@
     shard = width // owners
     share = shard // reps
     small = 2 * shard + gain_heads.shape[1]
+    units = (out_term.shape[0] + down_term.shape[0]) // shard
     shape = jax.ShapeDtypeStruct
     dma = pltpu.SemaphoreType.DMA
     return pl.pallas_call(
@@ -1590,9 +1710,9 @@
             shape((rows, width), BF16),
             shape((1, small), F32),
             shape((owners, reps, share, cols), BF16),
-            shape((1, reps, share, width), BF16),
+            shape((units, reps, share, width), BF16),
         ),
-        in_specs=[vmem()] * 8 + [anywhere()],
+        in_specs=[vmem()] * 9 + [anywhere()],
         out_specs=(vmem(),) * 2 + (anywhere(),) * 2,
         scratch_shapes=[
             pltpu.VMEM((2, owners, rows, shard), BF16),
@@ -1607,7 +1727,7 @@
         ]
         + Scatter.scratch(owners, rows, width, PARTS)
         + RepSum.scratch(reps, owners, share, cols)
-        + RepSum.scratch(reps, 1, share, width),
+        + RepSum.scratch(reps, units, share, width),
         compiler_params=pltpu.CompilerParams(
             collective_id=4, has_side_effects=True, vmem_limit_bytes=60 * 2**20
         ),
@@ -1624,6 +1744,7 @@
         grad_hidden,
         gain,
         out_term,
+        down_term,
         gain_mlp,
         gain_heads,
         entry_all,
@@ -1807,7 +1928,7 @@
         grad_hidden,
         branch_own,
         gain_mlp_sum,
-        rows_down,
+        down_term,
     ) = mlp(
         owners, reps, mlp_own, cotangent_all, in_cols, w_down, hidden, cotangent, gain_mlp[None]
     )
@@ -1835,7 +1956,7 @@
         grad_gate_up.reshape(owners, rows_here, 2 * hidden_units),
         mlp_input.reshape(owners, rows_here, width),
     )
-    grad_tokens, gains, rows_qkvg, rows_out = last(
+    grad_tokens, gains, rows_qkvg, rows_both = last(
         owners,
         reps,
         grad_projected,
@@ -1844,13 +1965,15 @@
         grad_hidden,
         gain_attn[None],
         out_term,
+        down_term,
         gain_mlp_sum,
         gain_heads_sum,
         attn_input,
     )
     shard_in = in_rows(rows_in)
-    shard_down = rows_down.reshape(w_down.shape).astype(jnp.float32)
-    shard_out = rows_out.reshape(w_out.shape).astype(jnp.float32)
+    rows_both = rows_both.reshape(-1, width).astype(jnp.float32)
+    shard_down = rows_both[: w_down.shape[0]]
+    shard_out = rows_both[w_down.shape[0] :]
     if sharers == 1:
         shard_qkvg = qkvg_rows(rows_qkvg, heads, kv_heads)
     else:

time: 890 us -> 849 us (0.954)
  Pallas kernels: 851 us -> 811 us
    pallas_call x1, Pallas kernels: 225 us -> 177 us  [mlp(): pl.pallas_call(functools.partial(mlp_kernel, owners, reps), out_shape=out...]
    pallas_call x1, Pallas kernels: 156 us -> 172 us  [last(): pl.pallas_call(functools.partial(last_kernel, owners, reps), out_shape=(s...]
    pallas_call x1, Pallas kernels: 219 us -> 210 us  [backward(): pl.pallas_call(functools.partial(backward_kernel, owners, reps, heads, kv...]
where the time goes in v5:
time: 849 us; the launch traced here: 842 us
  Pallas kernels  811 us (96%)
  local copies, waits for them, and re-layouts  21 us (2%)
  other arithmetic  8.89 us (1%)
    pallas_call x1, Pallas kernels, backward(): pl.pallas_call(functools.partial(backward_kernel, owners, reps, heads, kv...  210 us
    pallas_call x1, Pallas kernels, mlp(): pl.pallas_call(functools.partial(mlp_kernel, owners, reps), out_shape=out...  177 us
    pallas_call x1, Pallas kernels, last(): pl.pallas_call(functools.partial(last_kernel, owners, reps), out_shape=(s...  172 us
    pallas_call x1, Pallas kernels, attention(): pl.pallas_call(functools.partial(attention_kernel, owners, reps, heads, k...  137 us
    pallas_call x1, Pallas kernels, first(): pl.pallas_call(functools.partial(first_kernel, owners, reps, heads, kv_he...  104 us

profile of v5, /device:TPU:0, one launch (start us, length us, event | category | flops | bytes accessed | tf_op | source)
XLA Modules:
  0.0 841.6 jit_solution(18043138072576871367)
XLA Ops:
  0.6 0.7 maximum_convert_fusion
  1.3 0.1 dynamic_update_slice.3
  1.5 0.7 convert_element_type.20
  2.1 0.7 convert_element_type.21
  2.8 0.6 broadcast_in_dim.14.small_ref
  3.4 0.7 broadcast_multiply_fusion
  4.1 0.1 add.58
  4.2 0.1 add.59
  4.2 0.1 add.61
  4.3 3.7 multiply_cosine_fusion
  8.0 1.3 pad_maximum_fusion
  9.3 104.5 %first.1 = (bf16[8,256,2048]{2,1,0:T(8,128)(2,1)}, f32[8,256,256]{2,1,0:T(8,128)}, f32[8,256,256]{2,1,0:T(8,128)}, f32[8,256,128]{2,1,0:T(8,128)}, bf16[8,256,12...) custom-call(bf16[256,2048]{1,0:T(8,128)(2,1)} %tokens_ref.5, ...), custom_call_target="tpu_custom_call" | custom-call | flops 6442450944 | bytes 41943040 | tf_op jit(solution)/shard_map/first/pallas_call | solution.py:526
  113.8 0.7 copy.34
  114.6 0.6 slice_bitcast_fusion
  115.1 0.6 copy.31
  115.7 2.5 constant_dynamic-slice_fusion.2
  118.2 1.0 reshape.121
  119.3 1.2 copy.27
  120.5 1.9 reshape.118.in_pieces_ref
  122.4 0.1 add.64
  122.5 0.1 add.66
  122.6 0.6 broadcast_add_fusion.position_row_ref
  123.2 136.6 %attention.1 = (bf16[8,256,256]{2,1,0:T(8,128)(2,1)}, f32[256,2048]{1,0:T(8,128)}, bf16[256,2048]{1,0:T(8,128)(2,1)}, bf16[8,256,2048]{2,1,0:T(8,128)(2,1)}, bf16[8,4,64,1536]{3,2,1,0:T(8,128)(2,1)}) custom-call(bf16[256,2048]{1,0:T(8,128)(2,1)} %tokens_ref.5, bf16[8,256,256]{2,1,0:T(8,128)(2,1)} %get-tuple-element.40.query_ref.query_rot_ref, ...), custom_call_target="tpu_custom_call" | custom-call | flops 4294967296 | bytes 41943040 | tf_op jit(solution)/shard_map/attention/pallas_call | solution.py:986
  259.8 176.7 %mlp.1 = (bf16[8,256,2048]{2,1,0:T(8,128)(2,1)}, bf16[8,256,768]{2,1,0:T(8,128)(2,1)}, bf16[8,256,1536]{2,1,0:T(8,128)(2,1)}, f32[256,2048]{1,0:T(8,128)}, bf16[...) custom-call(bf16[256,2048]{1,0:T(8,128)(2,1)} %get-tuple-element.45.entry_ref, ...), custom_call_target="tpu_custom_call" | custom-call | flops 38654705664 | bytes 41943040 | tf_op jit(solution)/shard_map/mlp/pallas_call | solution.py:1156
  436.5 210.0 %backward.1 = (bf16[8,256,2048]{2,1,0:T(8,128)(2,1)}, bf16[256,2048]{1,0:T(8,128)(2,1)}, bf16[8,256,768]{2,1,0:T(8,128)(2,1)}, f32[1,256]{1,0:T(1,128)}, f32[256...) custom-call(bf16[256,2048]{1,0:T(8,128)(2,1)} %get-tuple-element.49.branch_ref, ...), custom_call_target="tpu_custom_call" | custom-call | flops 12884901888 | bytes 41943040 | tf_op jit(solution)/shard_map/backward/pallas_call | solution.py:1460
  646.5 0.6 copy.32
  647.1 172.3 %last.1 = (bf16[256,2048]{1,0:T(8,128)(2,1)}, f32[1,768]{1,0:T(1,128)}, bf16[8,4,64,768]{3,2,1,0:T(8,128)(2,1)}, bf16[4,4,64,2048]{3,2,1,0:T(8,128)(2,1)}) custom-call(bf16[8,256,768]{2,1,0:T(8,128)(2,1)} %get-tuple-element.57.grads_ref, bf16[2048,768]{1,0:T(8,128)(2,1)} %bitcast.46, bf16[256,2048]{1,0:T(8,128)(2,1)} %tokens_ref.5, ...), custom_call_target="tpu_custom_call" | custom-call | flops 12884901888 | bytes 41943040 | tf_op jit(solution)/shard_map/last/pallas_call | solution.py:1707
  819.4 0.0 copy-start.1
  819.5 5.6 slice.40
  825.0 0.0 copy-done.1
  825.0 0.0 copy-start
  825.0 4.0 qkvg_rows.1
  829.0 1.0 copy-done
  830.0 0.0 copy-start.2
  830.0 6.5 in_rows.1
  836.5 0.0 copy-done.2
  836.5 0.0 copy-start.5
  836.5 0.0 copy-start.3
  836.5 0.0 copy-start.4
  836.5 1.6 slice.39
  838.1 0.0 copy-done.5
  838.1 0.6 fusion.1
  838.7 0.6 fusion.2
  839.2 0.0 copy-done.3
  839.2 1.0 copy.38
  840.2 0.0 copy-done.4
  840.2 1.0 copy.39
  (7 shorter events, 0.0 us)
Async XLA Ops:
  819.4 5.6 copy-start.1
  825.0 5.0 copy-start
  830.0 6.5 copy-start.2
  836.5 1.6 copy-start.5
  836.5 2.7 copy-start.3
  836.5 3.7 copy-start.4

commit v6 on v5

--- a/solution.py
+++ b/solution.py
@@ -1612,7 +1612,7 @@
             chips,
             k,
             term,
-            lambda: lax.fori_loop(TICKS * k, TICKS * (k + 1), one, 0),
+            lambda: lax.fori_loop(LAST_TICKS * k, LAST_TICKS * (k + 1), one, 0),
         )
         return 0
 
@@ -1665,7 +1665,7 @@
         tick(t)
         return 0
 
-    lax.fori_loop(TICKS * chips, max(columns.ticks(), rows.ticks()), one, 0)
+    lax.fori_loop(LAST_TICKS * chips, max(columns.ticks(), rows.ticks()), one, 0)
     for ahead in range(1, reps):
         source = lax.rem(rep + ahead, reps)
         arrived(gains_all.at[source], r_recv.at[source])
@@ -1679,7 +1679,8 @@
     rows.finish()
 
 
-TICKS = 5
+TICKS = 3
+LAST_TICKS = 4
 
 
 def last(
@@ -1971,9 +1972,9 @@
         attn_input,
     )
     shard_in = in_rows(rows_in)
-    rows_both = rows_both.reshape(-1, width).astype(jnp.float32)
-    shard_down = rows_both[: w_down.shape[0]]
-    shard_out = rows_both[w_down.shape[0] :]
+    down_units = w_down.shape[0] // shard
+    shard_down = rows_both[:down_units].reshape(w_down.shape).astype(jnp.float32)
+    shard_out = rows_both[down_units:].reshape(w_out.shape).astype(jnp.float32)
     if sharers == 1:
         shard_qkvg = qkvg_rows(rows_qkvg, heads, kv_heads)
     else:

time: 849 us -> 818 us (0.963)
  Pallas kernels: 811 us -> 778 us
    pallas_call x1, Pallas kernels: 172 us -> 155 us  [last(): pl.pallas_call(functools.partial(last_kernel, owners, reps), out_shape=(s...]
    pallas_call x1, Pallas kernels: 210 us -> 196 us  [backward(): pl.pallas_call(functools.partial(backward_kernel, owners, reps, heads, kv...]
where the time goes in v6:
time: 818 us; the launch traced here: 810 us
  Pallas kernels  778 us (95%)
  local copies, waits for them, and re-layouts  16.5 us (2%)
  other arithmetic  14.3 us (2%)
    pallas_call x1, Pallas kernels, backward(): pl.pallas_call(functools.partial(backward_kernel, owners, reps, heads, kv...  196 us
    pallas_call x1, Pallas kernels, mlp(): pl.pallas_call(functools.partial(mlp_kernel, owners, reps), out_shape=out...  177 us
    pallas_call x1, Pallas kernels, last(): pl.pallas_call(functools.partial(last_kernel, owners, reps), out_shape=(s...  155 us
    pallas_call x1, Pallas kernels, attention(): pl.pallas_call(functools.partial(attention_kernel, owners, reps, heads, k...  137 us
    pallas_call x1, Pallas kernels, first(): pl.pallas_call(functools.partial(first_kernel, owners, reps, heads, kv_he...  104 us

profile of v6, /device:TPU:0, one launch (start us, length us, event | category | flops | bytes accessed | tf_op | source)
XLA Modules:
  0.0 810.4 jit_solution(12961144283818750809)
XLA Ops:
  0.6 0.7 maximum_convert_fusion
  1.3 0.1 dynamic_update_slice.3
  1.5 0.7 convert_element_type.28
  2.1 0.7 convert_element_type.29
  2.8 0.6 broadcast_in_dim.14.small_ref
  3.4 0.7 broadcast_multiply_fusion
  4.1 0.1 add.58
  4.2 0.1 add.59
  4.2 0.1 add.61
  4.3 3.7 multiply_cosine_fusion
  8.0 1.3 pad_maximum_fusion
  9.3 104.5 %first.1 = (bf16[8,256,2048]{2,1,0:T(8,128)(2,1)}, f32[8,256,256]{2,1,0:T(8,128)}, f32[8,256,256]{2,1,0:T(8,128)}, f32[8,256,128]{2,1,0:T(8,128)}, bf16[8,256,12...) custom-call(bf16[256,2048]{1,0:T(8,128)(2,1)} %tokens_ref.5, ...), custom_call_target="tpu_custom_call" | custom-call | flops 6442450944 | bytes 41943040 | tf_op jit(solution)/shard_map/first/pallas_call | solution.py:526
  113.8 0.7 copy.34
  114.6 0.6 slice_bitcast_fusion
  115.1 0.6 copy.31
  115.7 2.5 constant_dynamic-slice_fusion.2
  118.2 1.0 reshape.125
  119.3 1.2 copy.27
  120.5 1.9 reshape.120.in_pieces_ref
  122.4 0.1 add.64
  122.5 0.1 add.66
  122.6 0.6 broadcast_add_fusion.position_row_ref
  123.2 136.6 %attention.1 = (bf16[8,256,256]{2,1,0:T(8,128)(2,1)}, f32[256,2048]{1,0:T(8,128)}, bf16[256,2048]{1,0:T(8,128)(2,1)}, bf16[8,256,2048]{2,1,0:T(8,128)(2,1)}, bf16[8,4,64,1536]{3,2,1,0:T(8,128)(2,1)}) custom-call(bf16[256,2048]{1,0:T(8,128)(2,1)} %tokens_ref.5, bf16[8,256,256]{2,1,0:T(8,128)(2,1)} %get-tuple-element.40.query_ref.query_rot_ref, ...), custom_call_target="tpu_custom_call" | custom-call | flops 4294967296 | bytes 41943040 | tf_op jit(solution)/shard_map/attention/pallas_call | solution.py:986
  259.8 176.7 %mlp.1 = (bf16[8,256,2048]{2,1,0:T(8,128)(2,1)}, bf16[8,256,768]{2,1,0:T(8,128)(2,1)}, bf16[8,256,1536]{2,1,0:T(8,128)(2,1)}, f32[256,2048]{1,0:T(8,128)}, bf16[...) custom-call(bf16[256,2048]{1,0:T(8,128)(2,1)} %get-tuple-element.45.entry_ref, ...), custom_call_target="tpu_custom_call" | custom-call | flops 38654705664 | bytes 41943040 | tf_op jit(solution)/shard_map/mlp/pallas_call | solution.py:1156
  436.5 195.5 %backward.1 = (bf16[8,256,2048]{2,1,0:T(8,128)(2,1)}, bf16[256,2048]{1,0:T(8,128)(2,1)}, bf16[8,256,768]{2,1,0:T(8,128)(2,1)}, f32[1,256]{1,0:T(1,128)}, f32[256...) custom-call(bf16[256,2048]{1,0:T(8,128)(2,1)} %get-tuple-element.49.branch_ref, ...), custom_call_target="tpu_custom_call" | custom-call | flops 12884901888 | bytes 41943040 | tf_op jit(solution)/shard_map/backward/pallas_call | solution.py:1460
  632.0 0.6 copy.32
  632.6 154.6 %last.1 = (bf16[256,2048]{1,0:T(8,128)(2,1)}, f32[1,768]{1,0:T(1,128)}, bf16[8,4,64,768]{3,2,1,0:T(8,128)(2,1)}, bf16[4,4,64,2048]{3,2,1,0:T(8,128)(2,1)}) custom-call(bf16[8,256,768]{2,1,0:T(8,128)(2,1)} %get-tuple-element.57.grads_ref, bf16[2048,768]{1,0:T(8,128)(2,1)} %bitcast.50, bf16[256,2048]{1,0:T(8,128)(2,1)} %tokens_ref.5, ...), custom_call_target="tpu_custom_call" | custom-call | flops 12884901888 | bytes 41943040 | tf_op jit(solution)/shard_map/last/pallas_call | solution.py:1708
  787.3 2.3 slice.25
  789.6 0.0 copy-start
  789.6 3.8 bitcast_convert_fusion
  793.3 0.0 slice-start
  793.3 0.0 copy-done
  793.4 0.0 slice-start.1
  793.4 4.0 qkvg_rows.1
  797.4 1.3 slice.24
  798.7 1.6 bitcast_convert_fusion.1
  800.3 0.0 slice-done
  800.3 0.0 slice-done.1
  800.3 0.0 copy-start.3
  800.4 0.0 copy-start.1
  800.4 0.0 copy-start.2
  800.4 6.5 in_rows.1
  806.9 0.0 copy-done.3
  806.9 0.6 fusion.1
  807.4 0.6 fusion.2
  808.0 0.0 copy-done.1
  808.0 1.0 copy.38
  809.0 0.0 copy-done.2
  809.0 1.0 copy.39
  (8 shorter events, 0.0 us)
Async XLA Ops:
  789.6 3.8 copy-start
  793.3 7.0 slice-start
  793.4 7.0 slice-start.1
  800.3 6.5 copy-start.3
  800.4 7.7 copy-start.1
  800.4 8.6 %copy-start.2 = (bf16[256,2048]{1,0:T(8,128)(2,1)S(1)}, bf16[256,2048]{1,0:T(8,128)(2,1)}, u32[]{:S(2)}) copy-start(bf16[256,2048]{1,0:T(8,128)(2,1)} %get-tuple-element.90) | copy-start | bytes 3145732

commit v7 on v6

--- a/solution.py
+++ b/solution.py
@@ -370,6 +370,8 @@
     small_out,
     buf,
     weight_buf,
+    entry_buf,
+    entry_sem,
     small_send,
     small_recv,
     local_sem,
@@ -461,7 +463,10 @@
             values = buf[at].astype(F32)
             normed, _unused = head_norm(values)
             entry = (normed * gain).astype(BF16)
-            input_out[at] = entry
+            store = pltpu.make_async_copy(entry_buf.at[which], input_out.at[at], entry_sem.at[which])
+            pl.when(k > 0)(store.wait)
+            entry_buf[which] = entry
+            store.start()
             projected = dot(entry, weight[...])
             cosine, sine = angles(table_ref[at])
             for h in range(heads):
@@ -486,6 +491,8 @@
         return 0
 
     lax.fori_loop(0, gather.chips, block, 0)
+    for which in range(2):
+        pltpu.make_async_copy(entry_buf.at[which], input_out.at[0], entry_sem.at[which]).wait()
     columns_copy.wait()
     gather.finish()
     reshard.finish()
@@ -527,10 +534,12 @@
         functools.partial(first_kernel, owners, reps, heads, kv_heads, sharers),
         out_shape=outs,
         in_specs=[anywhere(), anywhere(), vmem(), vmem()],
-        out_specs=(vmem(),) * 7 + (anywhere(), vmem()),
+        out_specs=(anywhere(),) + (vmem(),) * 6 + (anywhere(), vmem()),
         scratch_shapes=[
             pltpu.VMEM((owners, rows, width), BF16),
             pltpu.VMEM((owners, reps, shard // reps, cols), BF16),
+            pltpu.VMEM((2, rows, width), BF16),
+            pltpu.SemaphoreType.DMA((2,)),
             pltpu.SemaphoreType.DMA((owners,)),
             pltpu.SemaphoreType.DMA((owners,)),
             pltpu.SemaphoreType.DMA,
@@ -1028,11 +1037,14 @@
     gain_ref,
     entry_all,
     activated_out,
-    grads_out,
+    grads_all,
     grad_hidden_out,
     grad_branch_out,
     gain_out,
+    down_out,
+    grads_out,
     down_sum,
+    out_sem,
     entry_buf,
     cotangent_buf,
     activated_buf,
@@ -1058,6 +1070,10 @@
         return pltpu.make_async_copy(
             activated_buf, activated_out.at[pl.ds(2 * at, 2)], store_sem
         )
+
+    def grads_store(at):
+        pair = pl.ds(2 * at, 2)
+        return pltpu.make_async_copy(grads_out.at[pair], grads_all.at[pair], out_sem.at[at])
 
     def compute(at, first=False):
         pair = pl.ds(2 * at, 2)
@@ -1086,6 +1102,7 @@
             (grad_activated * up * sig * (1.0 + gate * (1.0 - sig))).astype(BF16).reshape(shape)
         )
         grads_out[pair, :, units:] = (grad_activated * silu).astype(BF16).reshape(shape)
+        grads_store(at).start()
         down_sum[...] += dot_tn(activated, cotangent)
 
     def term(at):
@@ -1120,7 +1137,10 @@
         staged(scatter, chips, k, term, work)
         return 0
 
-    lax.fori_loop(0, chips, back, 0)
+    lax.fori_loop(0, chips - 1, back, 0)
+    down_store = pltpu.make_async_copy(down_sum, down_out, out_sem.at[chips])
+    down_store.start()
+    back(chips - 1, 0)
     hidden_buf = scatter.both.at[1 - scatter.core]
     load_hidden = pltpu.make_async_copy(hidden_ref, hidden_buf, local_sem)
     load_hidden.start()
@@ -1136,6 +1156,9 @@
     grad_hidden_out[...] = grad_hidden
     grad_branch_out[...] = grad_hidden.astype(BF16)
     stores(0).wait()
+    for at in range(chips):
+        grads_store(at).wait()
+    down_store.wait()
     gather.finish()
     scatter.finish()
 
@@ -1157,8 +1180,11 @@
         functools.partial(mlp_kernel, owners, reps),
         out_shape=outs,
         in_specs=[anywhere()] * 2 + [vmem()] * 2 + [anywhere()] + [vmem()] * 2,
-        out_specs=(anywhere(),) * 2 + (vmem(),) * 5,
+        out_specs=(anywhere(),) * 3 + (vmem(),) * 3 + (anywhere(),),
         scratch_shapes=[
+            pltpu.VMEM((owners, rows, 2 * units), BF16),
+            pltpu.VMEM((units, width), F32),
+            pltpu.SemaphoreType.DMA((owners // 2 + 1,)),
             pltpu.VMEM((2, rows, width), BF16),
             pltpu.VMEM((2, rows, width), BF16),
             pltpu.VMEM((2, rows, units), BF16),

time: 818 us -> 811 us (level)
  no operation moved by 1% of the time
where the time goes in v7:
time: 811 us; the launch traced here: 803 us
  Pallas kernels  772 us (95%)
  local copies, waits for them, and re-layouts  16.5 us (2%)
  other arithmetic  14.3 us (2%)
    pallas_call x1, Pallas kernels, backward(): pl.pallas_call(functools.partial(backward_kernel, owners, reps, heads, kv...  194 us
    pallas_call x1, Pallas kernels, mlp(): pl.pallas_call(functools.partial(mlp_kernel, owners, reps), out_shape=out...  174 us
    pallas_call x1, Pallas kernels, last(): pl.pallas_call(functools.partial(last_kernel, owners, reps), out_shape=(s...  154 us
    pallas_call x1, Pallas kernels, attention(): pl.pallas_call(functools.partial(attention_kernel, owners, reps, heads, k...  136 us
    pallas_call x1, Pallas kernels, first(): pl.pallas_call(functools.partial(first_kernel, owners, reps, heads, kv_he...  103 us

profile of v7, /device:TPU:0, one launch (start us, length us, event | category | flops | bytes accessed | tf_op | source)
XLA Modules:
  0.0 803.4 jit_solution(5193018853541099583)
XLA Ops:
  0.6 0.7 maximum_convert_fusion
  1.3 0.1 dynamic_update_slice.3
  1.5 0.7 convert_element_type.28
  2.1 0.7 convert_element_type.29
  2.8 0.6 broadcast_in_dim.14.small_ref
  3.4 0.7 broadcast_multiply_fusion
  4.1 0.1 add.58
  4.2 0.1 add.59
  4.2 0.1 add.61
  4.3 3.7 multiply_cosine_fusion
  8.0 1.3 pad_maximum_fusion
  9.3 103.3 %first.1 = (bf16[8,256,2048]{2,1,0:T(8,128)(2,1)}, f32[8,256,256]{2,1,0:T(8,128)}, f32[8,256,256]{2,1,0:T(8,128)}, f32[8,256,128]{2,1,0:T(8,128)}, bf16[8,256,12...) custom-call(bf16[256,2048]{1,0:T(8,128)(2,1)} %tokens_ref.5, ...), custom_call_target="tpu_custom_call" | custom-call | flops 6442450944 | bytes 41943040 | tf_op jit(solution)/shard_map/first/pallas_call | solution.py:533
  112.6 0.7 copy.34
  113.3 0.6 slice_bitcast_fusion
  113.9 0.6 copy.31
  114.5 2.5 constant_dynamic-slice_fusion.2
  117.0 1.0 reshape.125
  118.1 1.2 copy.27
  119.3 1.9 reshape.120.in_pieces_ref
  121.2 0.1 add.64
  121.3 0.1 add.66
  121.4 0.6 broadcast_add_fusion.position_row_ref
  122.0 136.4 %attention.1 = (bf16[8,256,256]{2,1,0:T(8,128)(2,1)}, f32[256,2048]{1,0:T(8,128)}, bf16[256,2048]{1,0:T(8,128)(2,1)}, bf16[8,256,2048]{2,1,0:T(8,128)(2,1)}, bf16[8,4,64,1536]{3,2,1,0:T(8,128)(2,1)}) custom-call(bf16[256,2048]{1,0:T(8,128)(2,1)} %tokens_ref.5, bf16[8,256,256]{2,1,0:T(8,128)(2,1)} %get-tuple-element.40.query_ref.query_rot_ref, ...), custom_call_target="tpu_custom_call" | custom-call | flops 4294967296 | bytes 41943040 | tf_op jit(solution)/shard_map/attention/pallas_call | solution.py:995
  258.4 173.5 %mlp.1 = (bf16[8,256,2048]{2,1,0:T(8,128)(2,1)}, bf16[8,256,768]{2,1,0:T(8,128)(2,1)}, bf16[8,256,1536]{2,1,0:T(8,128)(2,1)}, f32[256,2048]{1,0:T(8,128)}, bf16[...) custom-call(bf16[256,2048]{1,0:T(8,128)(2,1)} %get-tuple-element.45.entry_ref, ...), custom_call_target="tpu_custom_call" | custom-call | flops 38654705664 | bytes 41943040 | tf_op jit(solution)/shard_map/mlp/pallas_call | solution.py:1179
  431.9 194.1 %backward.1 = (bf16[8,256,2048]{2,1,0:T(8,128)(2,1)}, bf16[256,2048]{1,0:T(8,128)(2,1)}, bf16[8,256,768]{2,1,0:T(8,128)(2,1)}, f32[1,256]{1,0:T(1,128)}, f32[256...) custom-call(bf16[256,2048]{1,0:T(8,128)(2,1)} %get-tuple-element.49.branch_ref, ...), custom_call_target="tpu_custom_call" | custom-call | flops 12884901888 | bytes 41943040 | tf_op jit(solution)/shard_map/backward/pallas_call | solution.py:1486
  626.0 0.6 copy.32
  626.6 153.9 %last.1 = (bf16[256,2048]{1,0:T(8,128)(2,1)}, f32[1,768]{1,0:T(1,128)}, bf16[8,4,64,768]{3,2,1,0:T(8,128)(2,1)}, bf16[4,4,64,2048]{3,2,1,0:T(8,128)(2,1)}) custom-call(bf16[8,256,768]{2,1,0:T(8,128)(2,1)} %get-tuple-element.57.grads_ref, bf16[2048,768]{1,0:T(8,128)(2,1)} %bitcast.50, bf16[256,2048]{1,0:T(8,128)(2,1)} %tokens_ref.5, ...), custom_call_target="tpu_custom_call" | custom-call | flops 12884901888 | bytes 41943040 | tf_op jit(solution)/shard_map/last/pallas_call | solution.py:1734
  780.5 2.3 slice.25
  782.8 0.0 copy-start
  782.8 3.8 bitcast_convert_fusion
  786.6 0.0 slice-start
  786.6 0.0 copy-done
  786.6 0.0 slice-start.1
  786.6 4.0 qkvg_rows.1
  790.6 1.3 slice.24
  791.9 1.6 bitcast_convert_fusion.1
  793.6 0.0 slice-done
  793.6 0.0 slice-done.1
  793.6 0.0 copy-start.3
  793.6 0.0 copy-start.1
  793.6 0.0 copy-start.2
  793.6 6.5 in_rows.1
  800.1 0.0 copy-done.3
  800.1 0.6 fusion.1
  800.7 0.6 fusion.2
  801.2 0.0 copy-done.1
  801.2 1.0 copy.38
  802.2 0.0 copy-done.2
  802.2 1.0 copy.39
  (8 shorter events, 0.0 us)
Async XLA Ops:
  782.8 3.8 copy-start
  786.6 7.0 slice-start
  786.6 7.0 slice-start.1
  793.6 6.5 copy-start.3
  793.6 7.7 copy-start.1
  793.6 8.6 %copy-start.2 = (bf16[256,2048]{1,0:T(8,128)(2,1)S(1)}, bf16[256,2048]{1,0:T(8,128)(2,1)}, u32[]{:S(2)}) copy-start(bf16[256,2048]{1,0:T(8,128)(2,1)} %get-tuple-element.90) | copy-start | bytes 3145732
